TPU v7x, 32 devices: a whole 2x2x4 slice. The times are simulated.
32 devices in a mesh: tenant: 2 (over x), row: 2 (over core), col: 8 (over z, y).
Axes of the slice: x: 2, y: 2, z: 4, core: 2. Of those that a mesh axis runs over, the one named last changes fastest.
Arguments:
- tokens: bfloat16 [2048, 8192], P(('tenant', 'row'), 'col'), parts along dimension 0, may hold values from -6 to 6
- base_weight: bfloat16 [8192, 28672], P('row', 'col'), may hold values from -0.0625 to 0.0625
- delta_values: bfloat16 [24576, 1024], P(('tenant', 'row'), 'col'), parts along dimension 0, may hold values from -0.29882812 to 0.29882812
- delta_index: int32 [192, 8], P(('tenant', 'row'), 'col'), parts along dimension 0, may hold values from 0 to 895, as said below
- delta_count: int32 [4, 8], P(('tenant', 'row'), 'col'), parts along dimension 0, may hold values from 12 to 48, as said below
Outputs:
- hidden: bfloat16 [2048, 28672], P(('tenant', 'row'), 'col'), parts along dimension 0
There are 2 independent parts, one for each index of `tenant`. A program takes and returns all parts, laid end to end along the dimension named above; an argument that names none is the same for every part. Nothing has to cross between parts.
Inputs may be any that keep to these rules, and one draw needn't show every extreme that they name: `delta_index`: within one device's 48 slots the values are distinct. `delta_count`: some device uses all 48 slots in every draw.
All inputs are finite; a program needn't handle non-finite values.
Results may differ from a plain program's by a relative error of at most 0.0041.
Values may be sent and summed in bfloat16 or wider, within the bound.
No kernel may reach another device: no remote copies, remote signals or barrier semaphores. Data moves between devices by JAX's collectives and lax.ppermute only.
A program may use at most 320 MiB of HBM per device.

v0:
```python
import jax
import jax.numpy as jnp
from jax import lax
from jax.sharding import PartitionSpec as P


def apply_delta(weight, values, block_ids, counts, rows_half):
    block = values.shape[1]
    panel = weight.shape[1]
    col_blocks = panel // block
    row_blocks = weight.shape[0] // block
    owners = counts.shape[0]
    slot_total = block_ids.shape[0]
    slot_count = slot_total // owners
    position = jnp.arange(slot_total, dtype=jnp.int32)
    source = position // slot_count
    active = position % slot_count < counts[source, 0]
    row_block = source * rows_half + block_ids[:, 0] // col_blocks
    col_block = block_ids[:, 0] % col_blocks
    target_row = jnp.where(active, row_block, row_blocks)
    safe_row = jnp.where(active, row_block, 0)
    grid = weight.reshape(row_blocks, block, col_blocks, block)
    current = grid[safe_row, :, col_block, :]
    updated = (
        current.astype(jnp.float32) + values.reshape(slot_total, block, block).astype(jnp.float32)
    ).astype(jnp.bfloat16)
    grid = grid.at[target_row, :, col_block, :].set(updated, mode="drop")
    return grid.reshape(weight.shape)


def body(tokens, base_weight, delta_values, delta_index, delta_count):
    block = delta_values.shape[1]
    rows_half = base_weight.shape[0] // block
    merged = apply_delta(base_weight, delta_values, delta_index, delta_count, rows_half)
    effective = lax.all_gather(merged, "row", axis=0, tiled=True)
    result = jnp.dot(
        lax.all_gather(tokens, "col", axis=1, tiled=True),
        effective,
        preferred_element_type=jnp.float32,
    )
    return result.astype(jnp.bfloat16)


def solution(mesh):
    return jax.shard_map(
        body,
        mesh=mesh,
        in_specs=(
            P(("tenant", "row"), "col"),
            P("row", "col"),
            P(("tenant", "row"), "col"),
            P(("tenant", "row"), "col"),
            P(("tenant", "row"), "col"),
        ),
        out_specs=P(("tenant", "row"), "col"),
        check_vma=False,
    )
```

profile of v0, /device:TPU:0, one launch (start us, length us, event | category | flops | bytes accessed | tf_op | source)
XLA Modules:
  0.0 295.2 jit_solution(16242364331167194935)
XLA Ops:
  6.5 0.0 all-gather.5.cloned.1.call-start
  6.5 0.7 all-gather.5.cloned.1.call-update
  7.3 0.0 all-gather.3.cloned.1.call-start
  7.9 47.1 %reshape.66 = bf16[32,128,28,128]{3,2,1,0:T(8,128)(2,1)} reshape(bf16[4096,3584]{1,0:T(8,128)(2,1)} %param.6) | data formatting | bytes 58720256 | tf_op jit(solution)/shard_map/reshape | solution.py:22
  55.0 0.0 copy-start
  55.0 22.5 %copy.15 = bf16[32,128,28,128]{3,1,2,0:T(8,128)(2,1)} copy(bf16[32,128,28,128]{3,2,1,0:T(8,128)(2,1)} %reshape.66) | data formatting | bytes 58720256 | tf_op jit(solution)/shard_map/reshape | solution.py:22
  77.5 0.0 copy-done
  77.5 10.5 %gather_fusion = bf16[48,128,128]{2,1,0:T(8,128)(2,1)S(1)} fusion(bf16[32,128,28,128]{3,1,2,0:T(8,128)(2,1)} %copy.15, s32[48]{0:T(128)S(1)} %get-tuple-element.5), kind=kCustom, calls=%fused_computation | custom fusion | bytes 3146112 | tf_op jit(solution)/shard_map/gather | solution.py:23
  88.0 2.0 fusion.1
  90.0 7.7 %scatter_fusion = bf16[32,128,28,128]{3,1,2,0:T(8,128)(2,1)} fusion(bf16[32,128,28,128]{3,1,2,0:T(8,128)(2,1)} %copy.15, s32[48]{0:T(128)S(1)} %fusion.9, bf16[48,128,128]{2,1,0:T(8,128)(2,1)S(1)} %fusion.1), kind=kCustom, calls=%fused_computation.1 | custom fusion | bytes 4718976 | tf_op jit(solution)/shard_map/scatter | solution.py:27
  97.7 38.8 %copy.16 = bf16[32,128,28,128]{1,0,3,2:T(8,128)(2,1)} copy(bf16[32,128,28,128]{3,1,2,0:T(8,128)(2,1)} %scatter_fusion) | data formatting | bytes 58720256 | tf_op jit(solution)/shard_map/scatter | solution.py:27
  136.5 20.5 %copy.23 = bf16[448,8,32,128]{3,1,2,0:T(8,128)(2,1)} copy(bf16[448,8,32,128]{3,2,1,0:T(8,128)(2,1)} %bitcast.21) | data formatting | bytes 58720256
  156.9 0.0 all-gather.3.cloned.1.call-update
  157.0 0.0 all-gather.5.cloned.1.call-done
  157.0 86.8 %all-gather.3.cloned.1.call-done = bf16[8192,3584]{0,1:T(8,128)(2,1)} async-done(((bf16[4096,3584]{0,1:T(8,128)(2,1)}), bf16[8192,3584]{0,1:T(8,128)(2,1)}) %all-gather.3.cloned.1.call-update) | async-done | bytes 58720272 | tf_op jit(solution)/shard_map/all_gather | solution.py:35
  243.8 38.6 %fusion = bf16[512,3584]{0,1:T(8,128)(2,1)} fusion(bf16[8192,3584]{0,1:T(8,128)(2,1)} %all-gather.3.cloned.1.call-done, bf16[512,8192]{1,0:T(8,128)(2,1)} %all-gather.5.cloned.1.call-done), kind=kOutput, calls=%fused_computation.4 | convolution fusion | flops 30066606080 | bytes 70778880 | tf_op jit(solution)/shard_map/dot_general | solution.py:36
  282.5 5.9 %copy.17 = bf16[512,3584]{1,0:T(8,128)(2,1)} copy(bf16[512,3584]{0,1:T(8,128)(2,1)} %fusion) | data formatting | bytes 7340032 | tf_op jit(solution)/shard_map/convert_element_type | solution.py:41
  (2 shorter events, 0.0 us)
Async XLA Ops:
  6.5 150.4 %all-gather.5.cloned.1.call-start = ((), (), s32[]{:S(2)}) async-start(), calls=%async_computation.1 | async-start | bytes 9437184 | tf_op jit(solution)/shard_map/all_gather | solution.py:37
  7.3 236.6 %all-gather.3.cloned.1.call-start = ((), (), s32[]{:S(2)}) async-start(), calls=%async_computation | async-start | bytes 88080384 | tf_op jit(solution)/shard_map/all_gather | solution.py:35
  55.0 22.5 %copy-start = (s32[48,1]{0,1:T(1,128)S(1)}, s32[48,1]{0,1:T(1,128)}, u32[]{:S(2)}) copy-start(s32[48,1]{0,1:T(1,128)} %param.8) | copy-start | bytes 580
Sparse Core Ops, SparseCore 0:
  9.5 127.6 all-gather.4
  157.1 86.7 all-gather.2
where the time goes:
time: 298 us; the launch traced here: 295 us
  local copies, waits for them, and re-layouts  153 us (51%)
  waiting for transfers between devices  87.6 us (29%)
  matrix products  38.6 us (13%)
  between operations  14.1 us (5%)
    all_gather x1, waiting for transfers between devices, body(): effective = lax.all_gather(merged, 'row', axis=0, tiled=True)  86.8 us
    reshape x2, local copies, waits for them, and re-layouts, apply_delta(): grid = weight.reshape(row_blocks, block, col_blocks, block)  69.6 us
    scatter x2, local copies, waits for them, and re-layouts, apply_delta(): grid = grid.at[target_row, :, col_block, :].set(updated, mode='drop')  46.5 us
    dot_general x1, matrix products, body(): jnp.dot(lax.all_gather(tokens, 'col', axis=1, tiled=True), effective, pre...  38.6 us
    unnamed x3, local copies, waits for them, and re-layouts  20.5 us
    gather x1, local copies, waits for them, and re-layouts, apply_delta(): current = grid[safe_row, :, col_block, :]  10.5 us
  transfers between devices with their start and end apart: 2, of which 1 were waited for; matrix products, arithmetic and copies ran while one was open for 50% of the time, Pallas kernels for 0%

commit v1 on v0

v1 whole, which is shorter than its diff:
```python
import functools

import jax
import jax.numpy as jnp
import numpy as np
from jax import lax
from jax.experimental import pallas as pl
from jax.experimental.pallas import tpu as pltpu
from jax.sharding import PartitionSpec as P

STREAMS = 2
W_SLOTS = 3


def ring_order(n):
    return list(range(0, n, 2)) + list(range(n - 1, 0, -2))


def plan(n):
    ring = ring_order(n)
    place = {c: k for k, c in enumerate(ring)}
    half = n // 2
    order = np.zeros((n, 2, half), np.int32)
    events = [(d, min(half, STREAMS * d)) for d in range(1, half)]
    phases = [[[[] for _ in range(2)] for _ in range(n)] for _ in events]
    kept = [[0, 0] for _ in range(n)]
    for col in range(n):
        me = place[col]

        def dist(c):
            ahead = (place[c] - me) % n
            return min(ahead, n - ahead)

        def token_id(c):
            ahead = (place[c] - me) % n
            if ahead == 0:
                return 0
            if ahead == half:
                return n - 1
            return 2 * ahead if ahead < half else 2 * (n - ahead) - 1

        for h in range(2):
            chunks = sorted(range(h * half, (h + 1) * half), key=lambda c: (dist(c), c))
            order[col, h] = [c - h * half for c in chunks]
            for row in range(2):
                for j, c in enumerate(chunks):
                    need = 0 if row == h else j + 1
                    piece = j if row == h else half + j
                    if dist(c) == half:
                        kept[col][row] = piece
                        continue
                    number = next(k for k, (d, r) in enumerate(events) if d >= dist(c) and r >= need)
                    phases[number][col][row].append((token_id(c), piece))
    return ring, order, events, phases, kept


def tie(values, after):
    values, after = tuple(values), tuple(after)
    return lax.optimization_barrier(values + after)[: len(values)]


def hbm(x):
    return pltpu.with_memory_space_constraint(x, pltpu.HBM)


def vmem(x):
    return pltpu.with_memory_space_constraint(x, pltpu.VMEM)


def merge(me, order, index, count, weight, values, piece, pieces):
    block = values.shape[1]
    blocks = weight.shape[0] // block // pieces
    width = weight.shape[1]
    col_blocks = width // block

    def kernel(me_ref, order_ref, index_ref, count_ref, w_ref, values_ref, out_ref, vbuf, wsem, vsem):
        first = order_ref[me_ref[0] * pieces + piece] * blocks
        value_copy = pltpu.make_async_copy(values_ref, vbuf, vsem)
        value_copy.start()

        def copy(k):
            rows = pl.ds(pl.multiple_of((first + k) * block, block), block)
            return pltpu.make_async_copy(w_ref.at[rows], out_ref.at[pl.ds(k * block, block)], wsem.at[k])

        for k in range(blocks):
            copy(k).start()
        value_copy.wait()
        for k in range(blocks):
            copy(k).wait()

        def slot(s, carry):
            which = index_ref[s]
            row = which // col_blocks
            row_here = row - first

            @pl.when(jnp.logical_and(row_here >= 0, row_here < blocks))
            def _():
                rows = pl.ds(pl.multiple_of(row_here * block, block), block)
                cols = pl.ds(pl.multiple_of((which - row * col_blocks) * block, block), block)
                value = vbuf[pl.ds(pl.multiple_of(s * block, block), block), :]
                old = out_ref[rows, cols]
                out_ref[rows, cols] = (old.astype(jnp.float32) + value.astype(jnp.float32)).astype(out_ref.dtype)

            return carry

        lax.fori_loop(0, count_ref[0], slot, 0)

    return pl.pallas_call(
        kernel,
        in_specs=[pl.BlockSpec(memory_space=pltpu.SMEM)] * 4 + [pl.BlockSpec(memory_space=pltpu.HBM)] * 2,
        out_specs=pl.BlockSpec(memory_space=pltpu.VMEM),
        out_shape=pltpu.VMEM((blocks * block, width), weight.dtype),
        scratch_shapes=[
            pltpu.VMEM(values.shape, values.dtype),
            pltpu.SemaphoreType.DMA((blocks,)),
            pltpu.SemaphoreType.DMA,
        ],
        compiler_params=pltpu.CompilerParams(vmem_limit_bytes=10 * 2**20),
        cost_estimate=pl.CostEstimate(flops=0, bytes_accessed=0, transcendentals=0),
        name=f"merge{piece}",
    )(me, order, index, count, hbm(weight), hbm(values))


def phase(me, table, tokens, pieces, spaces, acc, most, keep=None):
    rows, part = tokens[0][0].shape
    depth = part * STREAMS
    total = pieces[0].shape[1]
    width = 512 if total % 512 == 0 else 128
    tiles = total // width
    first = acc is None
    n_tokens, n_pieces = len(tokens), len(pieces)
    keep_pieces, keep_spaces = keep if keep else ([], [])
    n_keep = len(keep_pieces)

    def kernel(me_ref, table_ref, *refs):
        token_refs = refs[: n_tokens * STREAMS]
        refs = refs[n_tokens * STREAMS :]
        piece_refs, keep_refs, refs = refs[:n_pieces], refs[n_pieces : n_pieces + n_keep], refs[n_pieces + n_keep :]
        if not first:
            refs = refs[1:]
        out_ref, refs = refs[0], refs[1:]
        if keep:
            kept_ref, refs = refs[0], refs[1:]
        tbuf, wbuf, tsem, wsem, ksem = refs
        base = me_ref[0] * (2 + 2 * most)
        count = table_ref[base]

        def columns(tile):
            return pl.ds(pl.multiple_of(tile * width, width), width)

        def token_copy(ref, i, k):
            return pltpu.make_async_copy(ref, tbuf.at[i, :, pl.ds(k * part, part)], tsem.at[i, k])

        def piece_copy(ref, tile, slot):
            return pltpu.make_async_copy(ref.at[:, columns(tile)], wbuf.at[slot], wsem.at[slot])

        def start_piece(tile, i, slot):
            which = table_ref[base + 3 + 2 * i]
            for p in range(n_pieces):

                @pl.when(which == p)
                def _():
                    piece_copy(piece_refs[p], tile, slot).start()

        def following(tile, i, slot):
            wrap = i == count - 1
            slot = jnp.where(slot == W_SLOTS - 1, 0, slot + 1)
            return jnp.where(wrap, tile + 1, tile), jnp.where(wrap, 0, i + 1), slot

        @pl.when(count > 0)
        def _():
            ahead = (jnp.int32(0), jnp.int32(0), jnp.int32(0))
            for s in range(W_SLOTS - 1):
                start_piece(*ahead)
                ahead = following(*ahead)

                if s == 0:
                    for i in range(most):

                        @pl.when(i < count)
                        def _():
                            which = table_ref[base + 2 + 2 * i]
                            for t in range(n_tokens):

                                @pl.when(which == t)
                                def _():
                                    for k in range(STREAMS):
                                        token_copy(token_refs[t * STREAMS + k], i, k).start()

        if keep:
            which_kept = table_ref[base + 1]
            for p in range(n_keep):

                @pl.when(which_kept == p)
                def _():
                    pltpu.make_async_copy(keep_refs[p], kept_ref, ksem).start()

        @pl.when(count > 0)
        def _():
            def step_body(step, carry):
                tile, i, slot, ahead = carry

                @pl.when(ahead[0] < tiles)
                def _():
                    start_piece(*ahead)

                @pl.when(tile == 0)
                def _():
                    for k in range(STREAMS):
                        token_copy(token_refs[k], i, k).wait()

                piece_copy(piece_refs[0], tile, slot).wait()
                product = jnp.dot(tbuf[i], wbuf[slot], preferred_element_type=jnp.float32)
                if first:

                    @pl.when(i == 0)
                    def _():
                        out_ref[:, columns(tile)] = product

                    @pl.when(i > 0)
                    def _():
                        out_ref[:, columns(tile)] += product
                else:
                    out_ref[:, columns(tile)] += product
                return (*following(tile, i, slot), following(*ahead))

            zero = jnp.int32(0)
            ahead = (zero, zero, zero)
            for s in range(W_SLOTS - 1):
                ahead = following(*ahead)
            lax.fori_loop(0, count * tiles, step_body, (zero, zero, zero, ahead))

        if keep:
            pltpu.make_async_copy(keep_refs[0], kept_ref, ksem).wait()

    def specs(spaces):
        return [pl.BlockSpec(memory_space=space) for space in spaces]

    flat = [a for t in tokens for a in t]
    pin = {pl.ANY: lambda x: x, pltpu.HBM: hbm}
    pieces = [pin[space](p) for p, space in zip(pieces, spaces)]
    keep_pieces = [pin[space](p) for p, space in zip(keep_pieces, keep_spaces)]
    operands = [me, table] + flat + list(pieces) + list(keep_pieces) + ([] if first else [vmem(acc)])
    in_spaces = [pltpu.SMEM] * 2 + [pl.ANY] * len(flat) + list(spaces) + list(keep_spaces)
    in_spaces += [] if first else [pltpu.VMEM]
    out_shape = [pltpu.VMEM((rows, total), jnp.float32)]
    if keep:
        out_shape.append(pltpu.VMEM(pieces[0].shape, pieces[0].dtype))
    return pl.pallas_call(
        kernel,
        in_specs=specs(in_spaces),
        out_specs=specs([pltpu.VMEM] * len(out_shape)),
        out_shape=out_shape,
        scratch_shapes=[
            pltpu.VMEM((most, rows, depth), tokens[0][0].dtype),
            pltpu.VMEM((W_SLOTS, depth, width), pieces[0].dtype),
            pltpu.SemaphoreType.DMA((most, STREAMS)),
            pltpu.SemaphoreType.DMA((W_SLOTS,)),
            pltpu.SemaphoreType.DMA,
        ],
        input_output_aliases={} if first else {len(operands) - 1: 0},
        compiler_params=pltpu.CompilerParams(vmem_limit_bytes=12 * 2**20),
        cost_estimate=pl.CostEstimate(flops=0, bytes_accessed=0, transcendentals=0),
        name="phase",
    )(*operands)


def last_phase(tokens, weight, acc, out_dtype):
    rows, part = tokens[0].shape
    total = weight.shape[1]
    width = 512 if total % 512 == 0 else 128
    tiles = total // width
    n = len(tokens)

    def kernel(*refs):
        token_refs = refs[:n]
        w_ref, acc_ref, out_ref, obuf, osem = refs[n:]

        def store(tile):
            slot = lax.rem(tile, 2)
            at = pl.ds(pl.multiple_of(tile * width, width), width)
            return pltpu.make_async_copy(obuf.at[slot], out_ref.at[:, at], osem.at[slot])

        def step(tile, carry):
            at = pl.ds(pl.multiple_of(tile * width, width), width)
            total = acc_ref[:, at]
            for k in range(n):
                total = total + jnp.dot(
                    token_refs[k][...], w_ref[pl.ds(k * part, part), at], preferred_element_type=jnp.float32
                )

            @pl.when(tile >= 2)
            def _():
                store(tile - 2).wait()

            obuf[lax.rem(tile, 2)] = total.astype(out_dtype)
            store(tile).start()
            return carry

        lax.fori_loop(0, tiles, step, 0)
        for tile in range(max(0, tiles - 2), tiles):
            store(tile).wait()

    return pl.pallas_call(
        kernel,
        in_specs=[pl.BlockSpec(memory_space=pltpu.VMEM)] * (n + 2),
        out_specs=pl.BlockSpec(memory_space=pltpu.HBM),
        out_shape=jax.ShapeDtypeStruct((rows, total), out_dtype),
        scratch_shapes=[pltpu.VMEM((2, rows, width), out_dtype), pltpu.SemaphoreType.DMA((2,))],
        compiler_params=pltpu.CompilerParams(vmem_limit_bytes=24 * 2**20),
        cost_estimate=pl.CostEstimate(flops=0, bytes_accessed=0, transcendentals=0),
        name="last_phase",
    )(*tokens, vmem(weight), vmem(acc))


def body(tokens, base_weight, delta_values, delta_index, delta_count, n_col):
    ring, order, events, phases, kept = plan(n_col)
    half = n_col // 2
    ahead = [(ring[k], ring[(k + 1) % n_col]) for k in range(n_col)]
    behind = [(b, a) for a, b in ahead]
    swap = [(0, 1), (1, 0)]
    me = (lax.axis_index("col") * 2 + lax.axis_index("row")).astype(jnp.int32).reshape(1)
    index = delta_index.reshape(-1)
    count = delta_count.reshape(-1)
    order_table = jnp.asarray(order.reshape(-1))

    part = tokens.shape[1] // STREAMS
    own = [tokens[:, k * part : (k + 1) * part] for k in range(STREAMS)]
    buffers = [own]
    pieces = {}

    def step(d, k, fwd, bwd, after):
        fwd, bwd = tie((fwd, bwd), after)
        if d == half:
            return (lax.ppermute(fwd, "col", ahead),) * 2 if k < STREAMS // 2 else (lax.ppermute(bwd, "col", behind),) * 2
        return lax.ppermute(fwd, "col", ahead), lax.ppermute(bwd, "col", behind)

    def run(number, acc):
        lists = phases[number]
        most = max(1, max(len(lists[c][r]) for c in range(n_col) for r in range(2)))
        used_t = sorted({t for c in range(n_col) for r in range(2) for t, _ in lists[c][r]})
        used_p = sorted({p for c in range(n_col) for r in range(2) for _, p in lists[c][r]})
        final = number == len(events) - 1
        used_k = sorted({kept[c][r] for c in range(n_col) for r in range(2)}) if final else []
        table = np.zeros((n_col, 2, 2 + 2 * most), np.int32)
        for c in range(n_col):
            for r in range(2):
                table[c, r, 0] = len(lists[c][r])
                if final:
                    table[c, r, 1] = used_k.index(kept[c][r])
                for i, (t, p) in enumerate(lists[c][r]):
                    table[c, r, 2 + 2 * i] = used_t.index(t)
                    table[c, r, 3 + 2 * i] = used_p.index(p)

        def space(p):
            return pl.ANY if p < half else pltpu.HBM

        keep = ([pieces[p] for p in used_k], [space(p) for p in used_k]) if final else None
        return phase(
            me,
            jnp.asarray(table.reshape(-1)),
            [buffers[t] for t in used_t],
            [pieces[p] for p in used_p],
            [space(p) for p in used_p],
            acc,
            most,
            keep,
        )

    arrived = [step(1, k, own[k], own[k], ()) for k in range(STREAMS)]
    merged = []
    for j in range(half):
        merged.append(merge(me, order_table, index, count, base_weight, delta_values, j, half))
        pieces[j] = merged[j]
    pieces[half] = lax.ppermute(merged[0], "row", swap)

    acc = None
    sent = 1
    for d in range(1, half):
        for k in range(STREAMS):
            if sent < half:
                (piece,) = tie((merged[sent],), arrived[k])
                pieces[half + sent] = lax.ppermute(piece, "row", swap)
                sent += 1
        buffers += [[arrived[k][0] for k in range(STREAMS)], [arrived[k][1] for k in range(STREAMS)]]
        gates = [[acc]] * STREAMS if acc is not None else [[merged[half // 2]], [merged[half - 1]]]
        arrived = [step(d + 1, k, arrived[k][0], arrived[k][1], gates[k]) for k in range(STREAMS)]
        out = run(d - 1, acc)
        acc = out[0]
    return last_phase([arrived[k][0] for k in range(STREAMS)], out[1], acc, jnp.bfloat16)


def solution(mesh):
    spec = P(("tenant", "row"), "col")
    return jax.shard_map(
        functools.partial(body, n_col=mesh.shape["col"]),
        mesh=mesh,
        in_specs=(spec, P("row", "col"), spec, spec, spec),
        out_specs=spec,
        check_vma=False,
    )
```

time: 298 us -> 133 us (0.45)
  local copies, waits for them, and re-layouts: 153 us -> 29.8 us
  waiting for transfers between devices: 87.6 us -> 6.72 us
  Pallas kernels: 0 us -> 77 us
  matrix products: 38.6 us -> 0 us
  starting transfers between devices: 0.04 us -> 15.6 us
  between operations: 14.1 us -> 0.91 us
    all_gather x2 -> x0, waiting for transfers between devices: 86.9 us -> none  [the longest x1 86.8 us: body(): effective = lax.all_gather(merged, 'row', axis=0, tiled=True)]
    pallas_call x0 -> x8, Pallas kernels: none -> 77 us  [the longest x3 45.5 us: phase(): pl.pallas_call(kernel, in_specs=specs(in_spaces), out_specs=specs([pltpu....]
    reshape x2 -> x0, local copies, waits for them, and re-layouts: 69.6 us -> none  [apply_delta(): grid = weight.reshape(row_blocks, block, col_blocks, block)]
    scatter x2 -> x0, local copies, waits for them, and re-layouts: 46.5 us -> none  [apply_delta(): grid = grid.at[target_row, :, col_block, :].set(updated, mode='drop')]
    dot_general x1 -> x0, matrix products: 38.6 us -> none  [body(): jnp.dot(lax.all_gather(tokens, 'col', axis=1, tiled=True), effective, pre...]
    ppermute x0 -> x18, starting transfers between devices: none -> 15.6 us  [the longest x12 13.4 us: step(): return (lax.ppermute(fwd, 'col', ahead), lax.ppermute(bwd, 'col', behind))]
    gather x1 -> x0, local copies, waits for them, and re-layouts: 10.5 us -> none  [apply_delta(): current = grid[safe_row, :, col_block, :]]
    unnamed x3 -> x38, local copies, waits for them, and re-layouts: 20.5 us -> 28.5 us
  transfers between devices with their start and end apart: 2 -> 18, of which waited for: 1 -> 1; matrix products, arithmetic and copies ran while one was open for 50% -> 0% of each run, Pallas kernels for 0% -> 55%
where the time goes in v1:
time: 133 us; the launch traced here: 130 us
  Pallas kernels  77 us (58%)
  local copies, waits for them, and re-layouts  29.8 us (22%)
  starting transfers between devices  15.6 us (12%)
  waiting for transfers between devices  6.72 us (5%)
    pallas_call x3, Pallas kernels, phase(): pl.pallas_call(kernel, in_specs=specs(in_spaces), out_specs=specs([pltpu....  45.5 us
    unnamed x38, local copies, waits for them, and re-layouts  28.5 us
    pallas_call x4, Pallas kernels, merge(): pl.pallas_call(kernel, in_specs=[pl.BlockSpec(memory_space=pltpu.SMEM)] *...  25.4 us
    ppermute x12, starting transfers between devices, step(): return (lax.ppermute(fwd, 'col', ahead), lax.ppermute(bwd, 'col', behind))  13.4 us
    ppermute x12, waiting for transfers between devices, step(): return (lax.ppermute(fwd, 'col', ahead), lax.ppermute(bwd, 'col', behind))  6.71 us
    pallas_call x1, Pallas kernels, last_phase(): pl.pallas_call(kernel, in_specs=[pl.BlockSpec(memory_space=pltpu.VMEM)] *...  6.1 us
  transfers between devices with their start and end apart: 18, of which 1 were waited for; matrix products, arithmetic and copies ran while one was open for 0% of the time, Pallas kernels for 55%

profile of v1, /device:TPU:0, one launch (start us, length us, event | category | flops | bytes accessed | tf_op | source)
XLA Modules:
  0.0 130.0 jit_solution(2742901442041165694)
XLA Ops:
  0.0 1.3 fusion
  1.3 3.1 %collective-permute-start = (bf16[512,512]{1,0:T(8,128)(2,1)S(1)}, bf16[512,512]{1,0:T(8,128)(2,1)S(1)}, u32[]{:S(2)}, u32[]{:S(2)}) collective-permute-start(bf16[512,512]{1,0:T(8,128)(2,1)S(1)} %get-tuple-element.25.refs_0_), channel_id=1, source_target_pairs={{0,2},{2,4},{4,6},{6,7},{7,5},{5,3},{3,1},{1,0},{8,10},{10,12},{12... | collective-permute-start | bytes 1572872 | tf_op jit(solution)/shard_map/ppermute | solution.py:336
  4.3 0.0 collective-permute-start.1
  4.4 2.0 %collective-permute-start.4 = (bf16[512,512]{1,0:T(8,128)(2,1)S(1)}, bf16[512,512]{1,0:T(8,128)(2,1)S(1)}, u32[]{:S(2)}, u32[]{:S(2)}) collective-permute-start(bf16[512,512]{1,0:T(8,128)(2,1)S(1)} %get-tuple-element.29.refs_1_), channel_id=1, source_target_pairs={{0,2},{2,4},{4,6},{6,7},{7,5},{5,3},{3,1},{1,0},{8,10},{10,12},{12... | collective-permute-start | bytes 1572872 | tf_op jit(solution)/shard_map/ppermute | solution.py:336
  7.0 0.0 copy-start.10
  7.0 0.6 copy-done.10
  7.7 0.7 copy-done.12
  8.3 5.2 %merge0.1.refs_6_.refs_8_ = bf16[1024,3584]{1,0:T(8,128)(2,1)S(1)} custom-call(s32[1]{0:T(128)} %bitcast.me_ref, s32[64]{0:T(128)S(1)} %copy-done.12, s32[48]{0:T(128)S(1)} %bitcast.7, s32[1]{0:T(128)} %bitcast.4.count_ref, bf16[4096,3584]{1,0:T(8,128)(2,1)} %w_ref.7, bf16[6144,128]{1,0:T(8,128)(2,1)} %values_ref.7), custom_call_target="tpu_custom_call" | custom-call | tf_op jit(solution)/shard_map/merge0/pallas_call | solution.py:108
  13.6 0.1 collective-permute-start.6
  13.7 0.1 collective-permute-start.5
  13.7 7.3 %merge1.1.refs_7_.refs_9_.refs_4_ = bf16[1024,3584]{1,0:T(8,128)(2,1)S(1)} custom-call(s32[1]{0:T(128)} %bitcast.me_ref, s32[64]{0:T(128)S(1)} %copy-done.13, s32[48]{0:T(128)S(1)} %bitcast.8, s32[1]{0:T(128)} %bitcast.5.count_ref, bf16[4096,3584]{1,0:T(8,128)(2,1)} %w_ref.7, bf16[6144,128]{1,0:T(8,128)(2,1)} %values_ref.7), custom_call_target="tpu_custom_call" | custom-call | tf_op jit(solution)/shard_map/merge1/pallas_call | solution.py:108
  21.0 7.4 %merge2.1.refs_8_.refs_10_.refs_5_ = bf16[1024,3584]{1,0:T(8,128)(2,1)S(1)} custom-call(s32[1]{0:T(128)} %bitcast.me_ref, s32[64]{0:T(128)S(1)} %copy-done.13, s32[48]{0:T(128)S(1)} %bitcast.9, s32[1]{0:T(128)} %bitcast.3.count_ref, bf16[4096,3584]{1,0:T(8,128)(2,1)} %w_ref.7, bf16[6144,128]{1,0:T(8,128)(2,1)} %values_ref.7), custom_call_target="tpu_custom_call" | custom-call | tf_op jit(solution)/shard_map/merge2/pallas_call | solution.py:108
  28.4 0.0 collective-permute-done.refs_2_.refs_0_
  28.5 0.1 collective-permute-start.7
  28.5 0.3 collective-permute-start.2
  28.8 0.0 collective-permute-done.4.refs_3_.refs_1_
  28.8 1.8 %collective-permute-start.3 = (bf16[512,512]{1,0:T(8,128)(2,1)S(1)}, bf16[512,512]{1,0:T(8,128)(2,1)S(1)}, u32[]{:S(2)}, u32[]{:S(2)}) collective-permute-start(bf16[512,512]{1,0:T(8,128)(2,1)S(1)} %collective-permute-done.1.refs_4_.refs_2_), channel_id=1, source_target_pairs={{2,0},{4,2},{6,4},{7,6},{5,7},{3,5},{1,3},{0,1},{10,8},{12,10},{14... | collective-permute-start | bytes 1572872 | tf_op jit(solution)/shard_map/ppermute | solution.py:336
  30.6 0.0 collective-permute-done.5.refs_5_.refs_3_
  30.6 0.0 collective-permute-start.12
  30.6 5.5 %merge3.1.refs_11_.refs_6_.refs_10_ = bf16[1024,3584]{1,0:T(8,128)(2,1)S(1)} custom-call(s32[1]{0:T(128)} %bitcast.me_ref, s32[64]{0:T(128)S(1)} %copy-done.13, s32[48]{0:T(128)S(1)} %bitcast.10, s32[1]{0:T(128)} %bitcast.6.count_ref, bf16[4096,3584]{1,0:T(8,128)(2,1)} %w_ref.7, bf16[6144,128]{1,0:T(8,128)(2,1)} %values_ref.7), custom_call_target="tpu_custom_call" | custom-call | tf_op jit(solution)/shard_map/merge3/pallas_call | solution.py:108
  36.2 0.0 copy-start.14
  36.2 6.7 %collective-permute-done.2.refs_4_ = bf16[512,512]{1,0:T(8,128)(2,1)S(1)} collective-permute-done((bf16[512,512]{1,0:T(8,128)(2,1)S(1)}, bf16[512,512]{1,0:T(8,128)(2,1)S(1)}, u32[]{:S(2)}, u32[]{:S(2)}) %collective-permute-start.2) | collective-permute-done | bytes 524320 | tf_op jit(solution)/shard_map/ppermute | solution.py:336
  42.9 0.0 collective-permute-done.3.refs_6_
  42.9 2.1 %collective-permute-start.10 = (bf16[512,512]{1,0:T(8,128)(2,1)S(1)}, bf16[512,512]{1,0:T(8,128)(2,1)S(1)}, u32[]{:S(2)}, u32[]{:S(2)}) collective-permute-start(bf16[512,512]{1,0:T(8,128)(2,1)S(1)} %collective-permute-done.4.refs_3_.refs_1_), channel_id=1, source_target_pairs={{0,2},{2,4},{4,6},{6,7},{7,5},{5,3},{3,1},{1,0},{8,10},{10,12},{12... | collective-permute-start | bytes 1572872 | tf_op jit(solution)/shard_map/ppermute | solution.py:336
  45.0 0.0 collective-permute-done.6.refs_9_.refs_12_
  45.0 0.0 collective-permute-start.11
  45.0 3.0 %copy-done.18 = bf16[1024,3584]{1,0:T(8,128)(2,1)} copy-done((bf16[1024,3584]{1,0:T(8,128)(2,1)}, bf16[1024,3584]{1,0:T(8,128)(2,1)S(1)}, u32[]{:S(2)}) %copy-start.18) | copy-done | bytes 7340056
  48.0 0.0 collective-permute-done.7.refs_10_.refs_13_.refs_7_
  48.0 2.9 %copy-done.17 = bf16[1024,3584]{1,0:T(8,128)(2,1)} copy-done((bf16[1024,3584]{1,0:T(8,128)(2,1)}, bf16[1024,3584]{1,0:T(8,128)(2,1)S(1)}, u32[]{:S(2)}) %copy-start.17) | copy-done | bytes 7340056
  50.9 19.8 %phase.3.refs_16_ = f32[512,3584]{1,0:T(8,128)S(1)} custom-call(s32[1]{0:T(128)} %bitcast.me_ref, s32[128]{0:T(128)S(1)} %copy-done.15, bf16[512,512]{1,0:T(8,128)(2,1)S(1)} %get-tuple-element.25.refs_0_, bf16[512,512]{1,0:T(8,128)(2,1)S(1)} %get-tuple-element.29.refs_1_, bf16[512,512]{1,0:T(8,128)(2,1)S(1)} %collective-permute-done.refs_2_.refs_0_, ...), custom_call_target="tpu_custom_call" | custom-call | tf_op jit(solution)/shard_map/phase/pallas_call | solution.py:249
  70.7 2.9 %copy-done.4 = f32[512,3584]{1,0:T(8,128)} copy-done((f32[512,3584]{1,0:T(8,128)}, f32[512,3584]{1,0:T(8,128)S(1)}, u32[]{:S(2)}) %copy-start.4) | copy-done | bytes 7340056
  73.7 1.3 collective-permute-start.15
  75.0 0.8 collective-permute-start.16
  75.7 1.3 collective-permute-start.8
  77.0 0.8 collective-permute-start.9
  77.7 0.0 collective-permute-done.13.refs_15_.refs_9_.refs_11_
  77.8 3.1 %copy-done.1 = bf16[1024,3584]{1,0:T(8,128)(2,1)S(1)} copy-done((bf16[1024,3584]{1,0:T(8,128)(2,1)S(1)}, bf16[1024,3584]{1,0:T(8,128)(2,1)}, u32[]{:S(2)}) %copy-start.1) | copy-done | bytes 7340056
  80.8 3.1 %copy-done.3 = bf16[1024,3584]{1,0:T(8,128)(2,1)S(1)} copy-done((bf16[1024,3584]{1,0:T(8,128)(2,1)S(1)}, bf16[1024,3584]{1,0:T(8,128)(2,1)}, u32[]{:S(2)}) %copy-start.3) | copy-done | bytes 7340056
  83.9 3.1 %copy-done.5 = f32[512,3584]{1,0:T(8,128)S(1)} copy-done((f32[512,3584]{1,0:T(8,128)S(1)}, f32[512,3584]{1,0:T(8,128)}, u32[]{:S(2)}) %copy-start.5) | copy-done | bytes 7340056
  87.0 3.1 %copy-done.9 = bf16[1024,3584]{1,0:T(8,128)(2,1)S(1)} copy-done((bf16[1024,3584]{1,0:T(8,128)(2,1)S(1)}, bf16[1024,3584]{1,0:T(8,128)(2,1)}, u32[]{:S(2)}) %copy-start.9) | copy-done | bytes 7340056
  90.1 12.2 %phase.4.refs_12_ = f32[512,3584]{1,0:T(8,128)S(1)} custom-call(s32[1]{0:T(128)} %bitcast.me_ref, s32[128]{0:T(128)S(1)} %copy-done.14, bf16[512,512]{1,0:T(8,128)(2,1)S(1)} %collective-permute-done.refs_2_.refs_0_, bf16[512,512]{1,0:T(8,128)(2,1)S(1)} %collective-permute-done.4.refs_3_.refs_1_, ...), custom_call_target="tpu_custom_call", output_to_operand_aliasing={{}: (18, {})} | custom-call | tf_op jit(solution)/shard_map/phase/pallas_call | solution.py:249
  102.3 0.0 collective-permute-done.16.refs_3_
  102.4 0.1 collective-permute-start.17
  102.4 2.0 %collective-permute-start.14 = (bf16[512,512]{1,0:T(8,128)(2,1)S(1)}, bf16[512,512]{1,0:T(8,128)(2,1)S(1)}, u32[]{:S(2)}, u32[]{:S(2)}) collective-permute-start(bf16[512,512]{1,0:T(8,128)(2,1)S(1)} %collective-permute-done.8.refs_0_), channel_id=1, source_target_pairs={{0,2},{2,4},{4,6},{6,7},{7,5},{5,3},{3,1},{1,0},{8,10},{10,12},{12... | collective-permute-start | bytes 1572872 | tf_op jit(solution)/shard_map/ppermute | solution.py:335
  104.4 13.4 %phase.5 = (f32[512,3584]{1,0:T(8,128)S(1)}, bf16[1024,3584]{1,0:T(8,128)(2,1)S(1)}) custom-call(s32[1]{0:T(128)} %bitcast.me_ref, s32[96]{0:T(128)S(1)} %copy-done.16, bf16[512,512]{1,0:T(8,128)(2,1)S(1)} %collective-permute-done.8.refs_0_, bf16[512,512]{1,0:T(8,128)(2,1)S(1)} %collective-permute-done.15.refs_1_, ...), custom_call_target="tpu_custom_call", output_to_operand_aliasing={{0}: (14, {})} | custom-call | tf_op jit(solution)/shard_map/phase/pallas_call | solution.py:249
  117.9 2.9 %copy-done.6 = f32[512,3584]{1,0:T(8,128)} copy-done((f32[512,3584]{1,0:T(8,128)}, f32[512,3584]{1,0:T(8,128)S(1)}, u32[]{:S(2)}) %copy-start.6) | copy-done | bytes 7340056
  120.8 3.1 %copy-done.7 = f32[512,3584]{1,0:T(8,128)S(1)} copy-done((f32[512,3584]{1,0:T(8,128)S(1)}, f32[512,3584]{1,0:T(8,128)}, u32[]{:S(2)}) %copy-start.7) | copy-done | bytes 7340056
  123.9 6.1 %last_phase.1 = bf16[512,3584]{1,0:T(8,128)(2,1)} custom-call(bf16[512,512]{1,0:T(8,128)(2,1)S(1)} %collective-permute-done.14.refs_0_, bf16[512,512]{1,0:T(8,128)(2,1)S(1)} %collective-permute-done.17.refs_1_, bf16[1024,3584]{1,0:T(8,128)(2,1)S(1)} %get-tuple-element.41.refs_2_, f32[512,3584]{1,0:T(8,128)S(1)} %copy-done.7), custom_call_target="tpu_custom_call" | custom-call | tf_op jit(solution)/shard_map/last_phase/pallas_call | solution.py:304
  (35 shorter events, 0.1 us)
Async XLA Ops:
  1.3 27.2 %collective-permute-start = (bf16[512,512]{1,0:T(8,128)(2,1)S(1)}, bf16[512,512]{1,0:T(8,128)(2,1)S(1)}, u32[]{:S(2)}, u32[]{:S(2)}) collective-permute-start(bf16[512,512]{1,0:T(8,128)(2,1)S(1)} %get-tuple-element.25.refs_0_), channel_id=1, source_target_pairs={{0,2},{2,4},{4,6},{6,7},{7,5},{5,3},{3,1},{1,0},{8,10},{10,12},{12... | collective-permute-start | bytes 1572872 | tf_op jit(solution)/shard_map/ppermute | solution.py:336
  4.3 24.1 %collective-permute-start.1 = (bf16[512,512]{1,0:T(8,128)(2,1)S(1)}, bf16[512,512]{1,0:T(8,128)(2,1)S(1)}, u32[]{:S(2)}, u32[]{:S(2)}) collective-permute-start(bf16[512,512]{1,0:T(8,128)(2,1)S(1)} %get-tuple-element.25.refs_0_), channel_id=1, source_target_pairs={{2,0},{4,2},{6,4},{7,6},{5,7},{3,5},{1,3},{0,1},{10,8},{12,10},{14... | collective-permute-start | bytes 1572872 | tf_op jit(solution)/shard_map/ppermute | solution.py:336
  4.4 24.5 %collective-permute-start.4 = (bf16[512,512]{1,0:T(8,128)(2,1)S(1)}, bf16[512,512]{1,0:T(8,128)(2,1)S(1)}, u32[]{:S(2)}, u32[]{:S(2)}) collective-permute-start(bf16[512,512]{1,0:T(8,128)(2,1)S(1)} %get-tuple-element.29.refs_1_), channel_id=1, source_target_pairs={{0,2},{2,4},{4,6},{6,7},{7,5},{5,3},{3,1},{1,0},{8,10},{10,12},{12... | collective-permute-start | bytes 1572872 | tf_op jit(solution)/shard_map/ppermute | solution.py:336
  7.0 0.7 copy-start.10
  7.7 0.7 copy-start.12
  8.3 5.4 %copy-start.11 = (s32[48,1]{0,1:T(1,128)S(1)}, s32[48,1]{0,1:T(1,128)}, u32[]{:S(2)}) copy-start(s32[48,1]{0,1:T(1,128)} %param.12) | copy-start | bytes 580
  8.3 5.4 %copy-start.13 = (s32[64]{0:T(128)S(1)}, s32[64]{0:T(128)}, u32[]{:S(2)}) copy-start(s32[64]{0:T(128)} %constant.19.clone.order_ref) | copy-start | bytes 772
  13.6 34.4 %copy-start.8 = (bf16[1024,3584]{1,0:T(8,128)(2,1)}, bf16[1024,3584]{1,0:T(8,128)(2,1)S(1)}, u32[]{:S(2)}) copy-start(bf16[1024,3584]{1,0:T(8,128)(2,1)S(1)} %merge0.1.refs_6_.refs_8_) | copy-start | bytes 22020100
  13.6 31.4 %collective-permute-start.6 = (bf16[1024,3584]{1,0:T(8,128)(2,1)S(1)}, bf16[1024,3584]{1,0:T(8,128)(2,1)S(1)}, u32[]{:S(2)}, u32[]{:S(2)}) collective-permute-start(bf16[1024,3584]{1,0:T(8,128)(2,1)S(1)} %merge0.1.refs_6_.refs_8_), channel_id=1, source_target_pairs={{0,8},{8,0},{1,9},{9,1},{2,10},{10,2},{3,11},{11,3},{4,12},{12,4},... | collective-permute-start | bytes 22020104 | tf_op jit(solution)/shard_map/ppermute | solution.py:375
  13.7 17.0 %collective-permute-start.5 = (bf16[512,512]{1,0:T(8,128)(2,1)S(1)}, bf16[512,512]{1,0:T(8,128)(2,1)S(1)}, u32[]{:S(2)}, u32[]{:S(2)}) collective-permute-start(bf16[512,512]{1,0:T(8,128)(2,1)S(1)} %get-tuple-element.29.refs_1_), channel_id=1, source_target_pairs={{2,0},{4,2},{6,4},{7,6},{5,7},{3,5},{1,3},{0,1},{10,8},{12,10},{14... | collective-permute-start | bytes 1572872 | tf_op jit(solution)/shard_map/ppermute | solution.py:336
  21.0 26.9 %copy-start = (bf16[1024,3584]{1,0:T(8,128)(2,1)}, bf16[1024,3584]{1,0:T(8,128)(2,1)S(1)}, u32[]{:S(2)}) copy-start(bf16[1024,3584]{1,0:T(8,128)(2,1)S(1)} %merge1.1.refs_7_.refs_9_.refs_4_) | copy-start | bytes 22020100
  28.4 19.5 %copy-start.2 = (bf16[1024,3584]{1,0:T(8,128)(2,1)}, bf16[1024,3584]{1,0:T(8,128)(2,1)S(1)}, u32[]{:S(2)}) copy-start(bf16[1024,3584]{1,0:T(8,128)(2,1)S(1)} %merge2.1.refs_8_.refs_10_.refs_5_) | copy-start | bytes 22020100
  28.5 19.5 %collective-permute-start.7 = (bf16[1024,3584]{1,0:T(8,128)(2,1)S(1)}, bf16[1024,3584]{1,0:T(8,128)(2,1)S(1)}, u32[]{:S(2)}, u32[]{:S(2)}) collective-permute-start(bf16[1024,3584]{1,0:T(8,128)(2,1)S(1)} %merge1.1.refs_7_.refs_9_.refs_4_), channel_id=1, source_target_pairs={{0,8},{8,0},{1,9},{9,1},{2,10},{10,2},{3,11},{11,3},{4,12},{12,4},... | collective-permute-start | bytes 22020104 | tf_op jit(solution)/shard_map/ppermute | solution.py:383
  28.5 14.3 %collective-permute-start.2 = (bf16[512,512]{1,0:T(8,128)(2,1)S(1)}, bf16[512,512]{1,0:T(8,128)(2,1)S(1)}, u32[]{:S(2)}, u32[]{:S(2)}) collective-permute-start(bf16[512,512]{1,0:T(8,128)(2,1)S(1)} %collective-permute-done.refs_2_.refs_0_), channel_id=1, source_target_pairs={{0,2},{2,4},{4,6},{6,7},{7,5},{5,3},{3,1},{1,0},{8,10},{10,12},{12... | collective-permute-start | bytes 1572872 | tf_op jit(solution)/shard_map/ppermute | solution.py:336
  28.8 14.1 %collective-permute-start.3 = (bf16[512,512]{1,0:T(8,128)(2,1)S(1)}, bf16[512,512]{1,0:T(8,128)(2,1)S(1)}, u32[]{:S(2)}, u32[]{:S(2)}) collective-permute-start(bf16[512,512]{1,0:T(8,128)(2,1)S(1)} %collective-permute-done.1.refs_4_.refs_2_), channel_id=1, source_target_pairs={{2,0},{4,2},{6,4},{7,6},{5,7},{3,5},{1,3},{0,1},{10,8},{12,10},{14... | collective-permute-start | bytes 1572872 | tf_op jit(solution)/shard_map/ppermute | solution.py:336
  30.6 46.4 %collective-permute-start.12 = (bf16[1024,3584]{1,0:T(8,128)(2,1)S(1)}, bf16[1024,3584]{1,0:T(8,128)(2,1)}, u32[]{:S(2)}, u32[]{:S(2)}) collective-permute-start(bf16[1024,3584]{1,0:T(8,128)(2,1)S(1)} %merge2.1.refs_8_.refs_10_.refs_5_), channel_id=1, source_target_pairs={{0,8},{8,0},{1,9},{9,1},{2,10},{10,2},{3,11},{11,3},{4,12},{12,4},... | collective-permute-start | bytes 22020104 | tf_op jit(solution)/shard_map/ppermute | solution.py:383
  30.6 20.3 %copy-start.15 = (s32[128]{0:T(128)S(1)}, s32[128]{0:T(128)}, u32[]{:S(2)}) copy-start(s32[128]{0:T(128)} %constant.20.clone.table_ref) | copy-start | bytes 1540
  36.2 41.6 %copy-start.14 = (s32[128]{0:T(128)S(1)}, s32[128]{0:T(128)}, u32[]{:S(2)}) copy-start(s32[128]{0:T(128)} %constant.21.clone.table_ref) | copy-start | bytes 1540
  42.9 34.9 %collective-permute-start.13 = (bf16[1024,3584]{1,0:T(8,128)(2,1)S(1)}, bf16[1024,3584]{1,0:T(8,128)(2,1)}, u32[]{:S(2)}, u32[]{:S(2)}) collective-permute-start(bf16[1024,3584]{1,0:T(8,128)(2,1)S(1)} %merge3.1.refs_11_.refs_6_.refs_10_), channel_id=1, source_target_pairs={{0,8},{8,0},{1,9},{9,1},{2,10},{10,2},{3,11},{11,3},{4,12},{12,4},... | collective-permute-start | bytes 22020104 | tf_op jit(solution)/shard_map/ppermute | solution.py:383
  42.9 30.8 %collective-permute-start.10 = (bf16[512,512]{1,0:T(8,128)(2,1)S(1)}, bf16[512,512]{1,0:T(8,128)(2,1)S(1)}, u32[]{:S(2)}, u32[]{:S(2)}) collective-permute-start(bf16[512,512]{1,0:T(8,128)(2,1)S(1)} %collective-permute-done.4.refs_3_.refs_1_), channel_id=1, source_target_pairs={{0,2},{2,4},{4,6},{6,7},{7,5},{5,3},{3,1},{1,0},{8,10},{10,12},{12... | collective-permute-start | bytes 1572872 | tf_op jit(solution)/shard_map/ppermute | solution.py:336
  45.0 3.0 %copy-start.18 = (bf16[1024,3584]{1,0:T(8,128)(2,1)}, bf16[1024,3584]{1,0:T(8,128)(2,1)S(1)}, u32[]{:S(2)}) copy-start(bf16[1024,3584]{1,0:T(8,128)(2,1)S(1)} %collective-permute-done.6.refs_9_.refs_12_) | copy-start | bytes 22020100
  45.0 28.7 %collective-permute-start.11 = (bf16[512,512]{1,0:T(8,128)(2,1)S(1)}, bf16[512,512]{1,0:T(8,128)(2,1)S(1)}, u32[]{:S(2)}, u32[]{:S(2)}) collective-permute-start(bf16[512,512]{1,0:T(8,128)(2,1)S(1)} %collective-permute-done.5.refs_5_.refs_3_), channel_id=1, source_target_pairs={{2,0},{4,2},{6,4},{7,6},{5,7},{3,5},{1,3},{0,1},{10,8},{12,10},{14... | collective-permute-start | bytes 1572872 | tf_op jit(solution)/shard_map/ppermute | solution.py:336
  48.0 2.9 %copy-start.17 = (bf16[1024,3584]{1,0:T(8,128)(2,1)}, bf16[1024,3584]{1,0:T(8,128)(2,1)S(1)}, u32[]{:S(2)}) copy-start(bf16[1024,3584]{1,0:T(8,128)(2,1)S(1)} %collective-permute-done.7.refs_10_.refs_13_.refs_7_) | copy-start | bytes 22020100
  50.9 53.5 %copy-start.16 = (s32[96]{0:T(128)S(1)}, s32[96]{0:T(128)}, u32[]{:S(2)}) copy-start(s32[96]{0:T(128)} %constant.22.clone.table_ref) | copy-start | bytes 1156
  70.7 2.9 %copy-start.4 = (f32[512,3584]{1,0:T(8,128)}, f32[512,3584]{1,0:T(8,128)S(1)}, u32[]{:S(2)}) copy-start(f32[512,3584]{1,0:T(8,128)S(1)} %phase.3.refs_16_) | copy-start | bytes 22020100
  73.7 28.6 %collective-permute-start.15 = (bf16[512,512]{1,0:T(8,128)(2,1)S(1)}, bf16[512,512]{1,0:T(8,128)(2,1)S(1)}, u32[]{:S(2)}, u32[]{:S(2)}) collective-permute-start(bf16[512,512]{1,0:T(8,128)(2,1)S(1)} %collective-permute-done.10.refs_5_), channel_id=1, source_target_pairs={{0,2},{2,4},{4,6},{6,7},{7,5},{5,3},{3,1},{1,0},{8,10},{10,12},{12... | collective-permute-start | bytes 1572872 | tf_op jit(solution)/shard_map/ppermute | solution.py:336
  75.0 27.4 %collective-permute-start.16 = (bf16[512,512]{1,0:T(8,128)(2,1)S(1)}, bf16[512,512]{1,0:T(8,128)(2,1)S(1)}, u32[]{:S(2)}, u32[]{:S(2)}) collective-permute-start(bf16[512,512]{1,0:T(8,128)(2,1)S(1)} %collective-permute-done.11.refs_7_), channel_id=1, source_target_pairs={{2,0},{4,2},{6,4},{7,6},{5,7},{3,5},{1,3},{0,1},{10,8},{12,10},{14... | collective-permute-start | bytes 1572872 | tf_op jit(solution)/shard_map/ppermute | solution.py:336
  75.7 26.6 %collective-permute-start.8 = (bf16[512,512]{1,0:T(8,128)(2,1)S(1)}, bf16[512,512]{1,0:T(8,128)(2,1)S(1)}, u32[]{:S(2)}, u32[]{:S(2)}) collective-permute-start(bf16[512,512]{1,0:T(8,128)(2,1)S(1)} %collective-permute-done.2.refs_4_), channel_id=1, source_target_pairs={{0,2},{2,4},{4,6},{6,7},{7,5},{5,3},{3,1},{1,0},{8,10},{10,12},{12... | collective-permute-start | bytes 1572872 | tf_op jit(solution)/shard_map/ppermute | solution.py:336
  77.0 25.4 %collective-permute-start.9 = (bf16[512,512]{1,0:T(8,128)(2,1)S(1)}, bf16[512,512]{1,0:T(8,128)(2,1)S(1)}, u32[]{:S(2)}, u32[]{:S(2)}) collective-permute-start(bf16[512,512]{1,0:T(8,128)(2,1)S(1)} %collective-permute-done.3.refs_6_), channel_id=1, source_target_pairs={{2,0},{4,2},{6,4},{7,6},{5,7},{3,5},{1,3},{0,1},{10,8},{12,10},{14... | collective-permute-start | bytes 1572872 | tf_op jit(solution)/shard_map/ppermute | solution.py:336
  77.7 3.1 %copy-start.1 = (bf16[1024,3584]{1,0:T(8,128)(2,1)S(1)}, bf16[1024,3584]{1,0:T(8,128)(2,1)}, u32[]{:S(2)}) copy-start(bf16[1024,3584]{1,0:T(8,128)(2,1)} %copy-done) | copy-start | bytes 22020100
  80.8 3.1 %copy-start.3 = (bf16[1024,3584]{1,0:T(8,128)(2,1)S(1)}, bf16[1024,3584]{1,0:T(8,128)(2,1)}, u32[]{:S(2)}) copy-start(bf16[1024,3584]{1,0:T(8,128)(2,1)} %copy-done.2) | copy-start | bytes 22020100
  83.9 3.1 %copy-start.5 = (f32[512,3584]{1,0:T(8,128)S(1)}, f32[512,3584]{1,0:T(8,128)}, u32[]{:S(2)}) copy-start(f32[512,3584]{1,0:T(8,128)} %copy-done.4) | copy-start | bytes 22020100
  87.0 3.1 %copy-start.9 = (bf16[1024,3584]{1,0:T(8,128)(2,1)S(1)}, bf16[1024,3584]{1,0:T(8,128)(2,1)}, u32[]{:S(2)}) copy-start(bf16[1024,3584]{1,0:T(8,128)(2,1)} %copy-done.8) | copy-start | bytes 22020100
  102.4 18.4 %collective-permute-start.17 = (bf16[512,512]{1,0:T(8,128)(2,1)S(1)}, bf16[512,512]{1,0:T(8,128)(2,1)S(1)}, u32[]{:S(2)}, u32[]{:S(2)}) collective-permute-start(bf16[512,512]{1,0:T(8,128)(2,1)S(1)} %collective-permute-done.16.refs_3_), channel_id=1, source_target_pairs={{2,0},{4,2},{6,4},{7,6},{5,7},{3,5},{1,3},{0,1},{10,8},{12,10},{14... | collective-permute-start | bytes 1572872 | tf_op jit(solution)/shard_map/ppermute | solution.py:335
  102.4 18.4 %collective-permute-start.14 = (bf16[512,512]{1,0:T(8,128)(2,1)S(1)}, bf16[512,512]{1,0:T(8,128)(2,1)S(1)}, u32[]{:S(2)}, u32[]{:S(2)}) collective-permute-start(bf16[512,512]{1,0:T(8,128)(2,1)S(1)} %collective-permute-done.8.refs_0_), channel_id=1, source_target_pairs={{0,2},{2,4},{4,6},{6,7},{7,5},{5,3},{3,1},{1,0},{8,10},{10,12},{12... | collective-permute-start | bytes 1572872 | tf_op jit(solution)/shard_map/ppermute | solution.py:335
  117.9 2.9 %copy-start.6 = (f32[512,3584]{1,0:T(8,128)}, f32[512,3584]{1,0:T(8,128)S(1)}, u32[]{:S(2)}) copy-start(f32[512,3584]{1,0:T(8,128)S(1)} %get-tuple-element.42.refs_3_) | copy-start | bytes 22020100
  120.8 3.1 %copy-start.7 = (f32[512,3584]{1,0:T(8,128)S(1)}, f32[512,3584]{1,0:T(8,128)}, u32[]{:S(2)}) copy-start(f32[512,3584]{1,0:T(8,128)} %copy-done.6) | copy-start | bytes 22020100

commit v2 on v0

v2 whole, which is shorter than its diff:
```python
import functools

import jax
import jax.numpy as jnp
import numpy as np
from jax import lax
from jax.experimental import pallas as pl
from jax.experimental.pallas import tpu as pltpu
from jax.sharding import PartitionSpec as P

MERGE_VMEM = 10
PHASE_VMEM = 28


def ring_order(n):
    return list(range(0, n, 2)) + list(range(n - 1, 0, -2))


def plan(n):
    ring = ring_order(n)
    place = {c: k for k, c in enumerate(ring)}
    half = n // 2
    order = np.zeros((n, 2, half), np.int32)
    meets = np.zeros((n, 2, n), np.int32)
    for col in range(n):
        me = place[col]

        def dist(c):
            ahead = (place[c] - me) % n
            return min(ahead, n - ahead)

        def token_id(c):
            ahead = (place[c] - me) % n
            if ahead == 0:
                return 0
            if ahead == half:
                return n - 1
            return 2 * ahead if ahead < half else 2 * (n - ahead) - 1

        for h in range(2):
            chunks = sorted(range(h * half, (h + 1) * half), key=lambda c: (dist(c), c))
            order[col, h] = [c - h * half for c in chunks]
            for row in range(2):
                for j, c in enumerate(chunks):
                    meets[col, row, token_id(c)] = j if row == h else half + j
    return ring, order, meets.tolist()


def tie(values, after):
    n = len(values)

    def kernel(*refs):
        refs[-1][...] = jnp.zeros_like(refs[-1])

    return pl.pallas_call(
        kernel,
        in_specs=[pl.BlockSpec(memory_space=pl.ANY)] * (n + len(after)),
        out_specs=[pl.BlockSpec(memory_space=pl.ANY)] * n,
        out_shape=[jax.ShapeDtypeStruct(v.shape, v.dtype) for v in values],
        scratch_shapes=[pltpu.VMEM((8, 128), jnp.float32)],
        input_output_aliases={k: k for k in range(n)},
        compiler_params=pltpu.CompilerParams(vmem_limit_bytes=2**20),
        cost_estimate=pl.CostEstimate(flops=0, bytes_accessed=0, transcendentals=0),
        name="tie",
    )(*values, *after)


def hbm(x):
    return pltpu.with_memory_space_constraint(x, pltpu.HBM)


def merge(me, order, index, count, weight, values, piece, pieces, after=()):
    block = values.shape[1]
    blocks = weight.shape[0] // block // pieces
    width = weight.shape[1]
    col_blocks = width // block

    def kernel(me_ref, order_ref, index_ref, count_ref, w_ref, values_ref, *rest):
        out_ref, vbuf, wsem, vsem = rest[len(after) :]
        first = order_ref[me_ref[0] * pieces + piece] * blocks
        value_copy = pltpu.make_async_copy(values_ref, vbuf, vsem)
        value_copy.start()

        def copy(k):
            rows = pl.ds(pl.multiple_of((first + k) * block, block), block)
            return pltpu.make_async_copy(w_ref.at[rows], out_ref.at[pl.ds(k * block, block)], wsem.at[k])

        for k in range(blocks):
            copy(k).start()
        value_copy.wait()
        for k in range(blocks):
            copy(k).wait()

        def slot(s, carry):
            which = index_ref[s]
            row = which // col_blocks
            row_here = row - first

            @pl.when(jnp.logical_and(row_here >= 0, row_here < blocks))
            def _():
                rows = pl.ds(pl.multiple_of(row_here * block, block), block)
                cols = pl.ds(pl.multiple_of((which - row * col_blocks) * block, block), block)
                value = vbuf[pl.ds(pl.multiple_of(s * block, block), block), :]
                old = out_ref[rows, cols]
                out_ref[rows, cols] = (old.astype(jnp.float32) + value.astype(jnp.float32)).astype(out_ref.dtype)

            return carry

        lax.fori_loop(0, count_ref[0], slot, 0)

    return pl.pallas_call(
        kernel,
        in_specs=[pl.BlockSpec(memory_space=pltpu.SMEM)] * 4
        + [pl.BlockSpec(memory_space=pltpu.HBM)] * 2
        + [pl.BlockSpec(memory_space=pl.ANY)] * len(after),
        out_specs=pl.BlockSpec(memory_space=pltpu.VMEM),
        out_shape=pltpu.VMEM((blocks * block, width), weight.dtype),
        scratch_shapes=[
            pltpu.VMEM(values.shape, values.dtype),
            pltpu.SemaphoreType.DMA((blocks,)),
            pltpu.SemaphoreType.DMA,
        ],
        compiler_params=pltpu.CompilerParams(vmem_limit_bytes=MERGE_VMEM * 2**20),
        cost_estimate=pl.CostEstimate(flops=0, bytes_accessed=0, transcendentals=0),
        name=f"merge{piece}",
    )(me, order, index, count, hbm(weight), hbm(values), *after)


def tile_width(total):
    return 512 if total % 512 == 0 else total


def phase(me, table, counts, tokens, pieces, keep_pieces, accs, lo, hi):
    rows, depth = tokens[0].shape
    width = tile_width(pieces[0].shape[1])
    tiles = (hi - lo) // width
    n_tokens, n_pieces, n_keep, n_accs = len(tokens), len(pieces), len(keep_pieces), len(accs)
    starts = [0]
    for a in accs:
        starts.append(starts[-1] + a.shape[1] // width)
    most = max(counts)
    stride = 2 * most + 2

    def kernel(me_ref, table_ref, *refs):
        token_refs, refs = refs[:n_tokens], refs[n_tokens:]
        piece_refs, refs = refs[:n_pieces], refs[n_pieces:]
        keep_refs, refs = refs[:n_keep], refs[n_keep:]
        acc_refs, refs = refs[:n_accs], refs[n_accs:]
        out_ref, mark_ref, refs = refs[0], refs[1], refs[2:]
        if n_keep:
            kept_ref, refs = refs[0], refs[1:]
        tbuf, wbuf, abuf, tsem, wsem, asem, ksem = refs
        base = me_ref[0] * stride
        mark_ref[...] = jnp.zeros_like(mark_ref)

        def token_copy(ref, i):
            return pltpu.make_async_copy(ref, tbuf.at[:, pl.ds(i * depth, depth)], tsem.at[i])

        def piece_copy(ref, tile, i):
            slot = lax.rem(tile, 2)
            at = pl.ds(pl.multiple_of(lo + tile * width, 128), width)
            return pltpu.make_async_copy(ref.at[:, at], wbuf.at[slot, pl.ds(i * depth, depth)], wsem.at[slot, i])

        def acc_copy(ref, tile, start):
            slot = lax.rem(tile, 2)
            at = pl.ds(pl.multiple_of((tile - start) * width, 128), width)
            return pltpu.make_async_copy(ref.at[:, at], abuf.at[slot], asem.at[slot])

        def fetch(tile, count):
            for i in range(count):
                which = table_ref[base + 2 + 2 * i]
                for p in range(n_pieces):

                    @pl.when(which == p)
                    def _():
                        piece_copy(piece_refs[p], tile, i).start()

            for a in range(n_accs):

                @pl.when(jnp.logical_and(tile >= starts[a], tile < starts[a + 1]))
                def _():
                    acc_copy(acc_refs[a], tile, starts[a]).start()

        def work(count):
            for i in range(count):
                which = table_ref[base + 1 + 2 * i]
                for t in range(n_tokens):

                    @pl.when(which == t)
                    def _():
                        token_copy(token_refs[t], i).start()

            fetch(jnp.int32(0), count)
            for i in range(count):
                token_copy(token_refs[0], i).wait()

            def step(tile, carry):
                @pl.when(tile + 1 < tiles)
                def _():
                    fetch(tile + 1, count)

                slot = lax.rem(tile, 2)
                for i in range(count):
                    piece_copy(piece_refs[0], tile, i).wait()
                if n_accs:
                    acc_copy(acc_refs[0], tile, tile).wait()
                at = pl.ds(pl.multiple_of(tile * width, 128), width)
                deep = pl.ds(0, count * depth)
                product = jnp.dot(tbuf[:, deep], wbuf[slot, deep], preferred_element_type=jnp.float32)
                out_ref[:, at] = abuf[slot] + product if n_accs else product
                return carry

            lax.fori_loop(0, tiles, step, 0)

        if n_keep:
            which_kept = table_ref[base + stride - 1]
            for p in range(n_keep):

                @pl.when(which_kept == p)
                def _():
                    pltpu.make_async_copy(keep_refs[p], kept_ref, ksem).start()

        for count in counts:

            @pl.when(table_ref[base] == count)
            def _():
                work(count)

        if n_keep:
            pltpu.make_async_copy(keep_refs[0], kept_ref, ksem).wait()

    operands = [me, table] + list(tokens) + list(pieces) + list(keep_pieces) + list(accs)
    out_shape = [jax.ShapeDtypeStruct((rows, hi - lo), jnp.float32), jax.ShapeDtypeStruct((8, 128), jnp.float32)]
    if n_keep:
        out_shape.append(jax.ShapeDtypeStruct(pieces[0].shape, pieces[0].dtype))
    return pl.pallas_call(
        kernel,
        in_specs=[pl.BlockSpec(memory_space=pltpu.SMEM)] * 2 + [pl.BlockSpec(memory_space=pl.ANY)] * (len(operands) - 2),
        out_specs=[pl.BlockSpec(memory_space=pltpu.VMEM)] * len(out_shape),
        out_shape=out_shape,
        scratch_shapes=[
            pltpu.VMEM((rows, most * depth), tokens[0].dtype),
            pltpu.VMEM((2, most * depth, width), pieces[0].dtype),
            pltpu.VMEM((2, rows, width) if n_accs else (2, 8, 128), jnp.float32),
            pltpu.SemaphoreType.DMA((most,)),
            pltpu.SemaphoreType.DMA((2, most)),
            pltpu.SemaphoreType.DMA((2,)),
            pltpu.SemaphoreType.DMA,
        ],
        compiler_params=pltpu.CompilerParams(vmem_limit_bytes=PHASE_VMEM * 2**20),
        cost_estimate=pl.CostEstimate(flops=0, bytes_accessed=0, transcendentals=0),
        name="phase",
    )(*operands)


def last_phase(tokens, weight, acc, out_dtype):
    part, depth = tokens[0].shape
    rows = part * len(tokens)
    total = weight.shape[1]
    width = tile_width(total)
    tiles = total // width
    n = len(tokens)

    def kernel(*refs):
        token_refs = refs[:n]
        w_ref, acc_ref, out_ref, tbuf, obuf, tsem, osem = refs[n:]

        def store(tile):
            at = pl.ds(tile * width, width)
            return pltpu.make_async_copy(obuf.at[:, at], out_ref.at[:, at], osem.at[tile])

        copies = [
            pltpu.make_async_copy(token_refs[k], tbuf.at[pl.ds(k * part, part)], tsem.at[k]) for k in range(n)
        ]
        for copy in copies:
            copy.start()
        for copy in copies:
            copy.wait()
        for tile in range(tiles):
            at = pl.ds(tile * width, width)
            product = jnp.dot(tbuf[...], w_ref[:, at], preferred_element_type=jnp.float32)
            obuf[:, at] = (acc_ref[:, at] + product).astype(out_dtype)
            store(tile).start()
        for tile in range(tiles):
            store(tile).wait()

    return pl.pallas_call(
        kernel,
        in_specs=[pl.BlockSpec(memory_space=pl.ANY)] * n + [pl.BlockSpec(memory_space=pltpu.VMEM)] * 2,
        out_specs=pl.BlockSpec(memory_space=pltpu.HBM),
        out_shape=jax.ShapeDtypeStruct((rows, total), out_dtype),
        scratch_shapes=[
            pltpu.VMEM((rows, depth), tokens[0].dtype),
            pltpu.VMEM((rows, total), out_dtype),
            pltpu.SemaphoreType.DMA((n,)),
            pltpu.SemaphoreType.DMA((tiles,)),
        ],
        compiler_params=pltpu.CompilerParams(vmem_limit_bytes=28 * 2**20),
        cost_estimate=pl.CostEstimate(flops=0, bytes_accessed=0, transcendentals=0),
        name="last_phase",
    )(*tokens, weight, acc)


def body(tokens, base_weight, delta_values, delta_index, delta_count, n_col):
    ring, order, meets = plan(n_col)
    half = n_col // 2
    ahead = [(ring[k], ring[(k + 1) % n_col]) for k in range(n_col)]
    behind = [(b, a) for a, b in ahead]
    swap = [(0, 1), (1, 0)]
    me = (lax.axis_index("col") * 2 + lax.axis_index("row")).astype(jnp.int32).reshape(1)
    index = delta_index.reshape(-1)
    count = delta_count.reshape(-1)
    order_table = jnp.asarray(order.reshape(-1))

    buffers = [tokens]

    def run(want, accs, lo, hi, keep):
        lists = [[(t, p) for t, p in enumerate(row) if want(t, p)] for col in meets for row in col]
        counts = sorted({len(items) for items in lists})
        used_t = sorted({t for items in lists for t, _ in items})
        used_p = sorted({p for items in lists for _, p in items})
        last_pieces = [row[n_col - 1] for col in meets for row in col]
        used_k = sorted(set(last_pieces)) if keep else []
        table = np.zeros((len(lists), 2 * max(counts) + 2), np.int32)
        for k, items in enumerate(lists):
            table[k, 0] = len(items)
            for i, (t, p) in enumerate(items):
                table[k, 1 + 2 * i] = used_t.index(t)
                table[k, 2 + 2 * i] = used_p.index(p)
            if keep:
                table[k, -1] = used_k.index(last_pieces[k])
        return phase(
            me,
            jnp.asarray(table.reshape(-1)),
            counts,
            [buffers[t] for t in used_t],
            [pieces[p] for p in used_p],
            [pieces[p] for p in used_k],
            accs,
            lo,
            hi,
        )

    fwd, bwd = lax.ppermute(tokens, "col", ahead), lax.ppermute(tokens, "col", behind)
    local = [merge(me, order_table, index, count, base_weight, delta_values, j, half) for j in range(half)]
    remote = [lax.ppermute(piece, "row", swap) for piece in local[:-1]]
    late = n_col - 1

    total = base_weight.shape[1]
    width = tile_width(total)
    cut = -(-(total // width) // 2) * width
    cuts = [(0, cut), (cut, total)] if cut < total else [(0, total)]
    bounds = list(range(2, half - 1, 2)) + [half - 1]
    accs, start = [], 0
    gate = local[:-1]
    for d in range(2, half + 1):
        fwd, bwd = tie((fwd, bwd), gate)
        buffers += [fwd, bwd]
        if d == 3:
            (piece,) = tie((local[-1],), (fwd, bwd))
            remote.append(lax.ppermute(piece, "row", swap))
            pieces = local + remote
        if d < half:
            fwd, bwd = lax.ppermute(fwd, "col", ahead), lax.ppermute(bwd, "col", behind)
        else:
            part = tokens.shape[0] // 2
            fwd, bwd = lax.ppermute(fwd[:part], "col", ahead), lax.ppermute(bwd[part:], "col", behind)
        gate = []
        if d - 1 in bounds:
            stop = 2 * d - 1
            if d == half:
                acc, _, kept = run(lambda t, p: start <= t < stop or (t < start and p == late), accs, 0, total, True)
            else:
                outs = [
                    run(lambda t, p: start <= t < stop and p != late, accs[k : k + 1], lo, hi, False)
                    for k, (lo, hi) in enumerate(cuts)
                ]
                accs = [out[0] for out in outs]
                gate = [out[1] for out in outs]
            start = stop
    return last_phase([fwd, bwd], kept, acc, jnp.bfloat16)


def solution(mesh):
    spec = P(("tenant", "row"), "col")
    return jax.shard_map(
        functools.partial(body, n_col=mesh.shape["col"]),
        mesh=mesh,
        in_specs=(spec, P("row", "col"), spec, spec, spec),
        out_specs=spec,
        check_vma=False,
    )
```

time: 298 us -> 112 us (0.38)
  the two profiles are of different devices: /device:TPU:0 before, /device:TPU:1 now
where the time goes in v2:
time: 112 us
  Pallas kernels  74.8 us (67%)
  starting transfers between devices  15.2 us (14%)
  waiting for transfers between devices  14.3 us (13%)
  local copies, waits for them, and re-layouts  6.8 us (6%)
    pallas_call x3, Pallas kernels, phase(): pl.pallas_call(kernel, in_specs=[pl.BlockSpec(memory_space=pltpu.SMEM)] *...  42.5 us
    pallas_call x4, Pallas kernels, merge(): pl.pallas_call(kernel, in_specs=[pl.BlockSpec(memory_space=pltpu.SMEM)] *...  27.3 us
    ppermute x2, waiting for transfers between devices, body(): lax.ppermute(fwd, 'col', ahead)  11.6 us
    unnamed x17, local copies, waits for them, and re-layouts  6.73 us
    ppermute x1, starting transfers between devices, body(): lax.ppermute(fwd[:part], 'col', ahead)  5.33 us
    pallas_call x1, Pallas kernels, last_phase(): pl.pallas_call(kernel, in_specs=[pl.BlockSpec(memory_space=pl.ANY)] * n +...  4.91 us
    ppermute x2, starting transfers between devices, body(): lax.ppermute(fwd, 'col', ahead)  4.09 us
    ppermute x2, waiting for transfers between devices, body(): lax.ppermute(bwd, 'col', behind)  2.66 us
  transfers between devices with their start and end apart: 12, of which 3 were waited for; matrix products, arithmetic and copies ran while one was open for 3% of the time, Pallas kernels for 62%

profile of v2, /device:TPU:1, one launch (start us, length us, event | category | flops | bytes accessed | tf_op | source)
XLA Modules:
  0.0 112.1 jit_solution(4860005685312492101)
XLA Ops:
  0.0 2.1 %collective-permute-start = (bf16[512,1024]{1,0:T(8,128)(2,1)}, bf16[512,1024]{1,0:T(8,128)(2,1)S(1)}, u32[]{:S(2)}, u32[]{:S(2)}) collective-permute-start(bf16[512,1024]{1,0:T(8,128)(2,1)} %refs_0_.3), channel_id=1, source_target_pairs={{0,2},{2,4},{4,6},{6,7},{7,5},{5,3},{3,1},{1,0},{8,10},{10,12},{12... | collective-permute-start | bytes 3145736 | tf_op jit(solution)/shard_map/ppermute | solution.py:344
  2.1 0.0 collective-permute-start.1
  2.8 0.0 copy-start.2
  2.8 0.6 copy-done.2
  3.4 0.0 copy-start.4
  3.4 0.7 copy-done.4
  4.1 7.6 %merge1.1.refs_3_.refs_6_.refs_4_ = bf16[1024,3584]{1,0:T(8,128)(2,1)} custom-call(s32[1]{0:T(128)} %bitcast.me_ref, s32[64]{0:T(128)S(1)} %copy-done.4, s32[48]{0:T(128)S(1)} %bitcast.7, s32[1]{0:T(128)} %bitcast.4.count_ref, bf16[4096,3584]{1,0:T(8,128)(2,1)} %w_ref.7, bf16[6144,128]{1,0:T(8,128)(2,1)} %values_ref.7), custom_call_target="tpu_custom_call" | custom-call | tf_op jit(solution)/shard_map/merge1/pallas_call | solution.py:111
  11.7 1.7 %collective-permute-start.7 = (bf16[1024,3584]{1,0:T(8,128)(2,1)}, bf16[1024,3584]{1,0:T(8,128)(2,1)}, u32[]{:S(2)}, u32[]{:S(2)}) collective-permute-start(bf16[1024,3584]{1,0:T(8,128)(2,1)} %merge1.1.refs_3_.refs_6_.refs_4_), channel_id=1, source_target_pairs={{0,8},{8,0},{1,9},{9,1},{2,10},{10,2},{3,11},{11,3},{4,12},{12,4},... | collective-permute-start | bytes 22020104 | tf_op jit(solution)/shard_map/ppermute | solution.py:346
  13.4 7.5 %merge2.1.refs_4_.refs_7_.refs_5_ = bf16[1024,3584]{1,0:T(8,128)(2,1)} custom-call(s32[1]{0:T(128)} %bitcast.me_ref, s32[64]{0:T(128)S(1)} %copy-done.4, s32[48]{0:T(128)S(1)} %bitcast.8, s32[1]{0:T(128)} %bitcast.5.count_ref, bf16[4096,3584]{1,0:T(8,128)(2,1)} %w_ref.7, bf16[6144,128]{1,0:T(8,128)(2,1)} %values_ref.7), custom_call_target="tpu_custom_call" | custom-call | tf_op jit(solution)/shard_map/merge2/pallas_call | solution.py:111
  20.9 7.6 %merge0.1.refs_2_.refs_5_ = bf16[1024,3584]{1,0:T(8,128)(2,1)} custom-call(s32[1]{0:T(128)} %bitcast.me_ref, s32[64]{0:T(128)S(1)} %copy-done.4, s32[48]{0:T(128)S(1)} %bitcast.9, s32[1]{0:T(128)} %bitcast.3.count_ref, bf16[4096,3584]{1,0:T(8,128)(2,1)} %w_ref.7, bf16[6144,128]{1,0:T(8,128)(2,1)} %values_ref.7), custom_call_target="tpu_custom_call" | custom-call | tf_op jit(solution)/shard_map/merge0/pallas_call | solution.py:111
  28.5 0.0 copy-start.3
  28.6 0.0 copy-start.5
  28.6 0.0 collective-permute-done.refs_0_
  28.6 0.0 collective-permute-done.1.refs_1_
  28.6 3.0 %collective-permute-start.2 = (bf16[512,1024]{1,0:T(8,128)(2,1)S(1)}, bf16[512,1024]{1,0:T(8,128)(2,1)S(1)}, u32[]{:S(2)}, u32[]{:S(2)}) collective-permute-start(bf16[512,1024]{1,0:T(8,128)(2,1)S(1)} %get-tuple-element.17.refs_1_), channel_id=1, source_target_pairs={{0,2},{2,4},{4,6},{6,7},{7,5},{5,3},{3,1},{1,0},{8,10},{10,12},{12... | collective-permute-start | bytes 3145736 | tf_op jit(solution)/shard_map/ppermute | solution.py:364
  31.6 0.0 collective-permute-start.3
  31.6 0.9 collective-permute-start.8
  32.5 0.0 collective-permute-start.6
  32.5 0.0 copy-done.3
  32.5 0.0 copy-done.5
  32.5 4.6 %merge3.1.refs_8_.refs_6_.refs_10_ = bf16[1024,3584]{1,0:T(8,128)(2,1)S(1)} custom-call(s32[1]{0:T(128)} %bitcast.me_ref, s32[64]{0:T(128)S(1)} %copy-done.5, s32[48]{0:T(128)S(1)} %bitcast.10, s32[1]{0:T(128)} %bitcast.6.count_ref, bf16[4096,3584]{1,0:T(8,128)(2,1)} %w_ref.7, bf16[6144,128]{1,0:T(8,128)(2,1)} %values_ref.7), custom_call_target="tpu_custom_call" | custom-call | tf_op jit(solution)/shard_map/merge3/pallas_call | solution.py:111
  37.1 0.0 copy-start
  37.1 3.0 %copy.23.refs_0_ = bf16[1024,3584]{1,0:T(8,128)(2,1)} copy(bf16[1024,3584]{1,0:T(8,128)(2,1)S(1)} %merge3.1.refs_8_.refs_6_.refs_10_) | data formatting | bytes 14680064
  40.1 2.4 %copy-done = bf16[1024,3584]{1,0:T(8,128)(2,1)} copy-done((bf16[1024,3584]{1,0:T(8,128)(2,1)}, bf16[1024,3584]{1,0:T(8,128)(2,1)S(1)}, u32[]{:S(2)}) %copy-start) | copy-done | bytes 7340056
  42.5 11.6 %collective-permute-done.2.refs_0_ = bf16[512,1024]{1,0:T(8,128)(2,1)S(1)} collective-permute-done((bf16[512,1024]{1,0:T(8,128)(2,1)S(1)}, bf16[512,1024]{1,0:T(8,128)(2,1)S(1)}, u32[]{:S(2)}, u32[]{:S(2)}) %collective-permute-start.2) | collective-permute-done | bytes 1048608 | tf_op jit(solution)/shard_map/ppermute | solution.py:364
  54.1 2.3 %collective-permute-done.3.refs_1_ = bf16[512,1024]{1,0:T(8,128)(2,1)S(1)} collective-permute-done((bf16[512,1024]{1,0:T(8,128)(2,1)S(1)}, bf16[512,1024]{1,0:T(8,128)(2,1)S(1)}, u32[]{:S(2)}, u32[]{:S(2)}) %collective-permute-start.3) | collective-permute-done | bytes 1048608 | tf_op jit(solution)/shard_map/ppermute | solution.py:364
  56.4 0.0 copy-start.1
  56.4 0.4 collective-permute-start.11
  56.8 1.1 collective-permute-start.4
  57.9 0.0 collective-permute-done.7.refs_10_.refs_7_
  57.9 0.4 collective-permute-start.5
  58.2 0.0 collective-permute-done.8.refs_11_.refs_8_
  58.2 0.0 collective-permute-done.6.refs_9_
  58.2 0.0 copy-done.1
  58.2 0.0 copy-done.6
  58.3 10.6 %phase.4 = (f32[512,1536]{1,0:T(8,128)S(1)}, f32[8,128]{1,0:T(8,128)S(1)}) custom-call(s32[1]{0:T(128)} %bitcast.me_ref, s32[192]{0:T(256)S(1)} %copy-done.6, bf16[512,1024]{1,0:T(8,128)(2,1)S(1)} %copy-done.1, bf16[512,1024]{1,0:T(8,128)(2,1)S(1)} %get-tuple-element.17.refs_1_, bf16[512,1024]{1,0:T(8,128)(2,1)S(1)} %get-tuple-element.18.refs_2_, ...), custom_call_target="tpu_custom_call" | custom-call | tf_op jit(solution)/shard_map/phase/pallas_call | solution.py:236
  68.9 0.0 copy-start.7
  68.9 13.0 %phase.3 = (f32[512,2048]{1,0:T(8,128)S(1)}, f32[8,128]{1,0:T(8,128)S(1)}) custom-call(s32[1]{0:T(128)} %bitcast.me_ref, s32[192]{0:T(256)S(1)} %copy-done.6, bf16[512,1024]{1,0:T(8,128)(2,1)S(1)} %copy-done.1, bf16[512,1024]{1,0:T(8,128)(2,1)S(1)} %get-tuple-element.17.refs_1_, bf16[512,1024]{1,0:T(8,128)(2,1)S(1)} %get-tuple-element.18.refs_2_, ...), custom_call_target="tpu_custom_call" | custom-call | tf_op jit(solution)/shard_map/phase/pallas_call | solution.py:236
  81.9 0.0 collective-permute-done.4.refs_0_
  81.9 0.4 collective-permute-done.5.refs_1_
  82.3 0.3 collective-permute-start.10
  82.7 5.3 %collective-permute-start.9 = (bf16[256,1024]{1,0:T(8,128)(2,1)S(1)}, bf16[256,1024]{1,0:T(8,128)(2,1)S(1)}, u32[]{:S(2)}, u32[]{:S(2)}) collective-permute-start(bf16[256,1024]{1,0:T(8,128)(2,1)S(1)} %slice.6), channel_id=1, source_target_pairs={{0,2},{2,4},{4,6},{6,7},{7,5},{5,3},{3,1},{1,0},{8,10},{10,12},{12... | collective-permute-start | bytes 1572872 | tf_op jit(solution)/shard_map/ppermute | solution.py:367
  88.0 0.0 collective-permute-done.11.refs_9_.refs_11_
  88.0 0.0 copy-done.7
  88.0 19.0 %phase.5 = (f32[512,3584]{1,0:T(8,128)S(1)}, f32[8,128]{1,0:T(8,128)}, bf16[1024,3584]{1,0:T(8,128)(2,1)S(1)}) custom-call(s32[1]{0:T(128)} %bitcast.me_ref, s32[128]{0:T(128)S(1)} %copy-done.7, bf16[512,1024]{1,0:T(8,128)(2,1)S(1)} %get-tuple-element.19.refs_3_.refs_1_.refs_0_, bf16[512,1024]{1,0:T(8,128)(2,1)S(1)} %get-tuple-element.20.refs_4_.refs_2_.refs_1_, ...), custom_call_target="tpu_custom_call" | custom-call | tf_op jit(solution)/shard_map/phase/pallas_call | solution.py:236
  107.0 0.0 collective-permute-done.10.refs_1_
  107.0 0.0 collective-permute-done.9.refs_0_
  107.0 4.9 %last_phase.1 = bf16[512,3584]{1,0:T(8,128)(2,1)} custom-call(bf16[256,1024]{1,0:T(8,128)(2,1)S(1)} %collective-permute-done.9.refs_0_, bf16[256,1024]{1,0:T(8,128)(2,1)S(1)} %collective-permute-done.10.refs_1_, bf16[1024,3584]{1,0:T(8,128)(2,1)S(1)} %get-tuple-element.27.refs_2_, f32[512,3584]{1,0:T(8,128)S(1)} %get-tuple-element.28.refs_3_), custom_call_target="tpu_custom_call" | custom-call | tf_op jit(solution)/shard_map/last_phase/pallas_call | solution.py:287
  (7 shorter events, 0.1 us)
Async XLA Ops:
  0.0 28.6 %collective-permute-start = (bf16[512,1024]{1,0:T(8,128)(2,1)}, bf16[512,1024]{1,0:T(8,128)(2,1)S(1)}, u32[]{:S(2)}, u32[]{:S(2)}) collective-permute-start(bf16[512,1024]{1,0:T(8,128)(2,1)} %refs_0_.3), channel_id=1, source_target_pairs={{0,2},{2,4},{4,6},{6,7},{7,5},{5,3},{3,1},{1,0},{8,10},{10,12},{12... | collective-permute-start | bytes 3145736 | tf_op jit(solution)/shard_map/ppermute | solution.py:344
  2.1 26.5 %collective-permute-start.1 = (bf16[512,1024]{1,0:T(8,128)(2,1)}, bf16[512,1024]{1,0:T(8,128)(2,1)S(1)}, u32[]{:S(2)}, u32[]{:S(2)}) collective-permute-start(bf16[512,1024]{1,0:T(8,128)(2,1)} %refs_0_.3), channel_id=1, source_target_pairs={{2,0},{4,2},{6,4},{7,6},{5,7},{3,5},{1,3},{0,1},{10,8},{12,10},{14... | collective-permute-start | bytes 3145736 | tf_op jit(solution)/shard_map/ppermute | solution.py:344
  2.8 0.7 copy-start.2
  3.4 0.7 copy-start.4
  11.7 46.1 %collective-permute-start.7 = (bf16[1024,3584]{1,0:T(8,128)(2,1)}, bf16[1024,3584]{1,0:T(8,128)(2,1)}, u32[]{:S(2)}, u32[]{:S(2)}) collective-permute-start(bf16[1024,3584]{1,0:T(8,128)(2,1)} %merge1.1.refs_3_.refs_6_.refs_4_), channel_id=1, source_target_pairs={{0,8},{8,0},{1,9},{9,1},{2,10},{10,2},{3,11},{11,3},{4,12},{12,4},... | collective-permute-start | bytes 22020104 | tf_op jit(solution)/shard_map/ppermute | solution.py:346
  28.5 4.0 %copy-start.3 = (s32[48,1]{0,1:T(1,128)S(1)}, s32[48,1]{0,1:T(1,128)}, u32[]{:S(2)}) copy-start(s32[48,1]{0,1:T(1,128)} %param.12) | copy-start | bytes 580
  28.6 4.0 %copy-start.5 = (s32[64]{0:T(128)S(1)}, s32[64]{0:T(128)}, u32[]{:S(2)}) copy-start(s32[64]{0:T(128)} %constant.17.clone.order_ref) | copy-start | bytes 772
  28.6 25.5 %collective-permute-start.2 = (bf16[512,1024]{1,0:T(8,128)(2,1)S(1)}, bf16[512,1024]{1,0:T(8,128)(2,1)S(1)}, u32[]{:S(2)}, u32[]{:S(2)}) collective-permute-start(bf16[512,1024]{1,0:T(8,128)(2,1)S(1)} %get-tuple-element.17.refs_1_), channel_id=1, source_target_pairs={{0,2},{2,4},{4,6},{6,7},{7,5},{5,3},{3,1},{1,0},{8,10},{10,12},{12... | collective-permute-start | bytes 3145736 | tf_op jit(solution)/shard_map/ppermute | solution.py:364
  31.6 24.8 %collective-permute-start.3 = (bf16[512,1024]{1,0:T(8,128)(2,1)S(1)}, bf16[512,1024]{1,0:T(8,128)(2,1)S(1)}, u32[]{:S(2)}, u32[]{:S(2)}) collective-permute-start(bf16[512,1024]{1,0:T(8,128)(2,1)S(1)} %get-tuple-element.18.refs_2_), channel_id=1, source_target_pairs={{2,0},{4,2},{6,4},{7,6},{5,7},{3,5},{1,3},{0,1},{10,8},{12,10},{14... | collective-permute-start | bytes 3145736 | tf_op jit(solution)/shard_map/ppermute | solution.py:364
  31.6 26.6 %collective-permute-start.8 = (bf16[1024,3584]{1,0:T(8,128)(2,1)}, bf16[1024,3584]{1,0:T(8,128)(2,1)}, u32[]{:S(2)}, u32[]{:S(2)}) collective-permute-start(bf16[1024,3584]{1,0:T(8,128)(2,1)} %merge2.1.refs_4_.refs_7_.refs_5_), channel_id=1, source_target_pairs={{0,8},{8,0},{1,9},{9,1},{2,10},{10,2},{3,11},{11,3},{4,12},{12,4},... | collective-permute-start | bytes 22020104 | tf_op jit(solution)/shard_map/ppermute | solution.py:346
  32.5 25.7 %collective-permute-start.6 = (bf16[1024,3584]{1,0:T(8,128)(2,1)}, bf16[1024,3584]{1,0:T(8,128)(2,1)}, u32[]{:S(2)}, u32[]{:S(2)}) collective-permute-start(bf16[1024,3584]{1,0:T(8,128)(2,1)} %merge0.1.refs_2_.refs_5_), channel_id=1, source_target_pairs={{0,8},{8,0},{1,9},{9,1},{2,10},{10,2},{3,11},{11,3},{4,12},{12,4},... | collective-permute-start | bytes 22020104 | tf_op jit(solution)/shard_map/ppermute | solution.py:346
  37.1 5.4 %copy-start = (bf16[1024,3584]{1,0:T(8,128)(2,1)}, bf16[1024,3584]{1,0:T(8,128)(2,1)S(1)}, u32[]{:S(2)}) copy-start(bf16[1024,3584]{1,0:T(8,128)(2,1)S(1)} %merge3.1.refs_8_.refs_6_.refs_10_) | copy-start | bytes 22020100
  56.4 1.9 %copy-start.1 = (bf16[512,1024]{1,0:T(8,128)(2,1)S(1)}, bf16[512,1024]{1,0:T(8,128)(2,1)}, u32[]{:S(2)}) copy-start(bf16[512,1024]{1,0:T(8,128)(2,1)} %refs_0_.3) | copy-start | bytes 3145732
  56.4 1.9 %copy-start.6 = (s32[192]{0:T(256)S(1)}, s32[192]{0:T(256)}, u32[]{:S(2)}) copy-start(s32[192]{0:T(256)} %constant.18.clone.table_ref) | copy-start | bytes 2308
  56.4 31.6 %collective-permute-start.11 = (bf16[1024,3584]{1,0:T(8,128)(2,1)}, bf16[1024,3584]{1,0:T(8,128)(2,1)}, u32[]{:S(2)}, u32[]{:S(2)}) collective-permute-start(bf16[1024,3584]{1,0:T(8,128)(2,1)} %tie.7), channel_id=1, source_target_pairs={{0,8},{8,0},{1,9},{9,1},{2,10},{10,2},{3,11},{11,3},{4,12},{12,4},... | collective-permute-start | bytes 22020104 | tf_op jit(solution)/shard_map/ppermute | solution.py:361
  56.8 25.1 %collective-permute-start.4 = (bf16[512,1024]{1,0:T(8,128)(2,1)S(1)}, bf16[512,1024]{1,0:T(8,128)(2,1)S(1)}, u32[]{:S(2)}, u32[]{:S(2)}) collective-permute-start(bf16[512,1024]{1,0:T(8,128)(2,1)S(1)} %get-tuple-element.19.refs_3_.refs_1_.refs_0_), channel_id=1, source_target_pairs={{0,2},{2,4},{4,6},{6,7},{7,5},{5,3},{3,1},{1,0},{8,10},{10,12},{12... | collective-permute-start | bytes 3145736 | tf_op jit(solution)/shard_map/ppermute | solution.py:364
  57.9 24.4 %collective-permute-start.5 = (bf16[512,1024]{1,0:T(8,128)(2,1)S(1)}, bf16[512,1024]{1,0:T(8,128)(2,1)S(1)}, u32[]{:S(2)}, u32[]{:S(2)}) collective-permute-start(bf16[512,1024]{1,0:T(8,128)(2,1)S(1)} %get-tuple-element.20.refs_4_.refs_2_.refs_1_), channel_id=1, source_target_pairs={{2,0},{4,2},{6,4},{7,6},{5,7},{3,5},{1,3},{0,1},{10,8},{12,10},{14... | collective-permute-start | bytes 3145736 | tf_op jit(solution)/shard_map/ppermute | solution.py:364
  68.9 19.1 %copy-start.7 = (s32[128]{0:T(128)S(1)}, s32[128]{0:T(128)}, u32[]{:S(2)}) copy-start(s32[128]{0:T(128)} %constant.19.clone.table_ref) | copy-start | bytes 1540
  82.3 24.7 %collective-permute-start.10 = (bf16[256,1024]{1,0:T(8,128)(2,1)S(1)}, bf16[256,1024]{1,0:T(8,128)(2,1)S(1)}, u32[]{:S(2)}, u32[]{:S(2)}) collective-permute-start(bf16[256,1024]{1,0:T(8,128)(2,1)S(1)} %slice.7), channel_id=1, source_target_pairs={{2,0},{4,2},{6,4},{7,6},{5,7},{3,5},{1,3},{0,1},{10,8},{12,10},{14... | collective-permute-start | bytes 1572872 | tf_op jit(solution)/shard_map/ppermute | solution.py:367
  82.7 24.3 %collective-permute-start.9 = (bf16[256,1024]{1,0:T(8,128)(2,1)S(1)}, bf16[256,1024]{1,0:T(8,128)(2,1)S(1)}, u32[]{:S(2)}, u32[]{:S(2)}) collective-permute-start(bf16[256,1024]{1,0:T(8,128)(2,1)S(1)} %slice.6), channel_id=1, source_target_pairs={{0,2},{2,4},{4,6},{6,7},{7,5},{5,3},{3,1},{1,0},{8,10},{10,12},{12... | collective-permute-start | bytes 1572872 | tf_op jit(solution)/shard_map/ppermute | solution.py:367

commit v3 on v2

v3 whole, which is shorter than its diff:
```python
import functools

import jax
import jax.numpy as jnp
import numpy as np
from jax import lax
from jax.experimental import pallas as pl
from jax.experimental.pallas import tpu as pltpu
from jax.sharding import PartitionSpec as P

PHASE_VMEM = 30
SPARE = 64
PIN = 2


def ring_order(n):
    return list(range(0, n, 2)) + list(range(n - 1, 0, -2))


def plan(n):
    ring = ring_order(n)
    place = {c: k for k, c in enumerate(ring)}
    half = n // 2
    order = np.zeros((n, 2, half), np.int32)
    meets = np.zeros((n, 2, n), np.int32)
    for col in range(n):
        me = place[col]

        def dist(c):
            ahead = (place[c] - me) % n
            return min(ahead, n - ahead)

        def token_id(c):
            ahead = (place[c] - me) % n
            if ahead == 0:
                return 0
            if ahead == half:
                return n - 1
            return 2 * ahead if ahead < half else 2 * (n - ahead) - 1

        for h in range(2):
            chunks = sorted(range(h * half, (h + 1) * half), key=lambda c: (dist(c), c))
            order[col, h] = [c - h * half for c in chunks]
            for row in range(2):
                for j, c in enumerate(chunks):
                    meets[col, row, token_id(c)] = j if row == h else half + j
    return ring, order, meets.tolist()


def tie(values, after):
    n = len(values)

    def kernel(*refs):
        refs[-1][...] = jnp.zeros_like(refs[-1])

    return pl.pallas_call(
        kernel,
        in_specs=[pl.BlockSpec(memory_space=pl.ANY)] * (n + len(after)),
        out_specs=[pl.BlockSpec(memory_space=pl.ANY)] * n,
        out_shape=[jax.ShapeDtypeStruct(v.shape, v.dtype) for v in values],
        scratch_shapes=[pltpu.VMEM((8, 128), jnp.float32)],
        input_output_aliases={k: k for k in range(n)},
        compiler_params=pltpu.CompilerParams(vmem_limit_bytes=2**20),
        cost_estimate=pl.CostEstimate(flops=0, bytes_accessed=0, transcendentals=0),
        name="tie",
    )(*values, *after)


def hbm(x):
    return pltpu.with_memory_space_constraint(x, pltpu.HBM)


def merge(me, order, index, count, weight, values, numbers, total_pieces, spare):
    pieces = len(numbers)
    block = values.shape[1]
    blocks = weight.shape[0] // block // total_pieces
    width = weight.shape[1]
    col_blocks = width // block

    def kernel(me_ref, order_ref, index_ref, count_ref, w_ref, values_ref, out_ref, vbuf, wsem, vsem):
        value_copy = pltpu.make_async_copy(values_ref, vbuf, vsem)
        first = [order_ref[me_ref[0] * total_pieces + p] * blocks for p in numbers]

        def copy(k):
            rows = pl.ds(pl.multiple_of((first[k // blocks] + k % blocks) * block, block), block)
            return pltpu.make_async_copy(w_ref.at[rows], out_ref.at[pl.ds(k * block, block)], wsem.at[k])

        value_copy.start()
        for k in range(pieces * blocks):
            copy(k).start()
        if spare:
            rest = out_ref.at[pl.ds(pieces * blocks * block, spare)]
            rest[...] = jnp.zeros((spare, width), out_ref.dtype)
        value_copy.wait()
        for k in range(pieces * blocks):
            copy(k).wait()

        def slot(s, carry):
            which = index_ref[s]
            row = which // col_blocks
            for p in range(pieces):
                row_here = row - first[p]

                @pl.when(jnp.logical_and(row_here >= 0, row_here < blocks))
                def _():
                    rows = pl.ds(pl.multiple_of((p * blocks + row_here) * block, block), block)
                    cols = pl.ds(pl.multiple_of((which - row * col_blocks) * block, block), block)
                    value = vbuf[pl.ds(pl.multiple_of(s * block, block), block), :]
                    old = out_ref[rows, cols]
                    out_ref[rows, cols] = (old.astype(jnp.float32) + value.astype(jnp.float32)).astype(out_ref.dtype)

            return carry

        lax.fori_loop(0, count_ref[0], slot, 0)

    shape = (pieces * blocks * block + spare, width)
    held = 2 * (shape[0] * width + values.shape[0] * values.shape[1])
    return pl.pallas_call(
        kernel,
        in_specs=[pl.BlockSpec(memory_space=pltpu.SMEM)] * 4 + [pl.BlockSpec(memory_space=pltpu.HBM)] * 2,
        out_specs=pl.BlockSpec(memory_space=pltpu.VMEM),
        out_shape=pltpu.VMEM(shape, weight.dtype),
        scratch_shapes=[
            pltpu.VMEM(values.shape, values.dtype),
            pltpu.SemaphoreType.DMA((pieces * blocks,)),
            pltpu.SemaphoreType.DMA,
        ],
        compiler_params=pltpu.CompilerParams(vmem_limit_bytes=held + 2**20),
        cost_estimate=pl.CostEstimate(flops=0, bytes_accessed=0, transcendentals=0),
        name="merge",
    )(me, order, index, count, hbm(weight), hbm(values))


def tile_width(total):
    return 512 if total % 512 == 0 else total


def phase(me, table, kinds, tokens, weights, pinned, accs, last):
    n_tokens, n_weights, n_accs = len(tokens), len(weights), len(accs)
    rows, depth = tokens[0].shape
    total = weights[0].shape[1]
    width = tile_width(total)
    tiles = total // width
    most = max(max(count for count, _ in kinds), 1)
    stride = 4 + 3 * most
    slots = 3 if most > 3 else 4

    def kernel(me_ref, table_ref, *refs):
        token_refs, refs = refs[:n_tokens], refs[n_tokens:]
        weight_refs, refs = refs[:n_weights], refs[n_weights:]
        acc_refs, refs = refs[:n_accs], refs[n_accs:]
        out_ref, refs = refs[0], refs[1:]
        if last:
            kept_ref, refs = refs[0], refs[1:]
        tbuf, wbuf, abuf, obuf, tsem, wsem, asem, osem, ksem = refs
        base = me_ref[0] * stride

        def columns(tile):
            return pl.ds(pl.multiple_of(tile * width, 128), width)

        def token_copy(ref, i):
            return pltpu.make_async_copy(ref, tbuf.at[:, pl.ds(i * depth, depth)], tsem.at[i])

        def piece_rows(at):
            return pl.ds(pl.multiple_of(table_ref[at] * depth, depth), depth)

        def weight_copy(ref, tile, i):
            slot = lax.rem(tile, slots)
            return pltpu.make_async_copy(
                ref.at[piece_rows(base + 6 + 3 * i), columns(tile)], wbuf.at[slot, pl.ds(i * depth, depth)], wsem.at[slot, i]
            )

        def acc_copy(tile):
            slot = lax.rem(tile, slots)
            return pltpu.make_async_copy(acc_refs[0].at[:, columns(tile)], abuf.at[slot], asem.at[slot])

        def store(tile):
            slot = lax.rem(tile, 2)
            return pltpu.make_async_copy(obuf.at[slot], out_ref.at[:, columns(tile)], osem.at[slot])

        def fetch(tile, count, use_acc):
            for i in range(count):
                for w in range(n_weights):

                    @pl.when(table_ref[base + 5 + 3 * i] == w)
                    def _():
                        weight_copy(weight_refs[w], tile, i).start()

            if use_acc:
                acc_copy(tile).start()

        def work(count, use_acc):
            for i in range(count):
                for t in range(n_tokens):

                    @pl.when(table_ref[base + 4 + 3 * i] == t)
                    def _():
                        token_copy(token_refs[t], i).start()

            fetch(jnp.int32(0), count, use_acc)
            for i in range(count):
                token_copy(token_refs[0], i).wait()

            def step(tile, carry):
                if last:

                    @pl.when(tile == tiles // 2)
                    def _():
                        for w in range(n_weights):

                            @pl.when(table_ref[base + 2] == w)
                            def _():
                                pltpu.make_async_copy(weight_refs[w].at[piece_rows(base + 3)], kept_ref, ksem).start()

                slot = lax.rem(tile, slots)
                for i in range(count):
                    weight_copy(weight_refs[0], tile, i).wait()
                if use_acc:
                    acc_copy(tile).wait()

                @pl.when(tile == 0)
                def _():
                    for later in range(1, min(slots - 1, tiles)):
                        fetch(jnp.int32(later), count, use_acc)

                @pl.when(tile + slots - 1 < tiles)
                def _():
                    fetch(tile + slots - 1, count, use_acc)

                deep = pl.ds(0, count * depth)
                value = jnp.dot(tbuf[:, deep], wbuf[slot, deep], preferred_element_type=jnp.float32)
                if use_acc:
                    value = value + abuf[slot]
                if last:
                    out_ref[:, columns(tile)] = value
                else:

                    @pl.when(tile >= 2)
                    def _():
                        store(tile - 2).wait()

                    obuf[lax.rem(tile, 2)] = value
                    store(tile).start()
                return carry

            lax.fori_loop(0, tiles, step, 0)
            if last:
                pltpu.make_async_copy(weight_refs[0].at[pl.ds(0, depth)], kept_ref, ksem).wait()
            else:
                for tile in range(max(0, tiles - 2), tiles):
                    store(tile).wait()

        for count, use_acc in kinds:
            if count:

                @pl.when(jnp.logical_and(table_ref[base] == count, table_ref[base + 1] == use_acc))
                def _():
                    work(count, use_acc)

    place = pltpu.VMEM if last else pltpu.HBM
    out_shape = [place((rows, total), jnp.float32)]
    if last:
        out_shape.append(pltpu.VMEM((depth, total), weights[0].dtype))
    operands = [me, table] + list(tokens) + [hbm(w) if k in pinned else w for k, w in enumerate(weights)]
    operands += [hbm(a) for a in accs]
    return pl.pallas_call(
        kernel,
        in_specs=[pl.BlockSpec(memory_space=pltpu.SMEM)] * 2 + [pl.BlockSpec(memory_space=pl.ANY)] * (len(operands) - 2),
        out_specs=[pl.BlockSpec(memory_space=place)] * len(out_shape),
        out_shape=out_shape,
        scratch_shapes=[
            pltpu.VMEM((rows, most * depth), tokens[0].dtype),
            pltpu.VMEM((slots, most * depth, width), weights[0].dtype),
            pltpu.VMEM((slots, rows, width) if n_accs else (slots, 8, 128), jnp.float32),
            pltpu.VMEM((2, 8, 128) if last else (2, rows, width), jnp.float32),
            pltpu.SemaphoreType.DMA((most,)),
            pltpu.SemaphoreType.DMA((slots, most)),
            pltpu.SemaphoreType.DMA((slots,)),
            pltpu.SemaphoreType.DMA((2,)),
            pltpu.SemaphoreType.DMA,
        ],
        compiler_params=pltpu.CompilerParams(vmem_limit_bytes=PHASE_VMEM * 2**20),
        cost_estimate=pl.CostEstimate(flops=0, bytes_accessed=0, transcendentals=0),
        name="phase",
    )(*operands)


def last_phase(tokens, weight, acc, out_dtype):
    part, depth = tokens[0].shape
    rows = part * len(tokens)
    total = weight.shape[1]
    width = tile_width(total)
    tiles = total // width
    n = len(tokens)

    def kernel(*refs):
        token_refs = refs[:n]
        w_ref, acc_ref, out_ref, tbuf, obuf, tsem, osem = refs[n:]

        def store(tile):
            at = pl.ds(tile * width, width)
            return pltpu.make_async_copy(obuf.at[:, at], out_ref.at[:, at], osem.at[tile])

        copies = [
            pltpu.make_async_copy(token_refs[k], tbuf.at[pl.ds(k * part, part)], tsem.at[k]) for k in range(n)
        ]
        for copy in copies:
            copy.start()
        for copy in copies:
            copy.wait()
        for tile in range(tiles):
            at = pl.ds(tile * width, width)
            product = jnp.dot(tbuf[...], w_ref[:, at], preferred_element_type=jnp.float32)
            obuf[:, at] = (acc_ref[:, at] + product).astype(out_dtype)
            store(tile).start()
        for tile in range(tiles):
            store(tile).wait()

    return pl.pallas_call(
        kernel,
        in_specs=[pl.BlockSpec(memory_space=pl.ANY)] * n + [pl.BlockSpec(memory_space=pltpu.VMEM)] * 2,
        out_specs=pl.BlockSpec(memory_space=pltpu.HBM),
        out_shape=jax.ShapeDtypeStruct((rows, total), out_dtype),
        scratch_shapes=[
            pltpu.VMEM((rows, depth), tokens[0].dtype),
            pltpu.VMEM((rows, total), out_dtype),
            pltpu.SemaphoreType.DMA((n,)),
            pltpu.SemaphoreType.DMA((tiles,)),
        ],
        compiler_params=pltpu.CompilerParams(vmem_limit_bytes=28 * 2**20),
        cost_estimate=pl.CostEstimate(flops=0, bytes_accessed=0, transcendentals=0),
        name="last_phase",
    )(*tokens, weight, acc)


def body(tokens, base_weight, delta_values, delta_index, delta_count, n_col):
    ring, order, meets = plan(n_col)
    half = n_col // 2
    ahead = [(ring[k], ring[(k + 1) % n_col]) for k in range(n_col)]
    behind = [(b, a) for a, b in ahead]
    swap = [(0, 1), (1, 0)]
    me = (lax.axis_index("col") * 2 + lax.axis_index("row")).astype(jnp.int32).reshape(1)
    index = delta_index.reshape(-1)
    count = delta_count.reshape(-1)
    order_table = jnp.asarray(order.reshape(-1))
    devices = [row for col in meets for row in col]
    done = [set() for _ in devices]

    def run(want, acc, last):
        had = [bool(d) for d in done]
        lists = [
            [(t, p) for t, p in enumerate(row) if t not in d and want(t, p)] for row, d in zip(devices, done)
        ]
        kinds = sorted({(len(items), int(h)) for items, h in zip(lists, had)})
        used_t = sorted({t for items in lists for t, _ in items})
        ends = [row[n_col - 1] for row in devices] if last else []
        used_w = sorted({place[p][0] for items in lists for _, p in items} | {place[p][0] for p in ends})
        table = np.zeros((len(lists), 4 + 3 * max(max(k for k, _ in kinds), 1)), np.int32)
        for k, items in enumerate(lists):
            table[k, :2] = len(items), had[k]
            if last:
                table[k, 2:4] = used_w.index(place[ends[k]][0]), place[ends[k]][1]
            for i, (t, p) in enumerate(items):
                table[k, 4 + 3 * i : 7 + 3 * i] = used_t.index(t), used_w.index(place[p][0]), place[p][1]
                done[k].add(t)
        return phase(
            me,
            jnp.asarray(table.reshape(-1)),
            kinds,
            [buffers[t] for t in used_t],
            [weights[w] for w in used_w],
            [k for k, w in enumerate(used_w) if w < PIN],
            [] if acc is None else [acc],
            last,
        )

    fwd, bwd = lax.ppermute(tokens, "col", ahead), lax.ppermute(tokens, "col", behind)
    sets = [[0, half - 1], list(range(1, half - 1))]
    args = (me, order_table, index, count, base_weight, delta_values)
    local = [merge(*args, numbers, half, spare) for numbers, spare in zip(sets, (0, SPARE))]
    remote = [lax.ppermute(local[0], "row", swap), None]
    place = {}
    for w, numbers in enumerate(sets):
        for k, p in enumerate(numbers):
            place[p], place[half + p] = (w, k), (2 + w, k)
    buffers = [tokens]

    bounds = list(range(2, half - 1, 2)) + [half - 1]
    acc = None
    gate = list(local)
    for d in range(2, half + 1):
        fwd, bwd = tie((fwd, bwd), gate)
        buffers += [fwd, bwd]
        if d == 2:
            (local[1],) = tie((local[1],), (fwd, bwd))
            remote[1] = lax.ppermute(local[1], "row", swap)
            weights = local + remote
        if d < half:
            next_fwd, next_bwd = lax.ppermute(fwd, "col", ahead), lax.ppermute(bwd, "col", behind)
        else:
            part = tokens.shape[0] // 2
            next_fwd, next_bwd = lax.ppermute(fwd[:part], "col", ahead), lax.ppermute(bwd[part:], "col", behind)
        gate = []
        if d == 2:
            weights = local + remote
            acc = run(lambda t, p: t == 0, None, False)[0]
            gate = [hbm(acc)]
        elif d - 1 in bounds:
            out = run(lambda t, p: t < 2 * d - 1, acc, d == half)
            acc, gate = out[0], [hbm(out[0])]
        fwd, bwd = next_fwd, next_bwd
    return last_phase([fwd, bwd], out[1], acc, jnp.bfloat16)


def solution(mesh):
    spec = P(("tenant", "row"), "col")
    return jax.shard_map(
        functools.partial(body, n_col=mesh.shape["col"]),
        mesh=mesh,
        in_specs=(spec, P("row", "col"), spec, spec, spec),
        out_specs=spec,
        check_vma=False,
    )
```

time: 112 us -> 103 us (0.920)
  the two profiles are of different devices: /device:TPU:1 before, /device:TPU:0 now
where the time goes in v3:
time: 103 us
  Pallas kernels  70.1 us (68%)
  waiting for transfers between devices  20 us (19%)
  starting transfers between devices  9.35 us (9%)
  local copies, waits for them, and re-layouts  2.45 us (2%)
    pallas_call x3, Pallas kernels, phase(): pl.pallas_call(kernel, in_specs=[pl.BlockSpec(memory_space=pltpu.SMEM)] *...  45.1 us
    pallas_call x2, Pallas kernels, merge(): pl.pallas_call(kernel, in_specs=[pl.BlockSpec(memory_space=pltpu.SMEM)] *...  20 us
    ppermute x2, waiting for transfers between devices, body(): lax.ppermute(fwd, 'col', ahead)  9.51 us
    pallas_call x1, Pallas kernels, last_phase(): pl.pallas_call(kernel, in_specs=[pl.BlockSpec(memory_space=pl.ANY)] * n +...  4.93 us
    ppermute x1, waiting for transfers between devices, body(): remote = [lax.ppermute(local[0], 'row', swap), None]  4.9 us
    ppermute x2, starting transfers between devices, body(): lax.ppermute(fwd, 'col', ahead)  3.2 us
    ppermute x1, starting transfers between devices, body(): lax.ppermute(tokens, 'col', ahead)  3.02 us
    ppermute x2, waiting for transfers between devices, body(): lax.ppermute(bwd, 'col', behind)  2.8 us
  transfers between devices with their start and end apart: 10, of which 6 were waited for; matrix products, arithmetic and copies ran while one was open for 0% of the time, Pallas kernels for 63%

profile of v3, /device:TPU:0, one launch (start us, length us, event | category | flops | bytes accessed | tf_op | source)
XLA Modules:
  0.0 102.7 jit_solution(2533368786440313503)
XLA Ops:
  0.0 3.0 %collective-permute-start = (bf16[512,1024]{1,0:T(8,128)(2,1)}, bf16[512,1024]{1,0:T(8,128)(2,1)S(1)}, u32[]{:S(2)}, u32[]{:S(2)}) collective-permute-start(bf16[512,1024]{1,0:T(8,128)(2,1)} %refs_0_.1), channel_id=1, source_target_pairs={{0,2},{2,4},{4,6},{6,7},{7,5},{5,3},{3,1},{1,0},{8,10},{10,12},{12... | collective-permute-start | bytes 3145736 | tf_op jit(solution)/shard_map/ppermute | solution.py:377
  3.0 0.0 collective-permute-start.1
  3.7 0.0 copy-start.3
  3.7 0.6 copy-done.3
  4.3 0.0 copy-start.5
  4.3 0.7 copy-done.5
  5.0 0.0 copy-start.4
  5.0 0.0 copy-start.6
  5.0 7.7 %merge.2.refs_2_.refs_1_.refs_4_ = bf16[2048,3584]{1,0:T(8,128)(2,1)S(1)} custom-call(s32[1]{0:T(128)} %bitcast.me_ref, s32[64]{0:T(128)S(1)} %copy-done.5, s32[48]{0:T(128)S(1)} %bitcast.5, s32[1]{0:T(128)} %bitcast.3.count_ref, bf16[4096,3584]{1,0:T(8,128)(2,1)} %w_ref.3, bf16[6144,128]{1,0:T(8,128)(2,1)} %values_ref.3), custom_call_target="tpu_custom_call" | custom-call | tf_op jit(solution)/shard_map/merge/pallas_call | solution.py:118
  12.7 0.0 copy-start.1
  12.7 0.1 collective-permute-start.4
  12.8 0.0 copy-done.4
  12.8 0.0 copy-done.6
  12.8 12.3 %merge.3.refs_3_.refs_0_ = bf16[2112,3584]{1,0:T(8,128)(2,1)S(1)} custom-call(s32[1]{0:T(128)} %bitcast.me_ref, s32[64]{0:T(128)S(1)} %copy-done.6, s32[48]{0:T(128)S(1)} %bitcast.6, s32[1]{0:T(128)} %bitcast.4.count_ref, bf16[4096,3584]{1,0:T(8,128)(2,1)} %w_ref.3, bf16[6144,128]{1,0:T(8,128)(2,1)} %values_ref.3), custom_call_target="tpu_custom_call" | custom-call | tf_op jit(solution)/shard_map/merge/pallas_call | solution.py:118
  25.2 1.2 %collective-permute-done.refs_0_ = bf16[512,1024]{1,0:T(8,128)(2,1)S(1)} collective-permute-done((bf16[512,1024]{1,0:T(8,128)(2,1)}, bf16[512,1024]{1,0:T(8,128)(2,1)S(1)}, u32[]{:S(2)}, u32[]{:S(2)}) %collective-permute-start) | collective-permute-done | bytes 1048608 | tf_op jit(solution)/shard_map/ppermute | solution.py:377
  26.3 1.6 %collective-permute-done.1.refs_1_ = bf16[512,1024]{1,0:T(8,128)(2,1)} collective-permute-done((bf16[512,1024]{1,0:T(8,128)(2,1)}, bf16[512,1024]{1,0:T(8,128)(2,1)}, u32[]{:S(2)}, u32[]{:S(2)}) %collective-permute-start.1) | collective-permute-done | bytes 1048608 | tf_op jit(solution)/shard_map/ppermute | solution.py:377
  28.0 0.0 copy-done.1
  28.0 0.0 copy-start.2
  28.0 0.0 copy-start.9
  28.0 0.0 copy-start
  28.0 0.0 copy-start.7
  28.0 0.1 collective-permute-start.7
  28.1 1.6 %collective-permute-start.2 = (bf16[512,1024]{1,0:T(8,128)(2,1)S(1)}, bf16[512,1024]{1,0:T(8,128)(2,1)}, u32[]{:S(2)}, u32[]{:S(2)}) collective-permute-start(bf16[512,1024]{1,0:T(8,128)(2,1)S(1)} %get-tuple-element.13.refs_1_.refs_0_), channel_id=1, source_target_pairs={{0,2},{2,4},{4,6},{6,7},{7,5},{5,3},{3,1},{1,0},{8,10},{10,12},{12... | collective-permute-start | bytes 3145736 | tf_op jit(solution)/shard_map/ppermute | solution.py:399
  29.7 0.4 collective-permute-start.3
  30.2 4.9 %collective-permute-done.4.refs_2_.refs_6_.refs_4_ = bf16[2048,3584]{1,0:T(8,128)(2,1)} collective-permute-done((bf16[2048,3584]{1,0:T(8,128)(2,1)S(1)}, bf16[2048,3584]{1,0:T(8,128)(2,1)}, u32[]{:S(2)}, u32[]{:S(2)}) %collective-permute-start.4) | collective-permute-done | bytes 14680096 | tf_op jit(solution)/shard_map/ppermute | solution.py:381
  35.1 0.0 copy-done.2
  35.1 0.0 copy-done.9
  35.1 9.1 %phase.3.refs_2_.refs_8_ = f32[512,3584]{1,0:T(8,128)} custom-call(s32[1]{0:T(128)} %bitcast.me_ref, s32[112]{0:T(128)S(1)} %copy-done.9, bf16[512,1024]{1,0:T(8,128)(2,1)S(1)} %copy-done.2, bf16[2048,3584]{1,0:T(8,128)(2,1)} %copy-done.1, bf16[2048,3584]{1,0:T(8,128)(2,1)} %collective-permute-done.4.refs_2_.refs_6_.refs_4_), custom_call_target="tpu_custom_call" | custom-call | tf_op jit(solution)/shard_map/phase/pallas_call | solution.py:266
  44.2 0.0 copy-done
  44.2 9.5 %collective-permute-done.2.refs_0_ = bf16[512,1024]{1,0:T(8,128)(2,1)} collective-permute-done((bf16[512,1024]{1,0:T(8,128)(2,1)S(1)}, bf16[512,1024]{1,0:T(8,128)(2,1)}, u32[]{:S(2)}, u32[]{:S(2)}) %collective-permute-start.2) | collective-permute-done | bytes 1048608 | tf_op jit(solution)/shard_map/ppermute | solution.py:399
  53.7 1.5 %collective-permute-done.3.refs_1_ = bf16[512,1024]{1,0:T(8,128)(2,1)} collective-permute-done((bf16[512,1024]{1,0:T(8,128)(2,1)}, bf16[512,1024]{1,0:T(8,128)(2,1)}, u32[]{:S(2)}, u32[]{:S(2)}) %collective-permute-start.3) | collective-permute-done | bytes 1048608 | tf_op jit(solution)/shard_map/ppermute | solution.py:399
  55.3 1.6 %collective-permute-start.5 = (bf16[512,1024]{1,0:T(8,128)(2,1)}, bf16[512,1024]{1,0:T(8,128)(2,1)S(1)}, u32[]{:S(2)}, u32[]{:S(2)}) collective-permute-start(bf16[512,1024]{1,0:T(8,128)(2,1)} %get-tuple-element.15.refs_2_), channel_id=1, source_target_pairs={{0,2},{2,4},{4,6},{6,7},{7,5},{5,3},{3,1},{1,0},{8,10},{10,12},{12... | collective-permute-start | bytes 3145736 | tf_op jit(solution)/shard_map/ppermute | solution.py:399
  56.8 0.0 copy-start.8
  56.8 0.4 collective-permute-start.6
  57.3 0.0 collective-permute-done.7.refs_7_.refs_5_
  57.3 0.0 copy-done.7
  57.3 22.7 %phase.4.refs_2_.refs_6_ = f32[512,3584]{1,0:T(8,128)} custom-call(s32[1]{0:T(128)} %bitcast.me_ref, s32[256]{0:T(256)S(1)} %copy-done.7, bf16[512,1024]{1,0:T(8,128)(2,1)S(1)} %get-tuple-element.13.refs_1_.refs_0_, bf16[512,1024]{1,0:T(8,128)(2,1)} %get-tuple-element.14.refs_2_.refs_1_, bf16[512,1024]{1,0:T(8,128)(2,1)} %get-tuple-element.15.refs_2_, ...), custom_call_target="tpu_custom_call" | custom-call | tf_op jit(solution)/shard_map/phase/pallas_call | solution.py:266
  80.0 0.0 collective-permute-done.5.refs_0_
  80.0 1.3 %collective-permute-done.6.refs_1_ = bf16[512,1024]{1,0:T(8,128)(2,1)} collective-permute-done((bf16[512,1024]{1,0:T(8,128)(2,1)}, bf16[512,1024]{1,0:T(8,128)(2,1)}, u32[]{:S(2)}, u32[]{:S(2)}) %collective-permute-start.6) | collective-permute-done | bytes 1048608 | tf_op jit(solution)/shard_map/ppermute | solution.py:399
  81.3 1.1 %slice.7 = bf16[256,1024]{1,0:T(8,128)(2,1)S(1)} slice(bf16[512,1024]{1,0:T(8,128)(2,1)} %get-tuple-element.18.refs_1_), slice={[256:512], [0:1024]} | slice | bytes 1048576 | tf_op jit(solution)/shard_map/slice | solution.py:402
  82.4 1.6 %collective-permute-start.8 = (bf16[256,1024]{1,0:T(8,128)(2,1)S(1)}, bf16[256,1024]{1,0:T(8,128)(2,1)S(1)}, u32[]{:S(2)}, u32[]{:S(2)}) collective-permute-start(bf16[256,1024]{1,0:T(8,128)(2,1)S(1)} %slice.6), channel_id=1, source_target_pairs={{0,2},{2,4},{4,6},{6,7},{7,5},{5,3},{3,1},{1,0},{8,10},{10,12},{12... | collective-permute-start | bytes 1572872 | tf_op jit(solution)/shard_map/ppermute | solution.py:402
  84.0 0.5 collective-permute-start.9
  84.5 0.0 copy-done.8
  84.5 13.3 %phase.5 = (f32[512,3584]{1,0:T(8,128)S(1)}, bf16[1024,3584]{1,0:T(8,128)(2,1)S(1)}) custom-call(s32[1]{0:T(128)} %bitcast.me_ref, s32[160]{0:T(256)S(1)} %copy-done.8, bf16[512,1024]{1,0:T(8,128)(2,1)S(1)} %get-tuple-element.17.refs_0_, bf16[512,1024]{1,0:T(8,128)(2,1)} %get-tuple-element.18.refs_1_, bf16[2048,3584]{1,0:T(8,128)(2,1)} %copy-done.1, ...), custom_call_target="tpu_custom_call" | custom-call | tf_op jit(solution)/shard_map/phase/pallas_call | solution.py:266
  97.8 0.0 collective-permute-done.8.refs_0_
  97.8 0.0 collective-permute-done.9.refs_1_
  97.8 4.9 %last_phase.1 = bf16[512,3584]{1,0:T(8,128)(2,1)} custom-call(bf16[256,1024]{1,0:T(8,128)(2,1)S(1)} %collective-permute-done.8.refs_0_, bf16[256,1024]{1,0:T(8,128)(2,1)S(1)} %collective-permute-done.9.refs_1_, bf16[1024,3584]{1,0:T(8,128)(2,1)S(1)} %get-tuple-element.19.refs_2_, f32[512,3584]{1,0:T(8,128)S(1)} %get-tuple-element.20.refs_3_), custom_call_target="tpu_custom_call" | custom-call | tf_op jit(solution)/shard_map/last_phase/pallas_call | solution.py:319
  (5 shorter events, 0.0 us)
Async XLA Ops:
  0.0 26.3 %collective-permute-start = (bf16[512,1024]{1,0:T(8,128)(2,1)}, bf16[512,1024]{1,0:T(8,128)(2,1)S(1)}, u32[]{:S(2)}, u32[]{:S(2)}) collective-permute-start(bf16[512,1024]{1,0:T(8,128)(2,1)} %refs_0_.1), channel_id=1, source_target_pairs={{0,2},{2,4},{4,6},{6,7},{7,5},{5,3},{3,1},{1,0},{8,10},{10,12},{12... | collective-permute-start | bytes 3145736 | tf_op jit(solution)/shard_map/ppermute | solution.py:377
  3.0 24.9 %collective-permute-start.1 = (bf16[512,1024]{1,0:T(8,128)(2,1)}, bf16[512,1024]{1,0:T(8,128)(2,1)}, u32[]{:S(2)}, u32[]{:S(2)}) collective-permute-start(bf16[512,1024]{1,0:T(8,128)(2,1)} %refs_0_.1), channel_id=1, source_target_pairs={{2,0},{4,2},{6,4},{7,6},{5,7},{3,5},{1,3},{0,1},{10,8},{12,10},{14... | collective-permute-start | bytes 3145736 | tf_op jit(solution)/shard_map/ppermute | solution.py:377
  3.7 0.7 copy-start.3
  4.3 0.7 copy-start.5
  5.0 7.8 %copy-start.4 = (s32[48,1]{0,1:T(1,128)S(1)}, s32[48,1]{0,1:T(1,128)}, u32[]{:S(2)}) copy-start(s32[48,1]{0,1:T(1,128)} %param.12) | copy-start | bytes 580
  5.0 7.8 %copy-start.6 = (s32[64]{0:T(128)S(1)}, s32[64]{0:T(128)}, u32[]{:S(2)}) copy-start(s32[64]{0:T(128)} %constant.19.clone.order_ref) | copy-start | bytes 772
  12.7 15.3 %copy-start.1 = (bf16[2048,3584]{1,0:T(8,128)(2,1)}, bf16[2048,3584]{1,0:T(8,128)(2,1)S(1)}, u32[]{:S(2)}) copy-start(bf16[2048,3584]{1,0:T(8,128)(2,1)S(1)} %merge.2.refs_2_.refs_1_.refs_4_) | copy-start | bytes 44040196
  12.7 22.4 %collective-permute-start.4 = (bf16[2048,3584]{1,0:T(8,128)(2,1)S(1)}, bf16[2048,3584]{1,0:T(8,128)(2,1)}, u32[]{:S(2)}, u32[]{:S(2)}) collective-permute-start(bf16[2048,3584]{1,0:T(8,128)(2,1)S(1)} %merge.2.refs_2_.refs_1_.refs_4_), channel_id=1, source_target_pairs={{0,8},{8,0},{1,9},{9,1},{2,10},{10,2},{3,11},{11,3},{4,12},{12,4},... | collective-permute-start | bytes 44040200 | tf_op jit(solution)/shard_map/ppermute | solution.py:381
  28.0 7.1 %copy-start.2 = (bf16[512,1024]{1,0:T(8,128)(2,1)S(1)}, bf16[512,1024]{1,0:T(8,128)(2,1)}, u32[]{:S(2)}) copy-start(bf16[512,1024]{1,0:T(8,128)(2,1)} %refs_0_.1) | copy-start | bytes 3145732
  28.0 7.1 %copy-start.9 = (s32[112]{0:T(128)S(1)}, s32[112]{0:T(128)}, u32[]{:S(2)}) copy-start(s32[112]{0:T(128)} %constant.20.clone.table_ref) | copy-start | bytes 1348
  28.0 16.2 %copy-start = (bf16[2112,3584]{1,0:T(8,128)(2,1)}, bf16[2112,3584]{1,0:T(8,128)(2,1)S(1)}, u32[]{:S(2)}) copy-start(bf16[2112,3584]{1,0:T(8,128)(2,1)S(1)} %tie.6.refs_5_.refs_3_) | copy-start | bytes 45416452
  28.0 29.3 %copy-start.7 = (s32[256]{0:T(256)S(1)}, s32[256]{0:T(256)}, u32[]{:S(2)}) copy-start(s32[256]{0:T(256)} %constant.21.clone.table_ref) | copy-start | bytes 3076
  28.0 29.3 %collective-permute-start.7 = (bf16[2112,3584]{1,0:T(8,128)(2,1)S(1)}, bf16[2112,3584]{1,0:T(8,128)(2,1)}, u32[]{:S(2)}, u32[]{:S(2)}) collective-permute-start(bf16[2112,3584]{1,0:T(8,128)(2,1)S(1)} %tie.6.refs_5_.refs_3_), channel_id=1, source_target_pairs={{0,8},{8,0},{1,9},{9,1},{2,10},{10,2},{3,11},{11,3},{4,12},{12,4},... | collective-permute-start | bytes 45416456 | tf_op jit(solution)/shard_map/ppermute | solution.py:396
  28.1 25.7 %collective-permute-start.2 = (bf16[512,1024]{1,0:T(8,128)(2,1)S(1)}, bf16[512,1024]{1,0:T(8,128)(2,1)}, u32[]{:S(2)}, u32[]{:S(2)}) collective-permute-start(bf16[512,1024]{1,0:T(8,128)(2,1)S(1)} %get-tuple-element.13.refs_1_.refs_0_), channel_id=1, source_target_pairs={{0,2},{2,4},{4,6},{6,7},{7,5},{5,3},{3,1},{1,0},{8,10},{10,12},{12... | collective-permute-start | bytes 3145736 | tf_op jit(solution)/shard_map/ppermute | solution.py:399
  29.7 25.5 %collective-permute-start.3 = (bf16[512,1024]{1,0:T(8,128)(2,1)}, bf16[512,1024]{1,0:T(8,128)(2,1)}, u32[]{:S(2)}, u32[]{:S(2)}) collective-permute-start(bf16[512,1024]{1,0:T(8,128)(2,1)} %get-tuple-element.14.refs_2_.refs_1_), channel_id=1, source_target_pairs={{2,0},{4,2},{6,4},{7,6},{5,7},{3,5},{1,3},{0,1},{10,8},{12,10},{14... | collective-permute-start | bytes 3145736 | tf_op jit(solution)/shard_map/ppermute | solution.py:399
  55.3 24.7 %collective-permute-start.5 = (bf16[512,1024]{1,0:T(8,128)(2,1)}, bf16[512,1024]{1,0:T(8,128)(2,1)S(1)}, u32[]{:S(2)}, u32[]{:S(2)}) collective-permute-start(bf16[512,1024]{1,0:T(8,128)(2,1)} %get-tuple-element.15.refs_2_), channel_id=1, source_target_pairs={{0,2},{2,4},{4,6},{6,7},{7,5},{5,3},{3,1},{1,0},{8,10},{10,12},{12... | collective-permute-start | bytes 3145736 | tf_op jit(solution)/shard_map/ppermute | solution.py:399
  56.8 27.6 %copy-start.8 = (s32[160]{0:T(256)S(1)}, s32[160]{0:T(256)}, u32[]{:S(2)}) copy-start(s32[160]{0:T(256)} %constant.22.clone.table_ref) | copy-start | bytes 1924
  56.8 24.4 %collective-permute-start.6 = (bf16[512,1024]{1,0:T(8,128)(2,1)}, bf16[512,1024]{1,0:T(8,128)(2,1)}, u32[]{:S(2)}, u32[]{:S(2)}) collective-permute-start(bf16[512,1024]{1,0:T(8,128)(2,1)} %get-tuple-element.16.refs_3_), channel_id=1, source_target_pairs={{2,0},{4,2},{6,4},{7,6},{5,7},{3,5},{1,3},{0,1},{10,8},{12,10},{14... | collective-permute-start | bytes 3145736 | tf_op jit(solution)/shard_map/ppermute | solution.py:399
  82.4 15.4 %collective-permute-start.8 = (bf16[256,1024]{1,0:T(8,128)(2,1)S(1)}, bf16[256,1024]{1,0:T(8,128)(2,1)S(1)}, u32[]{:S(2)}, u32[]{:S(2)}) collective-permute-start(bf16[256,1024]{1,0:T(8,128)(2,1)S(1)} %slice.6), channel_id=1, source_target_pairs={{0,2},{2,4},{4,6},{6,7},{7,5},{5,3},{3,1},{1,0},{8,10},{10,12},{12... | collective-permute-start | bytes 1572872 | tf_op jit(solution)/shard_map/ppermute | solution.py:402
  84.0 13.8 %collective-permute-start.9 = (bf16[256,1024]{1,0:T(8,128)(2,1)S(1)}, bf16[256,1024]{1,0:T(8,128)(2,1)S(1)}, u32[]{:S(2)}, u32[]{:S(2)}) collective-permute-start(bf16[256,1024]{1,0:T(8,128)(2,1)S(1)} %slice.7), channel_id=1, source_target_pairs={{2,0},{4,2},{6,4},{7,6},{5,7},{3,5},{1,3},{0,1},{10,8},{12,10},{14... | collective-permute-start | bytes 1572872 | tf_op jit(solution)/shard_map/ppermute | solution.py:402

commit v4 on v3

--- a/solution.py
+++ b/solution.py
@@ -8,9 +8,9 @@
 from jax.experimental.pallas import tpu as pltpu
 from jax.sharding import PartitionSpec as P
 
-PHASE_VMEM = 30
+PHASE_VMEM = 26
 SPARE = 64
-PIN = 2
+PIN = 4
 
 
 def ring_order(n):
@@ -135,7 +135,7 @@
     return 512 if total % 512 == 0 else total
 
 
-def phase(me, table, kinds, tokens, weights, pinned, accs, last):
+def phase(me, table, kinds, tokens, weights, pinned, accs, last, keep):
     n_tokens, n_weights, n_accs = len(tokens), len(weights), len(accs)
     rows, depth = tokens[0].shape
     total = weights[0].shape[1]
@@ -150,7 +150,7 @@
         weight_refs, refs = refs[:n_weights], refs[n_weights:]
         acc_refs, refs = refs[:n_accs], refs[n_accs:]
         out_ref, refs = refs[0], refs[1:]
-        if last:
+        if keep:
             kept_ref, refs = refs[0], refs[1:]
         tbuf, wbuf, abuf, obuf, tsem, wsem, asem, osem, ksem = refs
         base = me_ref[0] * stride
@@ -202,7 +202,7 @@
                 token_copy(token_refs[0], i).wait()
 
             def step(tile, carry):
-                if last:
+                if keep:
 
                     @pl.when(tile == tiles // 2)
                     def _():
@@ -244,9 +244,9 @@
                 return carry
 
             lax.fori_loop(0, tiles, step, 0)
-            if last:
+            if keep:
                 pltpu.make_async_copy(weight_refs[0].at[pl.ds(0, depth)], kept_ref, ksem).wait()
-            else:
+            if not last:
                 for tile in range(max(0, tiles - 2), tiles):
                     store(tile).wait()
 
@@ -259,14 +259,16 @@
 
     place = pltpu.VMEM if last else pltpu.HBM
     out_shape = [place((rows, total), jnp.float32)]
-    if last:
+    out_spaces = [place]
+    if keep:
         out_shape.append(pltpu.VMEM((depth, total), weights[0].dtype))
+        out_spaces.append(pltpu.VMEM)
     operands = [me, table] + list(tokens) + [hbm(w) if k in pinned else w for k, w in enumerate(weights)]
     operands += [hbm(a) for a in accs]
     return pl.pallas_call(
         kernel,
         in_specs=[pl.BlockSpec(memory_space=pltpu.SMEM)] * 2 + [pl.BlockSpec(memory_space=pl.ANY)] * (len(operands) - 2),
-        out_specs=[pl.BlockSpec(memory_space=place)] * len(out_shape),
+        out_specs=[pl.BlockSpec(memory_space=space) for space in out_spaces],
         out_shape=out_shape,
         scratch_shapes=[
             pltpu.VMEM((rows, most * depth), tokens[0].dtype),
@@ -346,19 +348,19 @@
     devices = [row for col in meets for row in col]
     done = [set() for _ in devices]
 
-    def run(want, acc, last):
+    def run(want, acc, last, keep):
         had = [bool(d) for d in done]
         lists = [
             [(t, p) for t, p in enumerate(row) if t not in d and want(t, p)] for row, d in zip(devices, done)
         ]
         kinds = sorted({(len(items), int(h)) for items, h in zip(lists, had)})
         used_t = sorted({t for items in lists for t, _ in items})
-        ends = [row[n_col - 1] for row in devices] if last else []
+        ends = [row[n_col - 1] for row in devices] if keep else []
         used_w = sorted({place[p][0] for items in lists for _, p in items} | {place[p][0] for p in ends})
         table = np.zeros((len(lists), 4 + 3 * max(max(k for k, _ in kinds), 1)), np.int32)
         for k, items in enumerate(lists):
             table[k, :2] = len(items), had[k]
-            if last:
+            if keep:
                 table[k, 2:4] = used_w.index(place[ends[k]][0]), place[ends[k]][1]
             for i, (t, p) in enumerate(items):
                 table[k, 4 + 3 * i : 7 + 3 * i] = used_t.index(t), used_w.index(place[p][0]), place[p][1]
@@ -372,6 +374,7 @@
             [k for k, w in enumerate(used_w) if w < PIN],
             [] if acc is None else [acc],
             last,
+            keep,
         )
 
     fwd, bwd = lax.ppermute(tokens, "col", ahead), lax.ppermute(tokens, "col", behind)
@@ -389,7 +392,7 @@
     acc = None
     gate = list(local)
     for d in range(2, half + 1):
-        fwd, bwd = tie((fwd, bwd), gate)
+        (fwd,), (bwd,) = tie((fwd,), gate), tie((bwd,), gate)
         buffers += [fwd, bwd]
         if d == 2:
             (local[1],) = tie((local[1],), (fwd, bwd))
@@ -403,13 +406,13 @@
         gate = []
         if d == 2:
             weights = local + remote
-            acc = run(lambda t, p: t == 0, None, False)[0]
+            acc, kept = run(lambda t, p: t == 0, None, False, True)
             gate = [hbm(acc)]
         elif d - 1 in bounds:
-            out = run(lambda t, p: t < 2 * d - 1, acc, d == half)
-            acc, gate = out[0], [hbm(out[0])]
+            (acc,) = run(lambda t, p: t < 2 * d - 1, acc, d == half, False)
+            gate = [hbm(acc)]
         fwd, bwd = next_fwd, next_bwd
-    return last_phase([fwd, bwd], out[1], acc, jnp.bfloat16)
+    return last_phase([fwd, bwd], kept, acc, jnp.bfloat16)
 
 
 def solution(mesh):

time: 103 us -> 99.8 us (0.969)
  waiting for transfers between devices: 20 us -> 17.8 us
  local copies, waits for them, and re-layouts: 2.45 us -> 1.41 us
    ppermute x2, waiting for transfers between devices: 9.51 us -> 0.01 us  [body(): lax.ppermute(fwd, 'col', ahead)]
    ppermute x2, waiting for transfers between devices: 2.8 us -> 7.64 us  [body(): lax.ppermute(bwd, 'col', behind)]
    ppermute x1, starting transfers between devices: 0.01 us -> 2.97 us  [body(): lax.ppermute(tokens, 'col', behind)]
    ppermute x1, starting transfers between devices: 3.02 us -> 0.06 us  [body(): lax.ppermute(tokens, 'col', ahead)]
    ppermute x2, starting transfers between devices: 0.9 us -> 3.2 us  [body(): lax.ppermute(bwd, 'col', behind)]
    ppermute x2, starting transfers between devices: 3.2 us -> 0.9 us  [body(): lax.ppermute(fwd, 'col', ahead)]
    pallas_call x2, Pallas kernels: 20 us -> 17.9 us  [merge(): pl.pallas_call(kernel, in_specs=[pl.BlockSpec(memory_space=pltpu.SMEM)] *...]
    pallas_call x3, Pallas kernels: 45.1 us -> 46.5 us  [phase(): pl.pallas_call(kernel, in_specs=[pl.BlockSpec(memory_space=pltpu.SMEM)] *...]
  transfers between devices with their start and end apart: 10 -> 10, of which waited for: 6 -> 6; matrix products, arithmetic and copies ran while one was open for 0% -> 0% of each run, Pallas kernels for 63% -> 65%
where the time goes in v4:
time: 99.8 us; the launch traced here: 99.7 us
  Pallas kernels  69.4 us (70%)
  waiting for transfers between devices  17.8 us (18%)
  starting transfers between devices  10.3 us (10%)
  local copies, waits for them, and re-layouts  1.41 us (1%)
    pallas_call x3, Pallas kernels, phase(): pl.pallas_call(kernel, in_specs=[pl.BlockSpec(memory_space=pltpu.SMEM)] *...  46.5 us
    pallas_call x2, Pallas kernels, merge(): pl.pallas_call(kernel, in_specs=[pl.BlockSpec(memory_space=pltpu.SMEM)] *...  17.9 us
    ppermute x2, waiting for transfers between devices, body(): lax.ppermute(bwd, 'col', behind)  7.64 us
    pallas_call x1, Pallas kernels, last_phase(): pl.pallas_call(kernel, in_specs=[pl.BlockSpec(memory_space=pl.ANY)] * n +...  4.91 us
    ppermute x1, waiting for transfers between devices, body(): remote = [lax.ppermute(local[0], 'row', swap), None]  4.53 us
    ppermute x2, starting transfers between devices, body(): lax.ppermute(bwd, 'col', behind)  3.2 us
    ppermute x1, starting transfers between devices, body(): lax.ppermute(tokens, 'col', behind)  2.97 us
    ppermute x1, waiting for transfers between devices, body(): lax.ppermute(tokens, 'col', behind)  2.88 us
  transfers between devices with their start and end apart: 10, of which 6 were waited for; matrix products, arithmetic and copies ran while one was open for 0% of the time, Pallas kernels for 65%

profile of v4, /device:TPU:0, one launch (start us, length us, event | category | flops | bytes accessed | tf_op | source)
XLA Modules:
  0.0 99.7 jit_solution(11356324942477680996)
XLA Ops:
  0.0 3.0 %collective-permute-start.4 = (bf16[512,1024]{1,0:T(8,128)(2,1)}, bf16[512,1024]{1,0:T(8,128)(2,1)}, u32[]{:S(2)}, u32[]{:S(2)}) collective-permute-start(bf16[512,1024]{1,0:T(8,128)(2,1)} %refs_0_.1), channel_id=1, source_target_pairs={{2,0},{4,2},{6,4},{7,6},{5,7},{3,5},{1,3},{0,1},{10,8},{12,10},{14... | collective-permute-start | bytes 3145736 | tf_op jit(solution)/shard_map/ppermute | solution.py:380
  3.0 0.1 collective-permute-start
  3.7 0.0 copy-start.3
  3.7 0.6 copy-done.3
  4.3 0.0 copy-start.5
  4.3 0.7 copy-done.5
  5.0 0.0 copy-start.4
  5.0 0.0 copy-start.6
  5.0 7.0 %merge.2.refs_1_.refs_4_.refs_2_ = bf16[2048,3584]{1,0:T(8,128)(2,1)S(1)} custom-call(s32[1]{0:T(128)} %bitcast.me_ref, s32[64]{0:T(128)S(1)} %copy-done.5, s32[48]{0:T(128)S(1)} %bitcast.5, s32[1]{0:T(128)} %bitcast.3.count_ref, bf16[4096,3584]{1,0:T(8,128)(2,1)} %w_ref.3, bf16[6144,128]{1,0:T(8,128)(2,1)} %values_ref.3), custom_call_target="tpu_custom_call" | custom-call | tf_op jit(solution)/shard_map/merge/pallas_call | solution.py:118
  12.0 0.0 copy-start.1
  12.0 0.7 collective-permute-start.2
  12.7 0.0 copy-done.4
  12.7 0.0 copy-done.6
  12.7 10.9 %merge.3.refs_2_.refs_0_ = bf16[2112,3584]{1,0:T(8,128)(2,1)S(1)} custom-call(s32[1]{0:T(128)} %bitcast.me_ref, s32[64]{0:T(128)S(1)} %copy-done.6, s32[48]{0:T(128)S(1)} %bitcast.6, s32[1]{0:T(128)} %bitcast.4.count_ref, bf16[4096,3584]{1,0:T(8,128)(2,1)} %w_ref.3, bf16[6144,128]{1,0:T(8,128)(2,1)} %values_ref.3), custom_call_target="tpu_custom_call" | custom-call | tf_op jit(solution)/shard_map/merge/pallas_call | solution.py:118
  23.6 2.9 %collective-permute-done.4.refs_0_ = bf16[512,1024]{1,0:T(8,128)(2,1)} collective-permute-done((bf16[512,1024]{1,0:T(8,128)(2,1)}, bf16[512,1024]{1,0:T(8,128)(2,1)}, u32[]{:S(2)}, u32[]{:S(2)}) %collective-permute-start.4) | collective-permute-done | bytes 1048608 | tf_op jit(solution)/shard_map/ppermute | solution.py:380
  26.5 1.4 %collective-permute-done.refs_0_ = bf16[512,1024]{1,0:T(8,128)(2,1)} collective-permute-done((bf16[512,1024]{1,0:T(8,128)(2,1)}, bf16[512,1024]{1,0:T(8,128)(2,1)}, u32[]{:S(2)}, u32[]{:S(2)}) %collective-permute-start) | collective-permute-done | bytes 1048608 | tf_op jit(solution)/shard_map/ppermute | solution.py:380
  27.9 0.0 copy-done.1
  27.9 0.0 copy-start.2
  27.9 0.0 copy-start.9
  27.9 0.0 copy-start
  27.9 0.1 collective-permute-start.6
  28.0 1.6 %collective-permute-start.5 = (bf16[512,1024]{1,0:T(8,128)(2,1)}, bf16[512,1024]{1,0:T(8,128)(2,1)S(1)}, u32[]{:S(2)}, u32[]{:S(2)}) collective-permute-start(bf16[512,1024]{1,0:T(8,128)(2,1)} %tie.9.refs_2_.refs_1_), channel_id=1, source_target_pairs={{2,0},{4,2},{6,4},{7,6},{5,7},{3,5},{1,3},{0,1},{10,8},{12,10},{14... | collective-permute-start | bytes 3145736 | tf_op jit(solution)/shard_map/ppermute | solution.py:402
  29.6 0.4 collective-permute-start.1
  30.1 4.5 %collective-permute-done.2.refs_2_.refs_6_.refs_4_ = bf16[2048,3584]{1,0:T(8,128)(2,1)} collective-permute-done((bf16[2048,3584]{1,0:T(8,128)(2,1)S(1)}, bf16[2048,3584]{1,0:T(8,128)(2,1)}, u32[]{:S(2)}, u32[]{:S(2)}) %collective-permute-start.2) | collective-permute-done | bytes 14680096 | tf_op jit(solution)/shard_map/ppermute | solution.py:384
  34.6 0.0 copy-done.2
  34.6 0.0 copy-done.9
  34.6 11.5 %phase.3 = (f32[512,3584]{1,0:T(8,128)}, bf16[1024,3584]{1,0:T(8,128)(2,1)S(1)}) custom-call(s32[1]{0:T(128)} %bitcast.me_ref, s32[112]{0:T(128)S(1)} %copy-done.9, bf16[512,1024]{1,0:T(8,128)(2,1)S(1)} %copy-done.2, bf16[2048,3584]{1,0:T(8,128)(2,1)} %copy-done.1, bf16[2048,3584]{1,0:T(8,128)(2,1)} %collective-permute-done.2.refs_2_.refs_6_.refs_4_), custom_call_target="tpu_custom_call" | custom-call | tf_op jit(solution)/shard_map/phase/pallas_call | solution.py:268
  46.1 0.0 copy-done
  46.1 0.0 copy-start.8
  46.1 7.6 %collective-permute-done.5.refs_0_ = bf16[512,1024]{1,0:T(8,128)(2,1)S(1)} collective-permute-done((bf16[512,1024]{1,0:T(8,128)(2,1)}, bf16[512,1024]{1,0:T(8,128)(2,1)S(1)}, u32[]{:S(2)}, u32[]{:S(2)}) %collective-permute-start.5) | collective-permute-done | bytes 1048608 | tf_op jit(solution)/shard_map/ppermute | solution.py:402
  53.8 1.6 %collective-permute-start.8 = (bf16[512,1024]{1,0:T(8,128)(2,1)S(1)}, bf16[512,1024]{1,0:T(8,128)(2,1)S(1)}, u32[]{:S(2)}, u32[]{:S(2)}) collective-permute-start(bf16[512,1024]{1,0:T(8,128)(2,1)S(1)} %tie.10.refs_3_), channel_id=1, source_target_pairs={{2,0},{4,2},{6,4},{7,6},{5,7},{3,5},{1,3},{0,1},{10,8},{12,10},{14... | collective-permute-start | bytes 3145736 | tf_op jit(solution)/shard_map/ppermute | solution.py:402
  55.4 0.0 collective-permute-done.1.refs_0_
  55.4 0.5 collective-permute-start.3
  55.8 0.5 collective-permute-done.6.refs_7_.refs_5_
  56.3 0.0 copy-done.8
  56.3 22.3 %phase.4.refs_1_.refs_6_ = f32[512,3584]{1,0:T(8,128)} custom-call(s32[1]{0:T(128)} %bitcast.me_ref, s32[256]{0:T(256)S(1)} %copy-done.8, bf16[512,1024]{1,0:T(8,128)(2,1)} %tie.7.refs_1_.refs_0_, bf16[512,1024]{1,0:T(8,128)(2,1)} %tie.9.refs_2_.refs_1_, bf16[512,1024]{1,0:T(8,128)(2,1)S(1)} %tie.8.refs_2_, bf16[512,1024]{1,0:T(8,128)(2,1)S(1)} %tie.10.refs_3_, ...), custom_call_target="tpu_custom_call" | custom-call | tf_op jit(solution)/shard_map/phase/pallas_call | solution.py:268
  78.5 0.0 copy-start.7
  78.6 0.0 collective-permute-done.8.refs_0_
  78.6 1.8 %collective-permute-start.9 = (bf16[256,1024]{1,0:T(8,128)(2,1)S(1)}, bf16[256,1024]{1,0:T(8,128)(2,1)S(1)}, u32[]{:S(2)}, u32[]{:S(2)}) collective-permute-start(bf16[256,1024]{1,0:T(8,128)(2,1)S(1)} %slice.9), channel_id=1, source_target_pairs={{2,0},{4,2},{6,4},{7,6},{5,7},{3,5},{1,3},{0,1},{10,8},{12,10},{14... | collective-permute-start | bytes 1572872 | tf_op jit(solution)/shard_map/ppermute | solution.py:405
  80.4 0.0 collective-permute-done.3.refs_0_
  80.5 0.7 collective-permute-start.7
  81.2 0.0 copy-done.7
  81.2 12.8 %phase.5.refs_3_ = f32[512,3584]{1,0:T(8,128)S(1)} custom-call(s32[1]{0:T(128)} %bitcast.me_ref, s32[160]{0:T(256)S(1)} %copy-done.7, bf16[512,1024]{1,0:T(8,128)(2,1)S(1)} %tie.12.refs_0_, bf16[512,1024]{1,0:T(8,128)(2,1)S(1)} %tie.13.refs_1_, bf16[2048,3584]{1,0:T(8,128)(2,1)} %copy-done.1, bf16[2112,3584]{1,0:T(8,128)(2,1)} %copy-done, ...), custom_call_target="tpu_custom_call" | custom-call | tf_op jit(solution)/shard_map/phase/pallas_call | solution.py:268
  94.0 0.0 collective-permute-done.9.refs_1_
  94.0 0.8 collective-permute-done.7.refs_0_
  94.8 4.9 %last_phase.1 = bf16[512,3584]{1,0:T(8,128)(2,1)} custom-call(bf16[256,1024]{1,0:T(8,128)(2,1)S(1)} %collective-permute-done.7.refs_0_, bf16[256,1024]{1,0:T(8,128)(2,1)S(1)} %collective-permute-done.9.refs_1_, bf16[1024,3584]{1,0:T(8,128)(2,1)S(1)} %get-tuple-element.8.refs_2_, f32[512,3584]{1,0:T(8,128)S(1)} %phase.5.refs_3_), custom_call_target="tpu_custom_call" | custom-call | tf_op jit(solution)/shard_map/last_phase/pallas_call | solution.py:321
  (9 shorter events, 0.1 us)
Async XLA Ops:
  0.0 26.5 %collective-permute-start.4 = (bf16[512,1024]{1,0:T(8,128)(2,1)}, bf16[512,1024]{1,0:T(8,128)(2,1)}, u32[]{:S(2)}, u32[]{:S(2)}) collective-permute-start(bf16[512,1024]{1,0:T(8,128)(2,1)} %refs_0_.1), channel_id=1, source_target_pairs={{2,0},{4,2},{6,4},{7,6},{5,7},{3,5},{1,3},{0,1},{10,8},{12,10},{14... | collective-permute-start | bytes 3145736 | tf_op jit(solution)/shard_map/ppermute | solution.py:380
  3.0 24.9 %collective-permute-start = (bf16[512,1024]{1,0:T(8,128)(2,1)}, bf16[512,1024]{1,0:T(8,128)(2,1)}, u32[]{:S(2)}, u32[]{:S(2)}) collective-permute-start(bf16[512,1024]{1,0:T(8,128)(2,1)} %refs_0_.1), channel_id=1, source_target_pairs={{0,2},{2,4},{4,6},{6,7},{7,5},{5,3},{3,1},{1,0},{8,10},{10,12},{12... | collective-permute-start | bytes 3145736 | tf_op jit(solution)/shard_map/ppermute | solution.py:380
  3.7 0.7 copy-start.3
  4.3 0.7 copy-start.5
  5.0 7.7 %copy-start.4 = (s32[48,1]{0,1:T(1,128)S(1)}, s32[48,1]{0,1:T(1,128)}, u32[]{:S(2)}) copy-start(s32[48,1]{0,1:T(1,128)} %param.12) | copy-start | bytes 580
  5.0 7.7 %copy-start.6 = (s32[64]{0:T(128)S(1)}, s32[64]{0:T(128)}, u32[]{:S(2)}) copy-start(s32[64]{0:T(128)} %constant.19.clone.order_ref) | copy-start | bytes 772
  12.0 15.9 %copy-start.1 = (bf16[2048,3584]{1,0:T(8,128)(2,1)}, bf16[2048,3584]{1,0:T(8,128)(2,1)S(1)}, u32[]{:S(2)}) copy-start(bf16[2048,3584]{1,0:T(8,128)(2,1)S(1)} %merge.2.refs_1_.refs_4_.refs_2_) | copy-start | bytes 44040196
  12.0 22.6 %collective-permute-start.2 = (bf16[2048,3584]{1,0:T(8,128)(2,1)S(1)}, bf16[2048,3584]{1,0:T(8,128)(2,1)}, u32[]{:S(2)}, u32[]{:S(2)}) collective-permute-start(bf16[2048,3584]{1,0:T(8,128)(2,1)S(1)} %merge.2.refs_1_.refs_4_.refs_2_), channel_id=1, source_target_pairs={{0,8},{8,0},{1,9},{9,1},{2,10},{10,2},{3,11},{11,3},{4,12},{12,4},... | collective-permute-start | bytes 44040200 | tf_op jit(solution)/shard_map/ppermute | solution.py:384
  27.9 6.7 %copy-start.2 = (bf16[512,1024]{1,0:T(8,128)(2,1)S(1)}, bf16[512,1024]{1,0:T(8,128)(2,1)}, u32[]{:S(2)}) copy-start(bf16[512,1024]{1,0:T(8,128)(2,1)} %refs_0_.1) | copy-start | bytes 3145732
  27.9 6.7 %copy-start.9 = (s32[112]{0:T(128)S(1)}, s32[112]{0:T(128)}, u32[]{:S(2)}) copy-start(s32[112]{0:T(128)} %constant.20.clone.table_ref) | copy-start | bytes 1348
  27.9 18.2 %copy-start = (bf16[2112,3584]{1,0:T(8,128)(2,1)}, bf16[2112,3584]{1,0:T(8,128)(2,1)S(1)}, u32[]{:S(2)}) copy-start(bf16[2112,3584]{1,0:T(8,128)(2,1)S(1)} %tie.11.refs_5_.refs_3_) | copy-start | bytes 45416452
  27.9 28.3 %collective-permute-start.6 = (bf16[2112,3584]{1,0:T(8,128)(2,1)S(1)}, bf16[2112,3584]{1,0:T(8,128)(2,1)}, u32[]{:S(2)}, u32[]{:S(2)}) collective-permute-start(bf16[2112,3584]{1,0:T(8,128)(2,1)S(1)} %tie.11.refs_5_.refs_3_), channel_id=1, source_target_pairs={{0,8},{8,0},{1,9},{9,1},{2,10},{10,2},{3,11},{11,3},{4,12},{12,4},... | collective-permute-start | bytes 45416456 | tf_op jit(solution)/shard_map/ppermute | solution.py:399
  28.0 25.8 %collective-permute-start.5 = (bf16[512,1024]{1,0:T(8,128)(2,1)}, bf16[512,1024]{1,0:T(8,128)(2,1)S(1)}, u32[]{:S(2)}, u32[]{:S(2)}) collective-permute-start(bf16[512,1024]{1,0:T(8,128)(2,1)} %tie.9.refs_2_.refs_1_), channel_id=1, source_target_pairs={{2,0},{4,2},{6,4},{7,6},{5,7},{3,5},{1,3},{0,1},{10,8},{12,10},{14... | collective-permute-start | bytes 3145736 | tf_op jit(solution)/shard_map/ppermute | solution.py:402
  29.6 25.7 %collective-permute-start.1 = (bf16[512,1024]{1,0:T(8,128)(2,1)}, bf16[512,1024]{1,0:T(8,128)(2,1)S(1)}, u32[]{:S(2)}, u32[]{:S(2)}) collective-permute-start(bf16[512,1024]{1,0:T(8,128)(2,1)} %tie.7.refs_1_.refs_0_), channel_id=1, source_target_pairs={{0,2},{2,4},{4,6},{6,7},{7,5},{5,3},{3,1},{1,0},{8,10},{10,12},{12... | collective-permute-start | bytes 3145736 | tf_op jit(solution)/shard_map/ppermute | solution.py:402
  46.1 10.1 %copy-start.8 = (s32[256]{0:T(256)S(1)}, s32[256]{0:T(256)}, u32[]{:S(2)}) copy-start(s32[256]{0:T(256)} %constant.21.clone.table_ref) | copy-start | bytes 3076
  53.8 24.8 %collective-permute-start.8 = (bf16[512,1024]{1,0:T(8,128)(2,1)S(1)}, bf16[512,1024]{1,0:T(8,128)(2,1)S(1)}, u32[]{:S(2)}, u32[]{:S(2)}) collective-permute-start(bf16[512,1024]{1,0:T(8,128)(2,1)S(1)} %tie.10.refs_3_), channel_id=1, source_target_pairs={{2,0},{4,2},{6,4},{7,6},{5,7},{3,5},{1,3},{0,1},{10,8},{12,10},{14... | collective-permute-start | bytes 3145736 | tf_op jit(solution)/shard_map/ppermute | solution.py:402
  55.4 25.0 %collective-permute-start.3 = (bf16[512,1024]{1,0:T(8,128)(2,1)S(1)}, bf16[512,1024]{1,0:T(8,128)(2,1)S(1)}, u32[]{:S(2)}, u32[]{:S(2)}) collective-permute-start(bf16[512,1024]{1,0:T(8,128)(2,1)S(1)} %tie.8.refs_2_), channel_id=1, source_target_pairs={{0,2},{2,4},{4,6},{6,7},{7,5},{5,3},{3,1},{1,0},{8,10},{10,12},{12... | collective-permute-start | bytes 3145736 | tf_op jit(solution)/shard_map/ppermute | solution.py:402
  78.5 2.6 %copy-start.7 = (s32[160]{0:T(256)S(1)}, s32[160]{0:T(256)}, u32[]{:S(2)}) copy-start(s32[160]{0:T(256)} %constant.22.clone.table_ref) | copy-start | bytes 1924
  78.6 15.3 %collective-permute-start.9 = (bf16[256,1024]{1,0:T(8,128)(2,1)S(1)}, bf16[256,1024]{1,0:T(8,128)(2,1)S(1)}, u32[]{:S(2)}, u32[]{:S(2)}) collective-permute-start(bf16[256,1024]{1,0:T(8,128)(2,1)S(1)} %slice.9), channel_id=1, source_target_pairs={{2,0},{4,2},{6,4},{7,6},{5,7},{3,5},{1,3},{0,1},{10,8},{12,10},{14... | collective-permute-start | bytes 1572872 | tf_op jit(solution)/shard_map/ppermute | solution.py:405
  80.5 14.4 %collective-permute-start.7 = (bf16[256,1024]{1,0:T(8,128)(2,1)S(1)}, bf16[256,1024]{1,0:T(8,128)(2,1)S(1)}, u32[]{:S(2)}, u32[]{:S(2)}) collective-permute-start(bf16[256,1024]{1,0:T(8,128)(2,1)S(1)} %slice.8), channel_id=1, source_target_pairs={{0,2},{2,4},{4,6},{6,7},{7,5},{5,3},{3,1},{1,0},{8,10},{10,12},{12... | collective-permute-start | bytes 1572872 | tf_op jit(solution)/shard_map/ppermute | solution.py:405

commit v5 on v4

--- a/solution.py
+++ b/solution.py
@@ -9,7 +9,7 @@
 from jax.sharding import PartitionSpec as P
 
 PHASE_VMEM = 26
-SPARE = 64
+SPARE = 16
 PIN = 4
 
 
@@ -77,9 +77,15 @@
     width = weight.shape[1]
     col_blocks = width // block
 
-    def kernel(me_ref, order_ref, index_ref, count_ref, w_ref, values_ref, out_ref, vbuf, wsem, vsem):
+    def kernel(me_ref, index_ref, count_ref, w_ref, values_ref, out_ref, vbuf, wsem, vsem):
+        def chunk(p):
+            found = jnp.int32(0)
+            for k, chunks in enumerate(order):
+                found = jnp.where(me_ref[0] == k, int(chunks[p]), found)
+            return found
+
         value_copy = pltpu.make_async_copy(values_ref, vbuf, vsem)
-        first = [order_ref[me_ref[0] * total_pieces + p] * blocks for p in numbers]
+        first = [chunk(p) * blocks for p in numbers]
 
         def copy(k):
             rows = pl.ds(pl.multiple_of((first[k // blocks] + k % blocks) * block, block), block)
@@ -117,7 +123,7 @@
     held = 2 * (shape[0] * width + values.shape[0] * values.shape[1])
     return pl.pallas_call(
         kernel,
-        in_specs=[pl.BlockSpec(memory_space=pltpu.SMEM)] * 4 + [pl.BlockSpec(memory_space=pltpu.HBM)] * 2,
+        in_specs=[pl.BlockSpec(memory_space=pltpu.SMEM)] * 3 + [pl.BlockSpec(memory_space=pltpu.HBM)] * 2,
         out_specs=pl.BlockSpec(memory_space=pltpu.VMEM),
         out_shape=pltpu.VMEM(shape, weight.dtype),
         scratch_shapes=[
@@ -128,7 +134,7 @@
         compiler_params=pltpu.CompilerParams(vmem_limit_bytes=held + 2**20),
         cost_estimate=pl.CostEstimate(flops=0, bytes_accessed=0, transcendentals=0),
         name="merge",
-    )(me, order, index, count, hbm(weight), hbm(values))
+    )(me, index, count, hbm(weight), hbm(values))
 
 
 def tile_width(total):
@@ -344,7 +350,6 @@
     me = (lax.axis_index("col") * 2 + lax.axis_index("row")).astype(jnp.int32).reshape(1)
     index = delta_index.reshape(-1)
     count = delta_count.reshape(-1)
-    order_table = jnp.asarray(order.reshape(-1))
     devices = [row for col in meets for row in col]
     done = [set() for _ in devices]
 
@@ -379,7 +384,7 @@
 
     fwd, bwd = lax.ppermute(tokens, "col", ahead), lax.ppermute(tokens, "col", behind)
     sets = [[0, half - 1], list(range(1, half - 1))]
-    args = (me, order_table, index, count, base_weight, delta_values)
+    args = (me, order.reshape(2 * n_col, half).tolist(), index, count, base_weight, delta_values)
     local = [merge(*args, numbers, half, spare) for numbers, spare in zip(sets, (0, SPARE))]
     remote = [lax.ppermute(local[0], "row", swap), None]
     place = {}

time: 99.8 us -> 98.8 us (0.990)
    ppermute x2, waiting for transfers between devices: 7.64 us -> 9.16 us  [body(): lax.ppermute(bwd, 'col', behind)]
    ppermute x1, waiting for transfers between devices: 4.53 us -> 3.41 us  [body(): remote = [lax.ppermute(local[0], 'row', swap), None]]
    ppermute x1, waiting for transfers between devices: 2.88 us -> 3.91 us  [body(): lax.ppermute(tokens, 'col', behind)]
where the time goes in v5:
time: 98.8 us; the launch traced here: 98.7 us
  Pallas kernels  69.2 us (70%)
  waiting for transfers between devices  18.1 us (18%)
  starting transfers between devices  9.75 us (10%)
    pallas_call x3, Pallas kernels, phase(): pl.pallas_call(kernel, in_specs=[pl.BlockSpec(memory_space=pltpu.SMEM)] *...  46.5 us
    pallas_call x2, Pallas kernels, merge(): pl.pallas_call(kernel, in_specs=[pl.BlockSpec(memory_space=pltpu.SMEM)] *...  17.8 us
    ppermute x2, waiting for transfers between devices, body(): lax.ppermute(bwd, 'col', behind)  9.16 us
    pallas_call x1, Pallas kernels, last_phase(): pl.pallas_call(kernel, in_specs=[pl.BlockSpec(memory_space=pl.ANY)] * n +...  4.91 us
    ppermute x1, waiting for transfers between devices, body(): lax.ppermute(tokens, 'col', behind)  3.91 us
    ppermute x1, waiting for transfers between devices, body(): remote = [lax.ppermute(local[0], 'row', swap), None]  3.41 us
    ppermute x2, starting transfers between devices, body(): lax.ppermute(bwd, 'col', behind)  3.2 us
    ppermute x1, starting transfers between devices, body(): lax.ppermute(tokens, 'col', behind)  2.97 us
  transfers between devices with their start and end apart: 10, of which 6 were waited for; matrix products, arithmetic and copies ran while one was open for 0% of the time, Pallas kernels for 65%

profile of v5, /device:TPU:0, one launch (start us, length us, event | category | flops | bytes accessed | tf_op | source)
XLA Modules:
  0.0 98.7 jit_solution(17868051421561153218)
XLA Ops:
  0.0 3.0 %collective-permute-start.4 = (bf16[512,1024]{1,0:T(8,128)(2,1)}, bf16[512,1024]{1,0:T(8,128)(2,1)}, u32[]{:S(2)}, u32[]{:S(2)}) collective-permute-start(bf16[512,1024]{1,0:T(8,128)(2,1)} %refs_0_.1), channel_id=1, source_target_pairs={{2,0},{4,2},{6,4},{7,6},{5,7},{3,5},{1,3},{0,1},{10,8},{12,10},{14... | collective-permute-start | bytes 3145736 | tf_op jit(solution)/shard_map/ppermute | solution.py:385
  3.0 0.1 collective-permute-start
  3.7 0.0 copy-start.3
  3.7 0.6 copy-done.3
  4.3 0.0 copy-start.4
  4.3 6.8 %merge.2.refs_1_.refs_4_.refs_2_ = bf16[2048,3584]{1,0:T(8,128)(2,1)S(1)} custom-call(s32[1]{0:T(128)} %bitcast.me_ref, s32[48]{0:T(128)S(1)} %bitcast.5, s32[1]{0:T(128)} %bitcast.3.count_ref, bf16[4096,3584]{1,0:T(8,128)(2,1)} %w_ref.3, bf16[6144,128]{1,0:T(8,128)(2,1)} %values_ref.3), custom_call_target="tpu_custom_call" | custom-call | tf_op jit(solution)/shard_map/merge/pallas_call | solution.py:124
  11.1 0.0 copy-start.1
  11.1 0.4 collective-permute-start.2
  11.6 0.0 copy-done.4
  11.6 11.0 %merge.3.refs_2_.refs_0_ = bf16[2064,3584]{1,0:T(8,128)(2,1)S(1)} custom-call(s32[1]{0:T(128)} %bitcast.me_ref, s32[48]{0:T(128)S(1)} %bitcast.6, s32[1]{0:T(128)} %bitcast.4.count_ref, bf16[4096,3584]{1,0:T(8,128)(2,1)} %w_ref.3, bf16[6144,128]{1,0:T(8,128)(2,1)} %values_ref.3), custom_call_target="tpu_custom_call" | custom-call | tf_op jit(solution)/shard_map/merge/pallas_call | solution.py:124
  22.6 3.9 %collective-permute-done.4.refs_0_ = bf16[512,1024]{1,0:T(8,128)(2,1)} collective-permute-done((bf16[512,1024]{1,0:T(8,128)(2,1)}, bf16[512,1024]{1,0:T(8,128)(2,1)}, u32[]{:S(2)}, u32[]{:S(2)}) %collective-permute-start.4) | collective-permute-done | bytes 1048608 | tf_op jit(solution)/shard_map/ppermute | solution.py:385
  26.5 1.4 %collective-permute-done.refs_0_ = bf16[512,1024]{1,0:T(8,128)(2,1)} collective-permute-done((bf16[512,1024]{1,0:T(8,128)(2,1)}, bf16[512,1024]{1,0:T(8,128)(2,1)}, u32[]{:S(2)}, u32[]{:S(2)}) %collective-permute-start) | collective-permute-done | bytes 1048608 | tf_op jit(solution)/shard_map/ppermute | solution.py:385
  27.9 0.0 copy-done.1
  27.9 0.0 copy-start.2
  27.9 0.0 copy-start.7
  27.9 0.0 copy-start
  27.9 0.1 collective-permute-start.6
  28.0 1.6 %collective-permute-start.5 = (bf16[512,1024]{1,0:T(8,128)(2,1)}, bf16[512,1024]{1,0:T(8,128)(2,1)S(1)}, u32[]{:S(2)}, u32[]{:S(2)}) collective-permute-start(bf16[512,1024]{1,0:T(8,128)(2,1)} %tie.9.refs_2_.refs_1_), channel_id=1, source_target_pairs={{2,0},{4,2},{6,4},{7,6},{5,7},{3,5},{1,3},{0,1},{10,8},{12,10},{14... | collective-permute-start | bytes 3145736 | tf_op jit(solution)/shard_map/ppermute | solution.py:407
  29.6 0.4 collective-permute-start.1
  30.1 3.4 %collective-permute-done.2.refs_2_.refs_6_.refs_4_ = bf16[2048,3584]{1,0:T(8,128)(2,1)} collective-permute-done((bf16[2048,3584]{1,0:T(8,128)(2,1)S(1)}, bf16[2048,3584]{1,0:T(8,128)(2,1)}, u32[]{:S(2)}, u32[]{:S(2)}) %collective-permute-start.2) | collective-permute-done | bytes 14680096 | tf_op jit(solution)/shard_map/ppermute | solution.py:389
  33.5 0.0 copy-done.2
  33.5 0.0 copy-done.7
  33.5 11.5 %phase.3 = (f32[512,3584]{1,0:T(8,128)}, bf16[1024,3584]{1,0:T(8,128)(2,1)S(1)}) custom-call(s32[1]{0:T(128)} %bitcast.me_ref, s32[112]{0:T(128)S(1)} %copy-done.7, bf16[512,1024]{1,0:T(8,128)(2,1)S(1)} %copy-done.2, bf16[2048,3584]{1,0:T(8,128)(2,1)} %copy-done.1, bf16[2048,3584]{1,0:T(8,128)(2,1)} %collective-permute-done.2.refs_2_.refs_6_.refs_4_), custom_call_target="tpu_custom_call" | custom-call | tf_op jit(solution)/shard_map/phase/pallas_call | solution.py:274
  45.0 0.0 copy-done
  45.0 0.0 copy-start.6
  45.0 8.8 %collective-permute-done.5.refs_0_ = bf16[512,1024]{1,0:T(8,128)(2,1)S(1)} collective-permute-done((bf16[512,1024]{1,0:T(8,128)(2,1)}, bf16[512,1024]{1,0:T(8,128)(2,1)S(1)}, u32[]{:S(2)}, u32[]{:S(2)}) %collective-permute-start.5) | collective-permute-done | bytes 1048608 | tf_op jit(solution)/shard_map/ppermute | solution.py:407
  53.8 1.6 %collective-permute-start.8 = (bf16[512,1024]{1,0:T(8,128)(2,1)S(1)}, bf16[512,1024]{1,0:T(8,128)(2,1)S(1)}, u32[]{:S(2)}, u32[]{:S(2)}) collective-permute-start(bf16[512,1024]{1,0:T(8,128)(2,1)S(1)} %tie.10.refs_3_), channel_id=1, source_target_pairs={{2,0},{4,2},{6,4},{7,6},{5,7},{3,5},{1,3},{0,1},{10,8},{12,10},{14... | collective-permute-start | bytes 3145736 | tf_op jit(solution)/shard_map/ppermute | solution.py:407
  55.4 0.0 collective-permute-done.1.refs_0_
  55.4 0.5 collective-permute-start.3
  55.8 0.0 collective-permute-done.6.refs_7_.refs_5_
  55.8 0.0 copy-done.6
  55.8 22.3 %phase.4.refs_1_.refs_6_ = f32[512,3584]{1,0:T(8,128)} custom-call(s32[1]{0:T(128)} %bitcast.me_ref, s32[256]{0:T(256)S(1)} %copy-done.6, bf16[512,1024]{1,0:T(8,128)(2,1)} %tie.7.refs_1_.refs_0_, bf16[512,1024]{1,0:T(8,128)(2,1)} %tie.9.refs_2_.refs_1_, bf16[512,1024]{1,0:T(8,128)(2,1)S(1)} %tie.8.refs_2_, bf16[512,1024]{1,0:T(8,128)(2,1)S(1)} %tie.10.refs_3_, ...), custom_call_target="tpu_custom_call" | custom-call | tf_op jit(solution)/shard_map/phase/pallas_call | solution.py:274
  78.1 0.0 copy-start.5
  78.1 0.4 collective-permute-done.8.refs_0_
  78.5 1.6 %collective-permute-start.9 = (bf16[256,1024]{1,0:T(8,128)(2,1)S(1)}, bf16[256,1024]{1,0:T(8,128)(2,1)S(1)}, u32[]{:S(2)}, u32[]{:S(2)}) collective-permute-start(bf16[256,1024]{1,0:T(8,128)(2,1)S(1)} %slice.9), channel_id=1, source_target_pairs={{2,0},{4,2},{6,4},{7,6},{5,7},{3,5},{1,3},{0,1},{10,8},{12,10},{14... | collective-permute-start | bytes 1572872 | tf_op jit(solution)/shard_map/ppermute | solution.py:410
  80.2 0.0 collective-permute-done.3.refs_0_
  80.2 0.5 collective-permute-start.7
  80.7 0.0 copy-done.5
  80.7 12.8 %phase.5.refs_3_ = f32[512,3584]{1,0:T(8,128)S(1)} custom-call(s32[1]{0:T(128)} %bitcast.me_ref, s32[160]{0:T(256)S(1)} %copy-done.5, bf16[512,1024]{1,0:T(8,128)(2,1)S(1)} %tie.12.refs_0_, bf16[512,1024]{1,0:T(8,128)(2,1)S(1)} %tie.13.refs_1_, bf16[2048,3584]{1,0:T(8,128)(2,1)} %copy-done.1, bf16[2064,3584]{1,0:T(8,128)(2,1)} %copy-done, ...), custom_call_target="tpu_custom_call" | custom-call | tf_op jit(solution)/shard_map/phase/pallas_call | solution.py:274
  93.5 0.0 collective-permute-done.9.refs_1_
  93.5 0.2 collective-permute-done.7.refs_0_
  93.8 4.9 %last_phase.1 = bf16[512,3584]{1,0:T(8,128)(2,1)} custom-call(bf16[256,1024]{1,0:T(8,128)(2,1)S(1)} %collective-permute-done.7.refs_0_, bf16[256,1024]{1,0:T(8,128)(2,1)S(1)} %collective-permute-done.9.refs_1_, bf16[1024,3584]{1,0:T(8,128)(2,1)S(1)} %get-tuple-element.8.refs_2_, f32[512,3584]{1,0:T(8,128)S(1)} %phase.5.refs_3_), custom_call_target="tpu_custom_call" | custom-call | tf_op jit(solution)/shard_map/last_phase/pallas_call | solution.py:327
  (9 shorter events, 0.1 us)
Async XLA Ops:
  0.0 26.5 %collective-permute-start.4 = (bf16[512,1024]{1,0:T(8,128)(2,1)}, bf16[512,1024]{1,0:T(8,128)(2,1)}, u32[]{:S(2)}, u32[]{:S(2)}) collective-permute-start(bf16[512,1024]{1,0:T(8,128)(2,1)} %refs_0_.1), channel_id=1, source_target_pairs={{2,0},{4,2},{6,4},{7,6},{5,7},{3,5},{1,3},{0,1},{10,8},{12,10},{14... | collective-permute-start | bytes 3145736 | tf_op jit(solution)/shard_map/ppermute | solution.py:385
  3.0 24.9 %collective-permute-start = (bf16[512,1024]{1,0:T(8,128)(2,1)}, bf16[512,1024]{1,0:T(8,128)(2,1)}, u32[]{:S(2)}, u32[]{:S(2)}) collective-permute-start(bf16[512,1024]{1,0:T(8,128)(2,1)} %refs_0_.1), channel_id=1, source_target_pairs={{0,2},{2,4},{4,6},{6,7},{7,5},{5,3},{3,1},{1,0},{8,10},{10,12},{12... | collective-permute-start | bytes 3145736 | tf_op jit(solution)/shard_map/ppermute | solution.py:385
  3.7 0.7 copy-start.3
  4.3 7.2 %copy-start.4 = (s32[48,1]{0,1:T(1,128)S(1)}, s32[48,1]{0,1:T(1,128)}, u32[]{:S(2)}) copy-start(s32[48,1]{0,1:T(1,128)} %param.11) | copy-start | bytes 580
  11.1 16.8 %copy-start.1 = (bf16[2048,3584]{1,0:T(8,128)(2,1)}, bf16[2048,3584]{1,0:T(8,128)(2,1)S(1)}, u32[]{:S(2)}) copy-start(bf16[2048,3584]{1,0:T(8,128)(2,1)S(1)} %merge.2.refs_1_.refs_4_.refs_2_) | copy-start | bytes 44040196
  11.1 22.4 %collective-permute-start.2 = (bf16[2048,3584]{1,0:T(8,128)(2,1)S(1)}, bf16[2048,3584]{1,0:T(8,128)(2,1)}, u32[]{:S(2)}, u32[]{:S(2)}) collective-permute-start(bf16[2048,3584]{1,0:T(8,128)(2,1)S(1)} %merge.2.refs_1_.refs_4_.refs_2_), channel_id=1, source_target_pairs={{0,8},{8,0},{1,9},{9,1},{2,10},{10,2},{3,11},{11,3},{4,12},{12,4},... | collective-permute-start | bytes 44040200 | tf_op jit(solution)/shard_map/ppermute | solution.py:389
  27.9 5.6 %copy-start.2 = (bf16[512,1024]{1,0:T(8,128)(2,1)S(1)}, bf16[512,1024]{1,0:T(8,128)(2,1)}, u32[]{:S(2)}) copy-start(bf16[512,1024]{1,0:T(8,128)(2,1)} %refs_0_.1) | copy-start | bytes 3145732
  27.9 5.6 %copy-start.7 = (s32[112]{0:T(128)S(1)}, s32[112]{0:T(128)}, u32[]{:S(2)}) copy-start(s32[112]{0:T(128)} %constant.17.clone.table_ref) | copy-start | bytes 1348
  27.9 17.1 %copy-start = (bf16[2064,3584]{1,0:T(8,128)(2,1)}, bf16[2064,3584]{1,0:T(8,128)(2,1)S(1)}, u32[]{:S(2)}) copy-start(bf16[2064,3584]{1,0:T(8,128)(2,1)S(1)} %tie.11.refs_5_.refs_3_) | copy-start | bytes 44384260
  27.9 27.9 %collective-permute-start.6 = (bf16[2064,3584]{1,0:T(8,128)(2,1)S(1)}, bf16[2064,3584]{1,0:T(8,128)(2,1)}, u32[]{:S(2)}, u32[]{:S(2)}) collective-permute-start(bf16[2064,3584]{1,0:T(8,128)(2,1)S(1)} %tie.11.refs_5_.refs_3_), channel_id=1, source_target_pairs={{0,8},{8,0},{1,9},{9,1},{2,10},{10,2},{3,11},{11,3},{4,12},{12,4},... | collective-permute-start | bytes 44384264 | tf_op jit(solution)/shard_map/ppermute | solution.py:404
  28.0 25.8 %collective-permute-start.5 = (bf16[512,1024]{1,0:T(8,128)(2,1)}, bf16[512,1024]{1,0:T(8,128)(2,1)S(1)}, u32[]{:S(2)}, u32[]{:S(2)}) collective-permute-start(bf16[512,1024]{1,0:T(8,128)(2,1)} %tie.9.refs_2_.refs_1_), channel_id=1, source_target_pairs={{2,0},{4,2},{6,4},{7,6},{5,7},{3,5},{1,3},{0,1},{10,8},{12,10},{14... | collective-permute-start | bytes 3145736 | tf_op jit(solution)/shard_map/ppermute | solution.py:407
  29.6 25.7 %collective-permute-start.1 = (bf16[512,1024]{1,0:T(8,128)(2,1)}, bf16[512,1024]{1,0:T(8,128)(2,1)S(1)}, u32[]{:S(2)}, u32[]{:S(2)}) collective-permute-start(bf16[512,1024]{1,0:T(8,128)(2,1)} %tie.7.refs_1_.refs_0_), channel_id=1, source_target_pairs={{0,2},{2,4},{4,6},{6,7},{7,5},{5,3},{3,1},{1,0},{8,10},{10,12},{12... | collective-permute-start | bytes 3145736 | tf_op jit(solution)/shard_map/ppermute | solution.py:407
  45.0 10.8 %copy-start.6 = (s32[256]{0:T(256)S(1)}, s32[256]{0:T(256)}, u32[]{:S(2)}) copy-start(s32[256]{0:T(256)} %constant.18.clone.table_ref) | copy-start | bytes 3076
  53.8 24.7 %collective-permute-start.8 = (bf16[512,1024]{1,0:T(8,128)(2,1)S(1)}, bf16[512,1024]{1,0:T(8,128)(2,1)S(1)}, u32[]{:S(2)}, u32[]{:S(2)}) collective-permute-start(bf16[512,1024]{1,0:T(8,128)(2,1)S(1)} %tie.10.refs_3_), channel_id=1, source_target_pairs={{2,0},{4,2},{6,4},{7,6},{5,7},{3,5},{1,3},{0,1},{10,8},{12,10},{14... | collective-permute-start | bytes 3145736 | tf_op jit(solution)/shard_map/ppermute | solution.py:407
  55.4 24.8 %collective-permute-start.3 = (bf16[512,1024]{1,0:T(8,128)(2,1)S(1)}, bf16[512,1024]{1,0:T(8,128)(2,1)S(1)}, u32[]{:S(2)}, u32[]{:S(2)}) collective-permute-start(bf16[512,1024]{1,0:T(8,128)(2,1)S(1)} %tie.8.refs_2_), channel_id=1, source_target_pairs={{0,2},{2,4},{4,6},{6,7},{7,5},{5,3},{3,1},{1,0},{8,10},{10,12},{12... | collective-permute-start | bytes 3145736 | tf_op jit(solution)/shard_map/ppermute | solution.py:407
  78.1 2.6 %copy-start.5 = (s32[160]{0:T(256)S(1)}, s32[160]{0:T(256)}, u32[]{:S(2)}) copy-start(s32[160]{0:T(256)} %constant.19.clone.table_ref) | copy-start | bytes 1924
  78.5 15.0 %collective-permute-start.9 = (bf16[256,1024]{1,0:T(8,128)(2,1)S(1)}, bf16[256,1024]{1,0:T(8,128)(2,1)S(1)}, u32[]{:S(2)}, u32[]{:S(2)}) collective-permute-start(bf16[256,1024]{1,0:T(8,128)(2,1)S(1)} %slice.9), channel_id=1, source_target_pairs={{2,0},{4,2},{6,4},{7,6},{5,7},{3,5},{1,3},{0,1},{10,8},{12,10},{14... | collective-permute-start | bytes 1572872 | tf_op jit(solution)/shard_map/ppermute | solution.py:410
  80.2 13.6 %collective-permute-start.7 = (bf16[256,1024]{1,0:T(8,128)(2,1)S(1)}, bf16[256,1024]{1,0:T(8,128)(2,1)S(1)}, u32[]{:S(2)}, u32[]{:S(2)}) collective-permute-start(bf16[256,1024]{1,0:T(8,128)(2,1)S(1)} %slice.8), channel_id=1, source_target_pairs={{0,2},{2,4},{4,6},{6,7},{7,5},{5,3},{3,1},{1,0},{8,10},{10,12},{12... | collective-permute-start | bytes 1572872 | tf_op jit(solution)/shard_map/ppermute | solution.py:410

commit v6 on v5

--- a/solution.py
+++ b/solution.py
@@ -8,7 +8,7 @@
 from jax.experimental.pallas import tpu as pltpu
 from jax.sharding import PartitionSpec as P
 
-PHASE_VMEM = 26
+PHASE_VMEM = 24
 SPARE = 16
 PIN = 4
 
@@ -141,7 +141,7 @@
     return 512 if total % 512 == 0 else total
 
 
-def phase(me, table, kinds, tokens, weights, pinned, accs, last, keep):
+def phase(me, table, kinds, tokens, weights, pinned, occur, accs, last, keep):
     n_tokens, n_weights, n_accs = len(tokens), len(weights), len(accs)
     rows, depth = tokens[0].shape
     total = weights[0].shape[1]
@@ -170,10 +170,10 @@
         def piece_rows(at):
             return pl.ds(pl.multiple_of(table_ref[at] * depth, depth), depth)
 
-        def weight_copy(ref, tile, i):
+        def weight_copy(ref, rows_there, tile, i):
             slot = lax.rem(tile, slots)
             return pltpu.make_async_copy(
-                ref.at[piece_rows(base + 6 + 3 * i), columns(tile)], wbuf.at[slot, pl.ds(i * depth, depth)], wsem.at[slot, i]
+                ref.at[rows_there, columns(tile)], wbuf.at[slot, pl.ds(i * depth, depth)], wsem.at[slot, i]
             )
 
         def acc_copy(tile):
@@ -186,18 +186,18 @@
 
         def fetch(tile, count, use_acc):
             for i in range(count):
-                for w in range(n_weights):
+                for w in occur[i][1]:
 
                     @pl.when(table_ref[base + 5 + 3 * i] == w)
                     def _():
-                        weight_copy(weight_refs[w], tile, i).start()
+                        weight_copy(weight_refs[w], piece_rows(base + 6 + 3 * i), tile, i).start()
 
             if use_acc:
                 acc_copy(tile).start()
 
         def work(count, use_acc):
             for i in range(count):
-                for t in range(n_tokens):
+                for t in occur[i][0]:
 
                     @pl.when(table_ref[base + 4 + 3 * i] == t)
                     def _():
@@ -220,7 +220,7 @@
 
                 slot = lax.rem(tile, slots)
                 for i in range(count):
-                    weight_copy(weight_refs[0], tile, i).wait()
+                    weight_copy(weight_refs[0], pl.ds(0, depth), tile, i).wait()
                 if use_acc:
                     acc_copy(tile).wait()
 
@@ -377,6 +377,10 @@
             [buffers[t] for t in used_t],
             [weights[w] for w in used_w],
             [k for k, w in enumerate(used_w) if w < PIN],
+            [
+                [sorted({int(row[at + 3 * i]) for row in table if row[0] > i}) for at in (4, 5)]
+                for i in range(max(k for k, _ in kinds))
+            ],
             [] if acc is None else [acc],
             last,
             keep,

time: 98.8 us -> 98.3 us (level)
  waiting for transfers between devices: 18.1 us -> 15.3 us
  Pallas kernels: 69.2 us -> 71.9 us
    pallas_call x2, Pallas kernels: 17.8 us -> 20.6 us  [merge(): pl.pallas_call(kernel, in_specs=[pl.BlockSpec(memory_space=pltpu.SMEM)] *...]
    ppermute x1, waiting for transfers between devices: 3.91 us -> 1.37 us  [body(): lax.ppermute(tokens, 'col', behind)]
    ppermute x2, waiting for transfers between devices: 9.16 us -> 7.26 us  [body(): lax.ppermute(bwd, 'col', behind)]
    ppermute x1, waiting for transfers between devices: 3.41 us -> 4.79 us  [body(): remote = [lax.ppermute(local[0], 'row', swap), None]]
  transfers between devices with their start and end apart: 10 -> 10, of which waited for: 6 -> 6; matrix products, arithmetic and copies ran while one was open for 0% -> 0% of each run, Pallas kernels for 65% -> 68%
where the time goes in v6:
time: 98.3 us; the launch traced here: 98.1 us
  Pallas kernels  71.9 us (73%)
  waiting for transfers between devices  15.3 us (16%)
  starting transfers between devices  9.4 us (10%)
    pallas_call x3, Pallas kernels, phase(): pl.pallas_call(kernel, in_specs=[pl.BlockSpec(memory_space=pltpu.SMEM)] *...  46.4 us
    pallas_call x2, Pallas kernels, merge(): pl.pallas_call(kernel, in_specs=[pl.BlockSpec(memory_space=pltpu.SMEM)] *...  20.6 us
    ppermute x2, waiting for transfers between devices, body(): lax.ppermute(bwd, 'col', behind)  7.26 us
    pallas_call x1, Pallas kernels, last_phase(): pl.pallas_call(kernel, in_specs=[pl.BlockSpec(memory_space=pl.ANY)] * n +...  4.91 us
    ppermute x1, waiting for transfers between devices, body(): remote = [lax.ppermute(local[0], 'row', swap), None]  4.79 us
    ppermute x2, starting transfers between devices, body(): lax.ppermute(bwd, 'col', behind)  3.2 us
    ppermute x1, starting transfers between devices, body(): lax.ppermute(tokens, 'col', behind)  2.97 us
  transfers between devices with their start and end apart: 10, of which 6 were waited for; matrix products, arithmetic and copies ran while one was open for 0% of the time, Pallas kernels for 68%

profile of v6, /device:TPU:0, one launch (start us, length us, event | category | flops | bytes accessed | tf_op | source)
XLA Modules:
  0.0 98.1 jit_solution(13658731116144724642)
XLA Ops:
  0.0 3.0 %collective-permute-start.4 = (bf16[512,1024]{1,0:T(8,128)(2,1)}, bf16[512,1024]{1,0:T(8,128)(2,1)S(1)}, u32[]{:S(2)}, u32[]{:S(2)}) collective-permute-start(bf16[512,1024]{1,0:T(8,128)(2,1)} %refs_0_.1), channel_id=1, source_target_pairs={{2,0},{4,2},{6,4},{7,6},{5,7},{3,5},{1,3},{0,1},{10,8},{12,10},{14... | collective-permute-start | bytes 3145736 | tf_op jit(solution)/shard_map/ppermute | solution.py:389
  3.0 0.1 collective-permute-start
  3.7 0.0 copy-start.3
  3.7 0.6 copy-done.3
  4.3 0.0 copy-start.4
  4.3 8.1 %merge.2.refs_1_.refs_4_.refs_2_ = bf16[2048,3584]{1,0:T(8,128)(2,1)S(1)} custom-call(s32[1]{0:T(128)} %bitcast.me_ref, s32[48]{0:T(128)S(1)} %bitcast.5, s32[1]{0:T(128)} %bitcast.3.count_ref, bf16[4096,3584]{1,0:T(8,128)(2,1)} %w_ref.3, bf16[6144,128]{1,0:T(8,128)(2,1)} %values_ref.3), custom_call_target="tpu_custom_call" | custom-call | tf_op jit(solution)/shard_map/merge/pallas_call | solution.py:124
  12.4 0.0 copy-start.1
  12.4 0.1 collective-permute-start.2
  12.5 0.0 copy-done.4
  12.5 12.5 %merge.3.refs_2_.refs_0_ = bf16[2064,3584]{1,0:T(8,128)(2,1)S(1)} custom-call(s32[1]{0:T(128)} %bitcast.me_ref, s32[48]{0:T(128)S(1)} %bitcast.6, s32[1]{0:T(128)} %bitcast.4.count_ref, bf16[4096,3584]{1,0:T(8,128)(2,1)} %w_ref.3, bf16[6144,128]{1,0:T(8,128)(2,1)} %values_ref.3), custom_call_target="tpu_custom_call" | custom-call | tf_op jit(solution)/shard_map/merge/pallas_call | solution.py:124
  25.0 1.4 %collective-permute-done.4.refs_0_ = bf16[512,1024]{1,0:T(8,128)(2,1)S(1)} collective-permute-done((bf16[512,1024]{1,0:T(8,128)(2,1)}, bf16[512,1024]{1,0:T(8,128)(2,1)S(1)}, u32[]{:S(2)}, u32[]{:S(2)}) %collective-permute-start.4) | collective-permute-done | bytes 1048608 | tf_op jit(solution)/shard_map/ppermute | solution.py:389
  26.4 1.4 %collective-permute-done.refs_0_ = bf16[512,1024]{1,0:T(8,128)(2,1)S(1)} collective-permute-done((bf16[512,1024]{1,0:T(8,128)(2,1)}, bf16[512,1024]{1,0:T(8,128)(2,1)S(1)}, u32[]{:S(2)}, u32[]{:S(2)}) %collective-permute-start) | collective-permute-done | bytes 1048608 | tf_op jit(solution)/shard_map/ppermute | solution.py:389
  27.8 0.0 copy-done.1
  27.8 0.0 copy-start.2
  27.8 0.0 copy-start.7
  27.8 0.0 copy-start
  27.8 0.1 collective-permute-start.6
  27.9 1.6 %collective-permute-start.5 = (bf16[512,1024]{1,0:T(8,128)(2,1)S(1)}, bf16[512,1024]{1,0:T(8,128)(2,1)S(1)}, u32[]{:S(2)}, u32[]{:S(2)}) collective-permute-start(bf16[512,1024]{1,0:T(8,128)(2,1)S(1)} %tie.9.refs_2_.refs_1_), channel_id=1, source_target_pairs={{2,0},{4,2},{6,4},{7,6},{5,7},{3,5},{1,3},{0,1},{10,8},{12,10},{14... | collective-permute-start | bytes 3145736 | tf_op jit(solution)/shard_map/ppermute | solution.py:411
  29.5 0.4 collective-permute-start.1
  30.0 4.8 %collective-permute-done.2.refs_2_.refs_6_.refs_4_ = bf16[2048,3584]{1,0:T(8,128)(2,1)} collective-permute-done((bf16[2048,3584]{1,0:T(8,128)(2,1)S(1)}, bf16[2048,3584]{1,0:T(8,128)(2,1)}, u32[]{:S(2)}, u32[]{:S(2)}) %collective-permute-start.2) | collective-permute-done | bytes 14680096 | tf_op jit(solution)/shard_map/ppermute | solution.py:393
  34.8 0.0 copy-done.2
  34.8 0.0 copy-done.7
  34.8 11.5 %phase.3 = (f32[512,3584]{1,0:T(8,128)}, bf16[1024,3584]{1,0:T(8,128)(2,1)S(1)}) custom-call(s32[1]{0:T(128)} %bitcast.me_ref, s32[112]{0:T(128)S(1)} %copy-done.7, bf16[512,1024]{1,0:T(8,128)(2,1)S(1)} %copy-done.2, bf16[2048,3584]{1,0:T(8,128)(2,1)} %copy-done.1, bf16[2048,3584]{1,0:T(8,128)(2,1)} %collective-permute-done.2.refs_2_.refs_6_.refs_4_), custom_call_target="tpu_custom_call" | custom-call | tf_op jit(solution)/shard_map/phase/pallas_call | solution.py:274
  46.3 0.0 copy-done
  46.3 0.0 copy-start.6
  46.3 7.2 %collective-permute-done.5.refs_0_ = bf16[512,1024]{1,0:T(8,128)(2,1)S(1)} collective-permute-done((bf16[512,1024]{1,0:T(8,128)(2,1)S(1)}, bf16[512,1024]{1,0:T(8,128)(2,1)S(1)}, u32[]{:S(2)}, u32[]{:S(2)}) %collective-permute-start.5) | collective-permute-done | bytes 1048608 | tf_op jit(solution)/shard_map/ppermute | solution.py:411
  53.5 1.6 %collective-permute-start.8 = (bf16[512,1024]{1,0:T(8,128)(2,1)S(1)}, bf16[512,1024]{1,0:T(8,128)(2,1)S(1)}, u32[]{:S(2)}, u32[]{:S(2)}) collective-permute-start(bf16[512,1024]{1,0:T(8,128)(2,1)S(1)} %tie.10.refs_3_), channel_id=1, source_target_pairs={{2,0},{4,2},{6,4},{7,6},{5,7},{3,5},{1,3},{0,1},{10,8},{12,10},{14... | collective-permute-start | bytes 3145736 | tf_op jit(solution)/shard_map/ppermute | solution.py:411
  55.0 0.0 collective-permute-done.1.refs_0_
  55.1 0.5 collective-permute-start.3
  55.5 0.4 collective-permute-done.6.refs_7_.refs_5_
  55.9 0.0 copy-done.6
  55.9 22.2 %phase.4.refs_1_.refs_6_ = f32[512,3584]{1,0:T(8,128)} custom-call(s32[1]{0:T(128)} %bitcast.me_ref, s32[256]{0:T(256)S(1)} %copy-done.6, bf16[512,1024]{1,0:T(8,128)(2,1)S(1)} %tie.7.refs_1_.refs_0_, bf16[512,1024]{1,0:T(8,128)(2,1)S(1)} %tie.9.refs_2_.refs_1_, bf16[512,1024]{1,0:T(8,128)(2,1)S(1)} %tie.8.refs_2_, bf16[512,1024]{1,0:T(8,128)(2,1)S(1)} %tie.10.refs_3_, ...), custom_call_target="tpu_custom_call" | custom-call | tf_op jit(solution)/shard_map/phase/pallas_call | solution.py:274
  78.1 0.0 copy-start.5
  78.1 0.1 collective-permute-done.8.refs_0_
  78.2 1.6 %collective-permute-start.9 = (bf16[256,1024]{1,0:T(8,128)(2,1)S(1)}, bf16[256,1024]{1,0:T(8,128)(2,1)S(1)}, u32[]{:S(2)}, u32[]{:S(2)}) collective-permute-start(bf16[256,1024]{1,0:T(8,128)(2,1)S(1)} %slice.9), channel_id=1, source_target_pairs={{2,0},{4,2},{6,4},{7,6},{5,7},{3,5},{1,3},{0,1},{10,8},{12,10},{14... | collective-permute-start | bytes 1572872 | tf_op jit(solution)/shard_map/ppermute | solution.py:414
  79.9 0.0 collective-permute-done.3.refs_0_
  79.9 0.5 collective-permute-start.7
  80.4 0.0 copy-done.5
  80.4 12.8 %phase.5.refs_3_ = f32[512,3584]{1,0:T(8,128)S(1)} custom-call(s32[1]{0:T(128)} %bitcast.me_ref, s32[160]{0:T(256)S(1)} %copy-done.5, bf16[512,1024]{1,0:T(8,128)(2,1)S(1)} %tie.12.refs_0_, bf16[512,1024]{1,0:T(8,128)(2,1)S(1)} %tie.13.refs_1_, bf16[2048,3584]{1,0:T(8,128)(2,1)} %copy-done.1, bf16[2064,3584]{1,0:T(8,128)(2,1)} %copy-done, ...), custom_call_target="tpu_custom_call" | custom-call | tf_op jit(solution)/shard_map/phase/pallas_call | solution.py:274
  93.2 0.0 collective-permute-done.9.refs_1_
  93.2 0.0 collective-permute-done.7.refs_0_
  93.2 4.9 %last_phase.1 = bf16[512,3584]{1,0:T(8,128)(2,1)} custom-call(bf16[256,1024]{1,0:T(8,128)(2,1)S(1)} %collective-permute-done.7.refs_0_, bf16[256,1024]{1,0:T(8,128)(2,1)S(1)} %collective-permute-done.9.refs_1_, bf16[1024,3584]{1,0:T(8,128)(2,1)S(1)} %get-tuple-element.8.refs_2_, f32[512,3584]{1,0:T(8,128)S(1)} %phase.5.refs_3_), custom_call_target="tpu_custom_call" | custom-call | tf_op jit(solution)/shard_map/last_phase/pallas_call | solution.py:327
  (9 shorter events, 0.1 us)
Async XLA Ops:
  0.0 26.4 %collective-permute-start.4 = (bf16[512,1024]{1,0:T(8,128)(2,1)}, bf16[512,1024]{1,0:T(8,128)(2,1)S(1)}, u32[]{:S(2)}, u32[]{:S(2)}) collective-permute-start(bf16[512,1024]{1,0:T(8,128)(2,1)} %refs_0_.1), channel_id=1, source_target_pairs={{2,0},{4,2},{6,4},{7,6},{5,7},{3,5},{1,3},{0,1},{10,8},{12,10},{14... | collective-permute-start | bytes 3145736 | tf_op jit(solution)/shard_map/ppermute | solution.py:389
  3.0 24.8 %collective-permute-start = (bf16[512,1024]{1,0:T(8,128)(2,1)}, bf16[512,1024]{1,0:T(8,128)(2,1)S(1)}, u32[]{:S(2)}, u32[]{:S(2)}) collective-permute-start(bf16[512,1024]{1,0:T(8,128)(2,1)} %refs_0_.1), channel_id=1, source_target_pairs={{0,2},{2,4},{4,6},{6,7},{7,5},{5,3},{3,1},{1,0},{8,10},{10,12},{12... | collective-permute-start | bytes 3145736 | tf_op jit(solution)/shard_map/ppermute | solution.py:389
  3.7 0.7 copy-start.3
  4.3 8.2 %copy-start.4 = (s32[48,1]{0,1:T(1,128)S(1)}, s32[48,1]{0,1:T(1,128)}, u32[]{:S(2)}) copy-start(s32[48,1]{0,1:T(1,128)} %param.11) | copy-start | bytes 580
  12.4 15.4 %copy-start.1 = (bf16[2048,3584]{1,0:T(8,128)(2,1)}, bf16[2048,3584]{1,0:T(8,128)(2,1)S(1)}, u32[]{:S(2)}) copy-start(bf16[2048,3584]{1,0:T(8,128)(2,1)S(1)} %merge.2.refs_1_.refs_4_.refs_2_) | copy-start | bytes 44040196
  12.4 22.4 %collective-permute-start.2 = (bf16[2048,3584]{1,0:T(8,128)(2,1)S(1)}, bf16[2048,3584]{1,0:T(8,128)(2,1)}, u32[]{:S(2)}, u32[]{:S(2)}) collective-permute-start(bf16[2048,3584]{1,0:T(8,128)(2,1)S(1)} %merge.2.refs_1_.refs_4_.refs_2_), channel_id=1, source_target_pairs={{0,8},{8,0},{1,9},{9,1},{2,10},{10,2},{3,11},{11,3},{4,12},{12,4},... | collective-permute-start | bytes 44040200 | tf_op jit(solution)/shard_map/ppermute | solution.py:393
  27.8 7.0 %copy-start.2 = (bf16[512,1024]{1,0:T(8,128)(2,1)S(1)}, bf16[512,1024]{1,0:T(8,128)(2,1)}, u32[]{:S(2)}) copy-start(bf16[512,1024]{1,0:T(8,128)(2,1)} %refs_0_.1) | copy-start | bytes 3145732
  27.8 7.0 %copy-start.7 = (s32[112]{0:T(128)S(1)}, s32[112]{0:T(128)}, u32[]{:S(2)}) copy-start(s32[112]{0:T(128)} %constant.17.clone.table_ref) | copy-start | bytes 1348
  27.8 18.4 %copy-start = (bf16[2064,3584]{1,0:T(8,128)(2,1)}, bf16[2064,3584]{1,0:T(8,128)(2,1)S(1)}, u32[]{:S(2)}) copy-start(bf16[2064,3584]{1,0:T(8,128)(2,1)S(1)} %tie.11.refs_5_.refs_3_) | copy-start | bytes 44384260
  27.8 28.1 %collective-permute-start.6 = (bf16[2064,3584]{1,0:T(8,128)(2,1)S(1)}, bf16[2064,3584]{1,0:T(8,128)(2,1)}, u32[]{:S(2)}, u32[]{:S(2)}) collective-permute-start(bf16[2064,3584]{1,0:T(8,128)(2,1)S(1)} %tie.11.refs_5_.refs_3_), channel_id=1, source_target_pairs={{0,8},{8,0},{1,9},{9,1},{2,10},{10,2},{3,11},{11,3},{4,12},{12,4},... | collective-permute-start | bytes 44384264 | tf_op jit(solution)/shard_map/ppermute | solution.py:408
  27.9 25.6 %collective-permute-start.5 = (bf16[512,1024]{1,0:T(8,128)(2,1)S(1)}, bf16[512,1024]{1,0:T(8,128)(2,1)S(1)}, u32[]{:S(2)}, u32[]{:S(2)}) collective-permute-start(bf16[512,1024]{1,0:T(8,128)(2,1)S(1)} %tie.9.refs_2_.refs_1_), channel_id=1, source_target_pairs={{2,0},{4,2},{6,4},{7,6},{5,7},{3,5},{1,3},{0,1},{10,8},{12,10},{14... | collective-permute-start | bytes 3145736 | tf_op jit(solution)/shard_map/ppermute | solution.py:411
  29.5 25.5 %collective-permute-start.1 = (bf16[512,1024]{1,0:T(8,128)(2,1)S(1)}, bf16[512,1024]{1,0:T(8,128)(2,1)S(1)}, u32[]{:S(2)}, u32[]{:S(2)}) collective-permute-start(bf16[512,1024]{1,0:T(8,128)(2,1)S(1)} %tie.7.refs_1_.refs_0_), channel_id=1, source_target_pairs={{0,2},{2,4},{4,6},{6,7},{7,5},{5,3},{3,1},{1,0},{8,10},{10,12},{12... | collective-permute-start | bytes 3145736 | tf_op jit(solution)/shard_map/ppermute | solution.py:411
  46.3 9.7 %copy-start.6 = (s32[256]{0:T(256)S(1)}, s32[256]{0:T(256)}, u32[]{:S(2)}) copy-start(s32[256]{0:T(256)} %constant.18.clone.table_ref) | copy-start | bytes 3076
  53.5 24.7 %collective-permute-start.8 = (bf16[512,1024]{1,0:T(8,128)(2,1)S(1)}, bf16[512,1024]{1,0:T(8,128)(2,1)S(1)}, u32[]{:S(2)}, u32[]{:S(2)}) collective-permute-start(bf16[512,1024]{1,0:T(8,128)(2,1)S(1)} %tie.10.refs_3_), channel_id=1, source_target_pairs={{2,0},{4,2},{6,4},{7,6},{5,7},{3,5},{1,3},{0,1},{10,8},{12,10},{14... | collective-permute-start | bytes 3145736 | tf_op jit(solution)/shard_map/ppermute | solution.py:411
  55.1 24.8 %collective-permute-start.3 = (bf16[512,1024]{1,0:T(8,128)(2,1)S(1)}, bf16[512,1024]{1,0:T(8,128)(2,1)S(1)}, u32[]{:S(2)}, u32[]{:S(2)}) collective-permute-start(bf16[512,1024]{1,0:T(8,128)(2,1)S(1)} %tie.8.refs_2_), channel_id=1, source_target_pairs={{0,2},{2,4},{4,6},{6,7},{7,5},{5,3},{3,1},{1,0},{8,10},{10,12},{12... | collective-permute-start | bytes 3145736 | tf_op jit(solution)/shard_map/ppermute | solution.py:411
  78.1 2.3 %copy-start.5 = (s32[160]{0:T(256)S(1)}, s32[160]{0:T(256)}, u32[]{:S(2)}) copy-start(s32[160]{0:T(256)} %constant.19.clone.table_ref) | copy-start | bytes 1924
  78.2 15.0 %collective-permute-start.9 = (bf16[256,1024]{1,0:T(8,128)(2,1)S(1)}, bf16[256,1024]{1,0:T(8,128)(2,1)S(1)}, u32[]{:S(2)}, u32[]{:S(2)}) collective-permute-start(bf16[256,1024]{1,0:T(8,128)(2,1)S(1)} %slice.9), channel_id=1, source_target_pairs={{2,0},{4,2},{6,4},{7,6},{5,7},{3,5},{1,3},{0,1},{10,8},{12,10},{14... | collective-permute-start | bytes 1572872 | tf_op jit(solution)/shard_map/ppermute | solution.py:414
  79.9 13.3 %collective-permute-start.7 = (bf16[256,1024]{1,0:T(8,128)(2,1)S(1)}, bf16[256,1024]{1,0:T(8,128)(2,1)S(1)}, u32[]{:S(2)}, u32[]{:S(2)}) collective-permute-start(bf16[256,1024]{1,0:T(8,128)(2,1)S(1)} %slice.8), channel_id=1, source_target_pairs={{0,2},{2,4},{4,6},{6,7},{7,5},{5,3},{3,1},{1,0},{8,10},{10,12},{12... | collective-permute-start | bytes 1572872 | tf_op jit(solution)/shard_map/ppermute | solution.py:414

commit v7 on v6

--- a/solution.py
+++ b/solution.py
@@ -97,27 +97,28 @@
         if spare:
             rest = out_ref.at[pl.ds(pieces * blocks * block, spare)]
             rest[...] = jnp.zeros((spare, width), out_ref.dtype)
-        value_copy.wait()
-        for k in range(pieces * blocks):
-            copy(k).wait()
-
-        def slot(s, carry):
-            which = index_ref[s]
-            row = which // col_blocks
-            for p in range(pieces):
-                row_here = row - first[p]
-
-                @pl.when(jnp.logical_and(row_here >= 0, row_here < blocks))
+        for p in range(pieces):
+            for k in range(p * blocks, (p + 1) * blocks):
+                copy(k).wait()
+            if p == 0:
+                value_copy.wait()
+
+            def slot(s, carry):
+                which = index_ref[s]
+                col = which - first[p] * col_blocks
+
+                @pl.when(jnp.logical_and(col >= 0, col < blocks * col_blocks))
                 def _():
+                    row_here = col // col_blocks
                     rows = pl.ds(pl.multiple_of((p * blocks + row_here) * block, block), block)
-                    cols = pl.ds(pl.multiple_of((which - row * col_blocks) * block, block), block)
+                    cols = pl.ds(pl.multiple_of((col - row_here * col_blocks) * block, block), block)
                     value = vbuf[pl.ds(pl.multiple_of(s * block, block), block), :]
                     old = out_ref[rows, cols]
                     out_ref[rows, cols] = (old.astype(jnp.float32) + value.astype(jnp.float32)).astype(out_ref.dtype)
 
-            return carry
-
-        lax.fori_loop(0, count_ref[0], slot, 0)
+                return carry
+
+            lax.fori_loop(0, count_ref[0], slot, 0)
 
     shape = (pieces * blocks * block + spare, width)
     held = 2 * (shape[0] * width + values.shape[0] * values.shape[1])

time: 98.3 us -> 98.3 us (level)
  Pallas kernels: 71.9 us -> 69.9 us
  waiting for transfers between devices: 15.3 us -> 17.2 us
    pallas_call x2, Pallas kernels: 20.6 us -> 18.6 us  [merge(): pl.pallas_call(kernel, in_specs=[pl.BlockSpec(memory_space=pltpu.SMEM)] *...]
    ppermute x1, waiting for transfers between devices: 1.37 us -> 3.32 us  [body(): lax.ppermute(tokens, 'col', behind)]
    ppermute x2, waiting for transfers between devices: 7.26 us -> 8.64 us  [body(): lax.ppermute(bwd, 'col', behind)]
  transfers between devices with their start and end apart: 10 -> 10, of which waited for: 6 -> 5; matrix products, arithmetic and copies ran while one was open for 0% -> 0% of each run, Pallas kernels for 68% -> 66%
where the time goes in v7:
time: 98.3 us; the launch traced here: 98.1 us
  Pallas kernels  69.9 us (71%)
  waiting for transfers between devices  17.2 us (17%)
  starting transfers between devices  9.4 us (10%)
    pallas_call x3, Pallas kernels, phase(): pl.pallas_call(kernel, in_specs=[pl.BlockSpec(memory_space=pltpu.SMEM)] *...  46.4 us
    pallas_call x2, Pallas kernels, merge(): pl.pallas_call(kernel, in_specs=[pl.BlockSpec(memory_space=pltpu.SMEM)] *...  18.6 us
    ppermute x2, waiting for transfers between devices, body(): lax.ppermute(bwd, 'col', behind)  8.64 us
    pallas_call x1, Pallas kernels, last_phase(): pl.pallas_call(kernel, in_specs=[pl.BlockSpec(memory_space=pl.ANY)] * n +...  4.91 us
    ppermute x1, waiting for transfers between devices, body(): remote = [lax.ppermute(local[0], 'row', swap), None]  3.84 us
    ppermute x1, waiting for transfers between devices, body(): lax.ppermute(tokens, 'col', behind)  3.32 us
    ppermute x2, starting transfers between devices, body(): lax.ppermute(bwd, 'col', behind)  3.2 us
    ppermute x1, starting transfers between devices, body(): lax.ppermute(tokens, 'col', behind)  2.97 us
  transfers between devices with their start and end apart: 10, of which 5 were waited for; matrix products, arithmetic and copies ran while one was open for 0% of the time, Pallas kernels for 66%

profile of v7, /device:TPU:0, one launch (start us, length us, event | category | flops | bytes accessed | tf_op | source)
XLA Modules:
  0.0 98.1 jit_solution(5745453007396454668)
XLA Ops:
  0.0 3.0 %collective-permute-start.4 = (bf16[512,1024]{1,0:T(8,128)(2,1)}, bf16[512,1024]{1,0:T(8,128)(2,1)S(1)}, u32[]{:S(2)}, u32[]{:S(2)}) collective-permute-start(bf16[512,1024]{1,0:T(8,128)(2,1)} %refs_0_.1), channel_id=1, source_target_pairs={{2,0},{4,2},{6,4},{7,6},{5,7},{3,5},{1,3},{0,1},{10,8},{12,10},{14... | collective-permute-start | bytes 3145736 | tf_op jit(solution)/shard_map/ppermute | solution.py:390
  3.0 0.1 collective-permute-start
  3.7 0.0 copy-start.3
  3.7 0.6 copy-done.3
  4.3 0.0 copy-start.4
  4.3 7.1 %merge.2.refs_1_.refs_4_.refs_2_ = bf16[2048,3584]{1,0:T(8,128)(2,1)S(1)} custom-call(s32[1]{0:T(128)} %bitcast.me_ref, s32[48]{0:T(128)S(1)} %bitcast.5, s32[1]{0:T(128)} %bitcast.3.count_ref, bf16[4096,3584]{1,0:T(8,128)(2,1)} %w_ref.3, bf16[6144,128]{1,0:T(8,128)(2,1)} %values_ref.3), custom_call_target="tpu_custom_call" | custom-call | tf_op jit(solution)/shard_map/merge/pallas_call | solution.py:125
  11.5 0.0 copy-start.1
  11.5 0.1 collective-permute-start.2
  11.6 0.0 copy-done.4
  11.6 11.5 %merge.3.refs_2_.refs_0_ = bf16[2064,3584]{1,0:T(8,128)(2,1)S(1)} custom-call(s32[1]{0:T(128)} %bitcast.me_ref, s32[48]{0:T(128)S(1)} %bitcast.6, s32[1]{0:T(128)} %bitcast.4.count_ref, bf16[4096,3584]{1,0:T(8,128)(2,1)} %w_ref.3, bf16[6144,128]{1,0:T(8,128)(2,1)} %values_ref.3), custom_call_target="tpu_custom_call" | custom-call | tf_op jit(solution)/shard_map/merge/pallas_call | solution.py:125
  23.1 3.3 %collective-permute-done.4.refs_0_ = bf16[512,1024]{1,0:T(8,128)(2,1)S(1)} collective-permute-done((bf16[512,1024]{1,0:T(8,128)(2,1)}, bf16[512,1024]{1,0:T(8,128)(2,1)S(1)}, u32[]{:S(2)}, u32[]{:S(2)}) %collective-permute-start.4) | collective-permute-done | bytes 1048608 | tf_op jit(solution)/shard_map/ppermute | solution.py:390
  26.4 1.4 %collective-permute-done.refs_0_ = bf16[512,1024]{1,0:T(8,128)(2,1)S(1)} collective-permute-done((bf16[512,1024]{1,0:T(8,128)(2,1)}, bf16[512,1024]{1,0:T(8,128)(2,1)S(1)}, u32[]{:S(2)}, u32[]{:S(2)}) %collective-permute-start) | collective-permute-done | bytes 1048608 | tf_op jit(solution)/shard_map/ppermute | solution.py:390
  27.8 0.0 copy-done.1
  27.8 0.0 copy-start.2
  27.8 0.0 copy-start.7
  27.8 0.0 copy-start
  27.8 0.1 collective-permute-start.6
  27.9 1.6 %collective-permute-start.5 = (bf16[512,1024]{1,0:T(8,128)(2,1)S(1)}, bf16[512,1024]{1,0:T(8,128)(2,1)S(1)}, u32[]{:S(2)}, u32[]{:S(2)}) collective-permute-start(bf16[512,1024]{1,0:T(8,128)(2,1)S(1)} %tie.9.refs_2_.refs_1_), channel_id=1, source_target_pairs={{2,0},{4,2},{6,4},{7,6},{5,7},{3,5},{1,3},{0,1},{10,8},{12,10},{14... | collective-permute-start | bytes 3145736 | tf_op jit(solution)/shard_map/ppermute | solution.py:412
  29.5 0.4 collective-permute-start.1
  30.0 3.8 %collective-permute-done.2.refs_2_.refs_6_.refs_4_ = bf16[2048,3584]{1,0:T(8,128)(2,1)} collective-permute-done((bf16[2048,3584]{1,0:T(8,128)(2,1)S(1)}, bf16[2048,3584]{1,0:T(8,128)(2,1)}, u32[]{:S(2)}, u32[]{:S(2)}) %collective-permute-start.2) | collective-permute-done | bytes 14680096 | tf_op jit(solution)/shard_map/ppermute | solution.py:394
  33.8 0.0 copy-done.2
  33.8 0.0 copy-done.7
  33.8 11.5 %phase.3 = (f32[512,3584]{1,0:T(8,128)}, bf16[1024,3584]{1,0:T(8,128)(2,1)S(1)}) custom-call(s32[1]{0:T(128)} %bitcast.me_ref, s32[112]{0:T(128)S(1)} %copy-done.7, bf16[512,1024]{1,0:T(8,128)(2,1)S(1)} %copy-done.2, bf16[2048,3584]{1,0:T(8,128)(2,1)} %copy-done.1, bf16[2048,3584]{1,0:T(8,128)(2,1)} %collective-permute-done.2.refs_2_.refs_6_.refs_4_), custom_call_target="tpu_custom_call" | custom-call | tf_op jit(solution)/shard_map/phase/pallas_call | solution.py:275
  45.3 0.0 copy-done
  45.3 0.0 copy-start.6
  45.3 8.1 %collective-permute-done.5.refs_0_ = bf16[512,1024]{1,0:T(8,128)(2,1)S(1)} collective-permute-done((bf16[512,1024]{1,0:T(8,128)(2,1)S(1)}, bf16[512,1024]{1,0:T(8,128)(2,1)S(1)}, u32[]{:S(2)}, u32[]{:S(2)}) %collective-permute-start.5) | collective-permute-done | bytes 1048608 | tf_op jit(solution)/shard_map/ppermute | solution.py:412
  53.5 1.6 %collective-permute-start.8 = (bf16[512,1024]{1,0:T(8,128)(2,1)S(1)}, bf16[512,1024]{1,0:T(8,128)(2,1)S(1)}, u32[]{:S(2)}, u32[]{:S(2)}) collective-permute-start(bf16[512,1024]{1,0:T(8,128)(2,1)S(1)} %tie.10.refs_3_), channel_id=1, source_target_pairs={{2,0},{4,2},{6,4},{7,6},{5,7},{3,5},{1,3},{0,1},{10,8},{12,10},{14... | collective-permute-start | bytes 3145736 | tf_op jit(solution)/shard_map/ppermute | solution.py:412
  55.0 0.0 collective-permute-done.1.refs_0_
  55.1 0.5 collective-permute-start.3
  55.5 0.0 collective-permute-done.6.refs_7_.refs_5_
  55.5 0.0 copy-done.6
  55.5 22.2 %phase.4.refs_1_.refs_6_ = f32[512,3584]{1,0:T(8,128)} custom-call(s32[1]{0:T(128)} %bitcast.me_ref, s32[256]{0:T(256)S(1)} %copy-done.6, bf16[512,1024]{1,0:T(8,128)(2,1)S(1)} %tie.7.refs_1_.refs_0_, bf16[512,1024]{1,0:T(8,128)(2,1)S(1)} %tie.9.refs_2_.refs_1_, bf16[512,1024]{1,0:T(8,128)(2,1)S(1)} %tie.8.refs_2_, bf16[512,1024]{1,0:T(8,128)(2,1)S(1)} %tie.10.refs_3_, ...), custom_call_target="tpu_custom_call" | custom-call | tf_op jit(solution)/shard_map/phase/pallas_call | solution.py:275
  77.7 0.0 copy-start.5
  77.7 0.5 collective-permute-done.8.refs_0_
  78.2 1.6 %collective-permute-start.9 = (bf16[256,1024]{1,0:T(8,128)(2,1)S(1)}, bf16[256,1024]{1,0:T(8,128)(2,1)S(1)}, u32[]{:S(2)}, u32[]{:S(2)}) collective-permute-start(bf16[256,1024]{1,0:T(8,128)(2,1)S(1)} %slice.9), channel_id=1, source_target_pairs={{2,0},{4,2},{6,4},{7,6},{5,7},{3,5},{1,3},{0,1},{10,8},{12,10},{14... | collective-permute-start | bytes 1572872 | tf_op jit(solution)/shard_map/ppermute | solution.py:415
  79.9 0.0 collective-permute-done.3.refs_0_
  79.9 0.5 collective-permute-start.7
  80.4 0.0 copy-done.5
  80.4 12.8 %phase.5.refs_3_ = f32[512,3584]{1,0:T(8,128)S(1)} custom-call(s32[1]{0:T(128)} %bitcast.me_ref, s32[160]{0:T(256)S(1)} %copy-done.5, bf16[512,1024]{1,0:T(8,128)(2,1)S(1)} %tie.12.refs_0_, bf16[512,1024]{1,0:T(8,128)(2,1)S(1)} %tie.13.refs_1_, bf16[2048,3584]{1,0:T(8,128)(2,1)} %copy-done.1, bf16[2064,3584]{1,0:T(8,128)(2,1)} %copy-done, ...), custom_call_target="tpu_custom_call" | custom-call | tf_op jit(solution)/shard_map/phase/pallas_call | solution.py:275
  93.2 0.0 collective-permute-done.9.refs_1_
  93.2 0.0 collective-permute-done.7.refs_0_
  93.2 4.9 %last_phase.1 = bf16[512,3584]{1,0:T(8,128)(2,1)} custom-call(bf16[256,1024]{1,0:T(8,128)(2,1)S(1)} %collective-permute-done.7.refs_0_, bf16[256,1024]{1,0:T(8,128)(2,1)S(1)} %collective-permute-done.9.refs_1_, bf16[1024,3584]{1,0:T(8,128)(2,1)S(1)} %get-tuple-element.8.refs_2_, f32[512,3584]{1,0:T(8,128)S(1)} %phase.5.refs_3_), custom_call_target="tpu_custom_call" | custom-call | tf_op jit(solution)/shard_map/last_phase/pallas_call | solution.py:328
  (9 shorter events, 0.1 us)
Async XLA Ops:
  0.0 26.4 %collective-permute-start.4 = (bf16[512,1024]{1,0:T(8,128)(2,1)}, bf16[512,1024]{1,0:T(8,128)(2,1)S(1)}, u32[]{:S(2)}, u32[]{:S(2)}) collective-permute-start(bf16[512,1024]{1,0:T(8,128)(2,1)} %refs_0_.1), channel_id=1, source_target_pairs={{2,0},{4,2},{6,4},{7,6},{5,7},{3,5},{1,3},{0,1},{10,8},{12,10},{14... | collective-permute-start | bytes 3145736 | tf_op jit(solution)/shard_map/ppermute | solution.py:390
  3.0 24.8 %collective-permute-start = (bf16[512,1024]{1,0:T(8,128)(2,1)}, bf16[512,1024]{1,0:T(8,128)(2,1)S(1)}, u32[]{:S(2)}, u32[]{:S(2)}) collective-permute-start(bf16[512,1024]{1,0:T(8,128)(2,1)} %refs_0_.1), channel_id=1, source_target_pairs={{0,2},{2,4},{4,6},{6,7},{7,5},{5,3},{3,1},{1,0},{8,10},{10,12},{12... | collective-permute-start | bytes 3145736 | tf_op jit(solution)/shard_map/ppermute | solution.py:390
  3.7 0.7 copy-start.3
  4.3 7.2 %copy-start.4 = (s32[48,1]{0,1:T(1,128)S(1)}, s32[48,1]{0,1:T(1,128)}, u32[]{:S(2)}) copy-start(s32[48,1]{0,1:T(1,128)} %param.11) | copy-start | bytes 580
  11.5 16.3 %copy-start.1 = (bf16[2048,3584]{1,0:T(8,128)(2,1)}, bf16[2048,3584]{1,0:T(8,128)(2,1)S(1)}, u32[]{:S(2)}) copy-start(bf16[2048,3584]{1,0:T(8,128)(2,1)S(1)} %merge.2.refs_1_.refs_4_.refs_2_) | copy-start | bytes 44040196
  11.5 22.4 %collective-permute-start.2 = (bf16[2048,3584]{1,0:T(8,128)(2,1)S(1)}, bf16[2048,3584]{1,0:T(8,128)(2,1)}, u32[]{:S(2)}, u32[]{:S(2)}) collective-permute-start(bf16[2048,3584]{1,0:T(8,128)(2,1)S(1)} %merge.2.refs_1_.refs_4_.refs_2_), channel_id=1, source_target_pairs={{0,8},{8,0},{1,9},{9,1},{2,10},{10,2},{3,11},{11,3},{4,12},{12,4},... | collective-permute-start | bytes 44040200 | tf_op jit(solution)/shard_map/ppermute | solution.py:394
  27.8 6.0 %copy-start.2 = (bf16[512,1024]{1,0:T(8,128)(2,1)S(1)}, bf16[512,1024]{1,0:T(8,128)(2,1)}, u32[]{:S(2)}) copy-start(bf16[512,1024]{1,0:T(8,128)(2,1)} %refs_0_.1) | copy-start | bytes 3145732
  27.8 6.0 %copy-start.7 = (s32[112]{0:T(128)S(1)}, s32[112]{0:T(128)}, u32[]{:S(2)}) copy-start(s32[112]{0:T(128)} %constant.17.clone.table_ref) | copy-start | bytes 1348
  27.8 17.5 %copy-start = (bf16[2064,3584]{1,0:T(8,128)(2,1)}, bf16[2064,3584]{1,0:T(8,128)(2,1)S(1)}, u32[]{:S(2)}) copy-start(bf16[2064,3584]{1,0:T(8,128)(2,1)S(1)} %tie.11.refs_5_.refs_3_) | copy-start | bytes 44384260
  27.8 27.7 %collective-permute-start.6 = (bf16[2064,3584]{1,0:T(8,128)(2,1)S(1)}, bf16[2064,3584]{1,0:T(8,128)(2,1)}, u32[]{:S(2)}, u32[]{:S(2)}) collective-permute-start(bf16[2064,3584]{1,0:T(8,128)(2,1)S(1)} %tie.11.refs_5_.refs_3_), channel_id=1, source_target_pairs={{0,8},{8,0},{1,9},{9,1},{2,10},{10,2},{3,11},{11,3},{4,12},{12,4},... | collective-permute-start | bytes 44384264 | tf_op jit(solution)/shard_map/ppermute | solution.py:409
  27.9 25.6 %collective-permute-start.5 = (bf16[512,1024]{1,0:T(8,128)(2,1)S(1)}, bf16[512,1024]{1,0:T(8,128)(2,1)S(1)}, u32[]{:S(2)}, u32[]{:S(2)}) collective-permute-start(bf16[512,1024]{1,0:T(8,128)(2,1)S(1)} %tie.9.refs_2_.refs_1_), channel_id=1, source_target_pairs={{2,0},{4,2},{6,4},{7,6},{5,7},{3,5},{1,3},{0,1},{10,8},{12,10},{14... | collective-permute-start | bytes 3145736 | tf_op jit(solution)/shard_map/ppermute | solution.py:412
  29.5 25.5 %collective-permute-start.1 = (bf16[512,1024]{1,0:T(8,128)(2,1)S(1)}, bf16[512,1024]{1,0:T(8,128)(2,1)S(1)}, u32[]{:S(2)}, u32[]{:S(2)}) collective-permute-start(bf16[512,1024]{1,0:T(8,128)(2,1)S(1)} %tie.7.refs_1_.refs_0_), channel_id=1, source_target_pairs={{0,2},{2,4},{4,6},{6,7},{7,5},{5,3},{3,1},{1,0},{8,10},{10,12},{12... | collective-permute-start | bytes 3145736 | tf_op jit(solution)/shard_map/ppermute | solution.py:412
  45.3 10.2 %copy-start.6 = (s32[256]{0:T(256)S(1)}, s32[256]{0:T(256)}, u32[]{:S(2)}) copy-start(s32[256]{0:T(256)} %constant.18.clone.table_ref) | copy-start | bytes 3076
  53.5 24.7 %collective-permute-start.8 = (bf16[512,1024]{1,0:T(8,128)(2,1)S(1)}, bf16[512,1024]{1,0:T(8,128)(2,1)S(1)}, u32[]{:S(2)}, u32[]{:S(2)}) collective-permute-start(bf16[512,1024]{1,0:T(8,128)(2,1)S(1)} %tie.10.refs_3_), channel_id=1, source_target_pairs={{2,0},{4,2},{6,4},{7,6},{5,7},{3,5},{1,3},{0,1},{10,8},{12,10},{14... | collective-permute-start | bytes 3145736 | tf_op jit(solution)/shard_map/ppermute | solution.py:412
  55.1 24.8 %collective-permute-start.3 = (bf16[512,1024]{1,0:T(8,128)(2,1)S(1)}, bf16[512,1024]{1,0:T(8,128)(2,1)S(1)}, u32[]{:S(2)}, u32[]{:S(2)}) collective-permute-start(bf16[512,1024]{1,0:T(8,128)(2,1)S(1)} %tie.8.refs_2_), channel_id=1, source_target_pairs={{0,2},{2,4},{4,6},{6,7},{7,5},{5,3},{3,1},{1,0},{8,10},{10,12},{12... | collective-permute-start | bytes 3145736 | tf_op jit(solution)/shard_map/ppermute | solution.py:412
  77.7 2.7 %copy-start.5 = (s32[160]{0:T(256)S(1)}, s32[160]{0:T(256)}, u32[]{:S(2)}) copy-start(s32[160]{0:T(256)} %constant.19.clone.table_ref) | copy-start | bytes 1924
  78.2 15.0 %collective-permute-start.9 = (bf16[256,1024]{1,0:T(8,128)(2,1)S(1)}, bf16[256,1024]{1,0:T(8,128)(2,1)S(1)}, u32[]{:S(2)}, u32[]{:S(2)}) collective-permute-start(bf16[256,1024]{1,0:T(8,128)(2,1)S(1)} %slice.9), channel_id=1, source_target_pairs={{2,0},{4,2},{6,4},{7,6},{5,7},{3,5},{1,3},{0,1},{10,8},{12,10},{14... | collective-permute-start | bytes 1572872 | tf_op jit(solution)/shard_map/ppermute | solution.py:415
  79.9 13.3 %collective-permute-start.7 = (bf16[256,1024]{1,0:T(8,128)(2,1)S(1)}, bf16[256,1024]{1,0:T(8,128)(2,1)S(1)}, u32[]{:S(2)}, u32[]{:S(2)}) collective-permute-start(bf16[256,1024]{1,0:T(8,128)(2,1)S(1)} %slice.8), channel_id=1, source_target_pairs={{0,2},{2,4},{4,6},{6,7},{7,5},{5,3},{3,1},{1,0},{8,10},{10,12},{12... | collective-permute-start | bytes 1572872 | tf_op jit(solution)/shard_map/ppermute | solution.py:415
